TPU v7x, 32 devices: a whole 2x2x4 slice. The times are simulated.
32 devices in a mesh: batch: 4 (over y, x), rows: 8 (over z, core).
Axes of the slice: x: 2, y: 2, z: 4, core: 2. Of those that a mesh axis runs over, the one named last changes fastest.
Arguments:
- features: bfloat16 [2, 4, 32, 96, 2048], P(None, 'batch', 'rows'), may hold values from -6 to 6
- task_grads: bfloat16 [3, 2, 4, 32, 96, 2048], P(None, None, 'batch', 'rows'), may hold values from -32 to 32
- row_counts: int32 [2, 4], replicated, may hold values from 8 to 32, as said below
- col_counts: int32 [2, 4], replicated, may hold values from 48 to 96, as said below
- weight_in: float32 [2048, 512], P(('batch', 'rows')), may hold values from -0.125 to 0.125
- weight_mid: float32 [4608, 512], P(('batch', 'rows')), may hold values from -0.09375 to 0.09375
- weight_out: float32 [512, 2048], P(None, ('batch', 'rows')), may hold values from -0.25 to 0.25
- first_in: float32 [2048, 512], P(('batch', 'rows')), may hold values from -0.0007324219 to 0.0007324219
- first_mid: float32 [4608, 512], P(('batch', 'rows')), may hold values from -0.0007324219 to 0.0007324219
- first_out: float32 [512, 2048], P(None, ('batch', 'rows')), may hold values from -0.0007324219 to 0.0007324219
- second_in: float32 [2048, 512], P(('batch', 'rows')), may hold values from 2.2408501e-10 to 8.9634006e-10
- second_mid: float32 [4608, 512], P(('batch', 'rows')), may hold values from 2.2408501e-10 to 8.9634006e-10
- second_out: float32 [512, 2048], P(None, ('batch', 'rows')), may hold values from 2.2408501e-10 to 8.9634006e-10
- norm_params: float32 [2, 3072], replicated, may hold values from -1.2 to 1.95, as said below
- norm_first: float32 [2, 3072], replicated, may hold values from -0.0007324219 to 0.0007324219
- norm_second: float32 [2, 3072], replicated, may hold values from 2.2408501e-10 to 8.9634006e-10
Outputs:
- block_out: bfloat16 [2, 4, 32, 96, 2048], P(None, 'batch', 'rows')
- input_grad: bfloat16 [2, 4, 32, 96, 2048], P(None, 'batch', 'rows')
- new_weight_in: float32 [2048, 512], P(('batch', 'rows'))
- new_weight_mid: float32 [4608, 512], P(('batch', 'rows'))
- new_weight_out: float32 [512, 2048], P(None, ('batch', 'rows'))
- new_first_in: float32 [2048, 512], P(('batch', 'rows'))
- new_first_mid: float32 [4608, 512], P(('batch', 'rows'))
- new_first_out: float32 [512, 2048], P(None, ('batch', 'rows'))
- new_second_in: float32 [2048, 512], P(('batch', 'rows'))
- new_second_mid: float32 [4608, 512], P(('batch', 'rows'))
- new_second_out: float32 [512, 2048], P(None, ('batch', 'rows'))
- new_norm: float32 [2, 3072], replicated
- new_norm_first: float32 [2, 3072], replicated
- new_norm_second: float32 [2, 3072], replicated
- grad_norm: float32 [1], replicated
Inputs may be any that keep to these rules, and one draw needn't show every extreme that they name: `row_counts`: in each micro-batch some crop has all 32 rows valid. `col_counts`: in each micro-batch some crop has all 96 columns valid. `norm_params`: row 0 holds positive gains.
All inputs are finite; a program needn't handle non-finite values.
Results may differ from a plain program's by a relative error of at most 0.0085.
Values may be sent and summed in bfloat16 or wider, within the bound.
No kernel may reach another device: no remote copies, remote signals or barrier semaphores. Data moves between devices by JAX's collectives and lax.ppermute only.
A program may use at most 192 MiB of HBM per device.

v0:
```python
import functools

import jax
import jax.numpy as jnp
from jax import lax
from jax.experimental import pallas as pl
from jax.experimental.pallas import tpu as pltpu
from jax.sharding import PartitionSpec as P

DILATION_SIZE = 4
NEWTON = 6
STEP = 10

EPS_NORM = 1e-05
CLIP = 1.0
RATE = 0.02
RATE_NORM = 0.3
BETA_ONE = 0.9
BETA_TWO = 0.999
ADAM_EPS = 1e-08
DECAY = 0.01

F32 = jnp.float32
BF16 = jnp.bfloat16


def swap(x, axis, mask):
    return lax.ppermute(x, axis, [(i, i ^ mask) for i in range(lax.axis_size(axis))])


def row_groups():
    groups = []
    bit, rest = 1, lax.axis_size("rows") // 2
    while rest > 1:
        size = min(4, rest)
        groups.append((bit, size))
        bit += size.bit_length() - 1
        rest //= size
    return groups


def group_sum(x, axis, shift, size):
    got = [x] + [swap(x, axis, m << shift) for m in range(1, size)]
    if size == 2:
        return got[0] + got[1]
    return (got[0] + got[1]) + (got[2] + got[3])


def chip_sums(x):
    return group_sum(group_sum(x, "rows", 0, 2), "batch", 0, lax.axis_size("batch"))


def all_sum(x):
    return line_sums(chip_sums(x))


def line_sums(x):
    for bit, size in row_groups():
        x = group_sum(x, "rows", bit, size)
    return x


def put(buf, piece, index, axis):
    return lax.dynamic_update_slice_in_dim(buf, jnp.expand_dims(piece, axis), index, axis)


def take(buf, index, axis):
    return lax.dynamic_index_in_dim(buf, index, axis, keepdims=False)


def gather_shards(shard):
    mine = lax.axis_index("rows")
    core = mine & 1
    batch = lax.axis_index("batch")
    block = shard[None]
    for bit, size in row_groups():
        place = (mine >> bit) & (size - 1)
        got = [block] + [swap(block, "rows", m << bit) for m in range(1, size)]
        buf = jnp.zeros((size,) + block.shape, block.dtype)
        for m, piece in enumerate(got):
            buf = put(buf, piece, place ^ m, 0)
        block = buf.reshape((-1,) + block.shape[1:])
    half = block.shape[0] // 2
    from_x = swap(block, "batch", 1)
    from_y = swap(block, "batch", 2)
    far_low = swap(from_x[:half], "batch", 2)
    far_high = swap(from_y[half:], "batch", 1)
    far = jnp.concatenate([far_low, far_high], axis=0)
    full = jnp.zeros((4, block.shape[0], 2) + block.shape[1:], block.dtype)
    for m, piece in enumerate((block, from_x, from_y, far)):
        other = swap(piece, "rows", 1)
        for value, where in ((piece, core), (other, 1 - core)):
            full = lax.dynamic_update_slice(
                full, value[None, :, None], (batch ^ m, 0, where, 0, 0)
            )
    return full


def scatter_sums(grad):
    mine = lax.axis_index("rows")
    core = mine & 1
    batch = lax.axis_index("batch")
    count = lax.axis_size("rows")
    grad = grad.reshape(4, count // 2, 2, -1, grad.shape[-1])
    got = swap(take(grad, 1 - core, 2).astype(BF16), "rows", 1)
    part = take(grad, core, 2).astype(F32) + got.astype(F32)
    half = part.shape[1] // 2
    own, to_x, to_y, far = [take(part, batch ^ m, 0) for m in range(4)]
    low = swap(far[:half].astype(BF16), "batch", 1).astype(F32)
    high = swap(far[half:].astype(BF16), "batch", 2).astype(F32)
    to_x = jnp.concatenate([to_x[:half], to_x[half:] + high], axis=0)
    to_y = jnp.concatenate([to_y[:half] + low, to_y[half:]], axis=0)
    from_x = swap(to_x.astype(BF16), "batch", 1)
    from_y = swap(to_y.astype(BF16), "batch", 2)
    own = own + from_x.astype(F32) + from_y.astype(F32)
    for bit, size in reversed(row_groups()):
        place = (mine >> bit) & (size - 1)
        own = own.reshape((size, -1) + own.shape[1:])
        total = take(own, place, 0)
        for m in range(1, size):
            total = total + swap(take(own, place ^ m, 0).astype(BF16), "rows", m << bit).astype(F32)
        own = total
    return own.reshape(own.shape[-2:])


def joined(pieces, *after):
    sizes = [piece.shape[0] for piece in pieces]

    def kernel(*refs):
        first = 0
        for ref, size in zip(refs, sizes):
            refs[-1][first : first + size] = ref[...].astype(BF16)
            first += size

    return pl.pallas_call(
        kernel,
        in_specs=[pl.BlockSpec(memory_space=pltpu.VMEM)] * len(pieces) + [pl.BlockSpec(memory_space=pl.ANY)] * len(after),
        out_specs=pl.BlockSpec(memory_space=pltpu.VMEM),
        out_shape=jax.ShapeDtypeStruct((sum(sizes),) + pieces[0].shape[1:], BF16),
    )(*pieces, *after)


def owners(batch_mask, core_mask, line):
    mine, batch = lax.axis_index("rows"), lax.axis_index("batch")
    chip = (batch ^ batch_mask) * (lax.axis_size("rows") // 2) + ((mine >> 1) ^ line)
    return chip * 2 + ((mine & 1) ^ core_mask)


def gather_pieces(shard, join):
    line = lax.axis_size("rows") // 2
    block = shard[None]
    for bit, size in row_groups():
        block = join([block] + [swap(block, "rows", m << bit) for m in range(1, size)])
    half = line // 2
    from_x = swap(block, "batch", 1)
    from_y = swap(block, "batch", 2)
    far_low = swap(from_x[:half], "batch", 2)
    far_high = swap(from_y[half:], "batch", 1)
    pieces = []
    for piece, mask, first in ((block, 0, 0), (from_x, 1, 0), (from_y, 2, 0), (far_low, 3, 0), (far_high, 3, half)):
        place = first + jnp.arange(piece.shape[0], dtype=jnp.int32)
        for array, core in ((piece, 0), (swap(piece, "rows", 1), 1)):
            pieces.append((array, owners(mask, core, place)))
    return pieces


class Assembly:
    def __init__(self, pieces, first, size):
        self.first, self.size = first, size
        owner = jnp.concatenate([owner for _, owner in pieces]).astype(jnp.int32)
        self.ins = [smem(owner * size)] + [whole(array) for array, _ in pieces]
        self.count = len(self.ins)

    def run(self, refs, held):
        starts, k = refs[0], 0
        for ref in refs[1:]:
            for j in range(ref.shape[0]):
                rows = pl.ds(pl.multiple_of(starts[k], self.size), self.size)
                held[rows, :] = ref[j, self.first : self.first + self.size, :]
                k += 1


def assemble_kernel(assembly, *refs):
    assembly.run(refs[:-1], refs[-1])


class Spread:
    def __init__(self, width, *rows):
        mine, batch = lax.axis_index("rows"), lax.axis_index("batch")
        line = lax.axis_size("rows") // 2
        self.chips = 4 * line
        self.sizes = [r // (2 * self.chips) for r in rows]
        self.direct = not any(size % 16 for size in self.sizes)
        chip = jnp.arange(self.chips, dtype=jnp.int32)
        far = (chip // line) ^ batch
        near = (chip % line) ^ (mine >> 1)
        half = line // 2
        place = ((near // half) * 4 + (far ^ (far >> 1))) * half + near % half
        self.ins = [smem(place.astype(jnp.int32)), smem((mine & 1).astype(jnp.int32).reshape(1))]
        shapes = [(r, width) for r in rows]
        if self.direct:
            shapes = [(self.chips, sum(self.sizes), width)] * 2
        self.outs = [out(shape, BF16, shape, lambda *_, n=len(shape): (0,) * n) for shape in shapes]

    def emit(self, weight, product, base, rows, place_ref, core_ref, outs):
        if not self.direct:
            outs[weight][pl.ds(base, rows), :] = product[0:rows, :].astype(BF16)
            return
        core = core_ref[0]
        size, low = self.sizes[weight], sum(self.sizes[:weight])
        pair = 2 * size
        first = base // pair
        for k in range(rows // pair):
            to = place_ref[first + k]
            for ref, c in ((outs[0], 1 - core), (outs[1], core)):
                start = pl.multiple_of(k * pair + c * size, 16)
                ref[to, low : low + size, :] = product[pl.ds(start, size), :].astype(BF16)


def in_order(*values):
    return lax.optimization_barrier(values)


class Sums:
    def __init__(self, spread, outs):
        self.direct = spread.direct
        if not self.direct:
            parts = [part.reshape(2 * spread.chips, size, -1) for part, size in zip(outs, spread.sizes)]
            self.total = scatter_sums(jnp.concatenate(parts, axis=1).reshape(-1, outs[0].shape[-1]))
            return
        shape = (2, 4, lax.axis_size("rows") // 4) + outs[0].shape[1:]
        self.keep = outs[1].reshape(shape)
        self.got = swap(outs[0], "rows", 1).reshape(shape)

    def part(self, half, index):
        return self.keep[half, index].astype(F32) + self.got[half, index].astype(F32)

    def send_far(self):
        return self.part(0, slice(1, 3)).astype(BF16), self.part(1, slice(2, 4)).astype(BF16)

    def take_far(self, sends):
        self.far = swap(sends[0], "batch", 1), swap(sends[1], "batch", 2)

    def send_near(self):
        from_x, from_y = self.far
        return (
            (self.part(1, 1) + from_y[0].astype(F32)).astype(BF16),
            (self.part(0, 3) + from_x[1].astype(F32)).astype(BF16),
        )

    def take_near(self, sends):
        self.near = swap(sends[0], "batch", 1), swap(sends[1], "batch", 2)

    def send_line(self):
        low = self.part(0, 0) + self.far[0][0].astype(F32) + self.near[1].astype(F32)
        high = self.part(1, 0) + self.far[1][1].astype(F32) + self.near[0].astype(F32)
        return jnp.concatenate([low, high], axis=0)

    def take_line(self, own):
        for bit, size in reversed(row_groups()):
            own = own.reshape((size, -1) + own.shape[1:])
            total = own[0]
            for m in range(1, size):
                total = total + swap(own[m].astype(BF16), "rows", m << bit).astype(F32)
            own = total
        self.total = own.reshape(own.shape[-2:])


CHUNK = 16
PAD = 8
NN, NT, TN = (1, 0), (1, 1), (0, 0)


def dot(left, right, dims):
    return lax.dot_general(left, right, ((dims[:1], dims[1:]), ((), ())), preferred_element_type=F32)


def softplus(z):
    e = jnp.exp(-jnp.abs(z))
    return jnp.maximum(z, 0.0) + jnp.where(e < 1e-3, e * (1.0 - 0.5 * e), jnp.log(1.0 + e))


def sigmoid(z):
    return 0.5 * jnp.tanh(0.5 * z) + 0.5


def wide(mask, width):
    return jnp.concatenate([mask] * (width // mask.shape[-1]), axis=-1)


def fold(v):
    return v[:8] + v[8:]


def down(v):
    return jnp.sum(v, axis=0, keepdims=True)


def loop(rows, body, init, unroll=2):
    def step(i, carry):
        return body(pl.ds(pl.multiple_of(i * CHUNK, CHUNK), CHUNK), carry)

    return lax.fori_loop(0, rows // CHUNK, step, init, unroll=unroll)


def zeros8(width, count=2):
    return tuple(jnp.zeros((8, width), F32) for _ in range(count))


def norm_stats(sums_ref, inv, gain):
    mean = sums_ref[0, 0:1, :] * inv
    rstd = lax.rsqrt(sums_ref[0, 1:2, :] * inv - mean * mean + EPS_NORM)
    return mean, rstd, gain * rstd


def call(kernel, grid, ins, outs, scratch=(), flops=0, nbytes=0, vmem=48):
    got = pl.pallas_call(
        kernel,
        grid=grid,
        in_specs=[spec for _, spec in ins],
        out_specs=[spec for _, spec in outs],
        out_shape=[shape for shape, _ in outs],
        scratch_shapes=list(scratch),
        compiler_params=pltpu.CompilerParams(
            dimension_semantics=("arbitrary",) * len(grid), vmem_limit_bytes=vmem * 1024 * 1024
        ),
        cost_estimate=pl.CostEstimate(flops=flops, bytes_accessed=nbytes, transcendentals=0),
    )(*[array for array, _ in ins])
    return got[0] if len(outs) == 1 else got


def block(shape, index, **kw):
    return pl.BlockSpec(shape, index, **kw)


def listed(got):
    return list(got) if isinstance(got, (list, tuple)) else [got]


def whole(array):
    zeros = (0,) * len(array.shape)
    return (array, pl.BlockSpec(array.shape, lambda *_: zeros, pipeline_mode=pl.Buffered(1)))


def smem(array):
    return (array, pl.BlockSpec(memory_space=pltpu.SMEM))


def anywhere(array):
    return (array, pl.BlockSpec(memory_space=pl.ANY))


def out(shape, dtype, spec_shape, index):
    return (jax.ShapeDtypeStruct(shape, dtype), pl.BlockSpec(spec_shape, index))


def gram_kernel(task_ref, mask_ref, out_ref):
    lanes = mask_ref.shape[-1]
    chan = task_ref.shape[-1]

    @pl.when(pl.program_id(0) == 0)
    def _():
        out_ref[...] = jnp.zeros_like(out_ref)

    def step(rows, carry):
        sums = [jnp.zeros((CHUNK, lanes), F32)] * 6
        for col in range(chan // lanes):
            cols = pl.ds(col * lanes, lanes)
            t = [task_ref[k, 0, 0, 0, rows, cols].astype(F32) for k in range(3)]
            pairs = [t[i] * t[j] for i in range(3) for j in range(i, 3)]
            sums = [s + p for s, p in zip(sums, pairs)]
        mask = mask_ref[0, 0, rows, :]
        return tuple(c + fold(s * mask) for c, s in zip(carry, sums))

    got = loop(task_ref.shape[4], step, zeros8(lanes, 6), unroll=1)
    for k in range(6):
        out_ref[k : k + 1, :] += down(got[k])


def first_kernel(assembly, x_ref, mask_ref, gram_ref, *refs):
    pieces, (wide_ref, low_ref, sums_ref, w_ref) = refs[: assembly.count], refs[assembly.count :]
    width = w_ref.shape[1]

    @pl.when(pl.program_id(0) == 0)
    def _():
        assembly.run(pieces, w_ref)

    wide_ref[0] = dot(x_ref[0], w_ref[...], NN)

    def step(rows, carry):
        v = wide_ref[0, rows, :]
        low_ref[0, rows, :] = v.astype(BF16)
        kept = v * wide(mask_ref[0, 0, rows, :], width)
        return carry[0] + fold(kept), carry[1] + fold(kept * v)

    got = loop(x_ref.shape[1], step, zeros8(width))
    sums_ref[0] = jnp.zeros_like(sums_ref[0])
    sums_ref[0, 0:1, :] = down(got[0])
    sums_ref[0, 1:2, :] = down(got[1])
    for k in range(6):
        lane = (k % 4) * 128
        sums_ref[0, 2 + k // 4 : 3 + k // 4, lane : lane + 128] = gram_ref[0, k : k + 1, :]


def upstream_kernel(sums_ref, task_ref, mask_ref, *refs):
    out_ref, coeff_ref = refs[-2:]
    lanes = mask_ref.shape[-1]

    @pl.when((pl.program_id(0) == 0) & (pl.program_id(1) == 0))
    def _():
        def entry(k):
            lane, row = (k % 4) * 128, 2 + k // 4
            both = sums_ref[0, row : row + 1, lane : lane + 128] + sums_ref[1, row : row + 1, lane : lane + 128]
            return jnp.sum(both, axis=1, keepdims=True)

        place = {}
        k = 0
        for i in range(3):
            for j in range(i, 3):
                place[i, j] = place[j, i] = entry(k)
                k += 1
        trace = place[0, 0] + place[1, 1] + place[2, 2]
        ymat = [[place[i, j] / trace for j in range(3)] for i in range(3)]
        zmat = [[jnp.full((1, 1), 1.0 if i == j else 0.0, F32) for j in range(3)] for i in range(3)]

        def mul(a, b):
            return [
                [a[i][0] * b[0][j] + a[i][1] * b[1][j] + a[i][2] * b[2][j] for j in range(3)]
                for i in range(3)
            ]

        for _ in range(NEWTON):
            zy = mul(zmat, ymat)
            pmat = [[(1.5 if i == j else 0.0) - 0.5 * zy[i][j] for j in range(3)] for i in range(3)]
            ymat = mul(ymat, pmat)
            zmat = mul(pmat, zmat)
        for i in range(3):
            value = (zmat[i][0] + zmat[i][1] + zmat[i][2]) / jnp.sqrt(F32(3.0))
            coeff_ref[i] = jnp.broadcast_to(value, (8, lanes))

    def step(rows, carry):
        mask = mask_ref[0, 0, rows, :]
        c = [jnp.concatenate([coeff_ref[i]] * (CHUNK // 8), axis=0) * mask for i in range(3)]
        for col in range(task_ref.shape[-1] // lanes):
            cols = pl.ds(col * lanes, lanes)
            t = [task_ref[k, 0, 0, 0, rows, cols].astype(F32) for k in range(3)]
            out_ref[0, rows, cols] = c[0] * t[0] + c[1] * t[1] + c[2] * t[2]
        return carry

    loop(task_ref.shape[4], step, 0, unroll=1)


def shifted_sum(parts, row, start, rows, sign):
    at = PAD + start
    low, high = at + sign * DILATION_SIZE, at - sign * DILATION_SIZE
    return (
        parts[1, row, at : at + rows, :]
        + parts[0, row, low : low + rows, :]
        + parts[2, row, high : high + rows, :]
    )


def clear_pads(ref):
    edge = ref.shape[-2]
    zero = jnp.zeros(ref.shape[:-2] + (PAD, ref.shape[-1]), ref.dtype)
    ref[..., 0:PAD, :] = zero
    ref[..., edge - PAD : edge, :] = zero


def second_kernel(
    inv_ref, sums_ref, param_ref, own_ref, up_ref, down_ref, mask_ref, w_ref, *refs
):
    h_ref, wide_ref, low_ref, out_ref, cat_ref, part_ref = refs[-6:]
    micro = pl.program_id(0)
    width = own_ref.shape[-1]
    pixels = own_ref.shape[1]
    columns = part_ref.shape[2] - 2 * PAD

    @pl.when(micro == 0)
    def _():
        clear_pads(part_ref)

    mean, rstd, scale = norm_stats(sums_ref, inv_ref[micro], param_ref[0:1, :])
    offset = param_ref[1:2, :] - mean * scale
    for k, ref in enumerate((up_ref, own_ref, down_ref)):
        def step(rows, carry):
            z = ref[0, rows, :].astype(F32) * scale + offset
            h = (softplus(z) * wide(mask_ref[k, 0, rows, :], width)).astype(BF16)
            h_ref[k, 0, rows, :] = h
            cat_ref[rows, k * width : (k + 1) * width] = h
            return carry

        loop(pixels, step, 0)

    for tx in range(3):
        taps = [w_ref[(3 * ty + tx) * width : (3 * ty + tx + 1) * width, :] for ty in range(3)]
        product = dot(cat_ref[...], jnp.concatenate(taps, axis=0), NN)
        part_ref[tx, :, PAD : PAD + columns, :] = product.reshape(-1, columns, width)

    def row_step(row, carry):
        for start in range(0, columns, CHUNK):
            rows = pl.ds(pl.multiple_of(row * columns + start, CHUNK), CHUNK)
            v = shifted_sum(part_ref, row, start, CHUNK, -1)
            wide_ref[0, rows, :] = v
            low_ref[0, rows, :] = v.astype(BF16)
            kept = v * wide(mask_ref[1, 0, rows, :], width)
            carry = carry[0] + fold(kept), carry[1] + fold(kept * v)
        return carry

    got = lax.fori_loop(0, pixels // columns, row_step, zeros8(width))
    out_ref[0, 0:1, :] = down(got[0])
    out_ref[0, 1:2, :] = down(got[1])


def third_kernel(inv_ref, sums_ref, param_ref, a_ref, mask_ref, w_ref, h_ref, wide_ref, out_ref):
    micro = pl.program_id(0)
    width = a_ref.shape[-1]
    tile = 512
    mean, rstd, scale = norm_stats(sums_ref, inv_ref[micro], param_ref[0:1, :])
    offset = param_ref[1:2, :] - mean * scale

    def step(rows, carry):
        z = a_ref[0, rows, :] * scale + offset
        h_ref[0, rows, :] = (softplus(z) * wide(mask_ref[0, 0, rows, :], width)).astype(BF16)
        return carry

    loop(a_ref.shape[1], step, 0)
    for col in range(0, w_ref.shape[0], tile):
        cols = pl.ds(col, tile)
        wide_ref[0, :, cols] = dot(h_ref[0], w_ref[cols, :], NT)

        def sum_step(rows, carry):
            v = wide_ref[0, rows, cols]
            kept = v * wide(mask_ref[0, 0, rows, :], tile)
            return carry[0] + fold(kept), carry[1] + fold(kept * v)

        got = loop(a_ref.shape[1], sum_step, zeros8(tile))
        out_ref[0, 0:1, cols] = down(got[0])
        out_ref[0, 1:2, cols] = down(got[1])


def peak_kernel(
    inv_ref, sums_ref, param_ref, a_ref, x_ref, up_ref, mask_ref, after_ref, late_ref, block_ref, du_ref, out_ref
):
    width = a_ref.shape[-1]
    mean, rstd, scale = norm_stats(sums_ref, inv_ref[pl.program_id(0)], param_ref[0:1, :])
    shift = param_ref[1:2, :]

    def step(rows, carry):
        centred = a_ref[0, rows, :] - mean
        u = centred * scale + (shift + x_ref[0, rows, :].astype(F32))
        mask = wide(mask_ref[0, 0, rows, :], width)
        block_ref[0, rows, :] = (softplus(u) * mask).astype(BF16)
        du = up_ref[0, rows, :] * sigmoid(u)
        du_ref[0, rows, :] = du
        return carry[0] + fold(du), carry[1] + fold(du * centred)

    got = loop(a_ref.shape[1], step, zeros8(width))
    out_ref[0, 0:1, :] = down(got[0])
    out_ref[0, 1:2, :] = down(got[1]) * rstd


def lower_consts(stats_ref, grads_ref, inv, gain):
    mean, rstd, scale = norm_stats(stats_ref, inv, gain)
    return mean, scale, grads_ref[0, 0:1, :] * inv, grads_ref[0, 1:2, :] * inv * rstd


def back_third_kernel(
    inv_ref, stats3_ref, grads3_ref, stats2_ref, param3_ref, param2_ref,
    a3_ref, du_ref, a2_ref, mask_ref, w_ref,
    d_ref, wide_ref, low_ref, out_ref,
):
    inv = inv_ref[pl.program_id(0)]
    tile = 512
    for col in range(0, a3_ref.shape[2], tile):
        cols = pl.ds(col, tile)
        mean = stats3_ref[0, 0:1, cols] * inv
        rstd = lax.rsqrt(stats3_ref[0, 1:2, cols] * inv - mean * mean + EPS_NORM)
        scale = param3_ref[0:1, cols] * rstd
        base = grads3_ref[0, 0:1, cols] * inv
        slope = grads3_ref[0, 1:2, cols] * inv * rstd

        def step(rows, carry):
            d = du_ref[0, rows, cols] - (base + (a3_ref[0, rows, cols] - mean) * slope)
            d_ref[0, rows, cols] = (d * scale * wide(mask_ref[0, 0, rows, :], tile)).astype(BF16)
            return carry

        loop(a3_ref.shape[1], step, 0)
    wide_ref[0] = dot(d_ref[0], w_ref[...], NN)
    width = w_ref.shape[1]
    mean, rstd, scale = norm_stats(stats2_ref, inv, param2_ref[0:1, :])
    shift = param2_ref[1:2, :]

    def last(rows, carry):
        centred = a2_ref[0, rows, :] - mean
        gate = sigmoid(centred * scale + shift) * wide(mask_ref[0, 0, rows, :], width)
        dz = wide_ref[0, rows, :] * gate
        wide_ref[0, rows, :] = dz
        low_ref[0, rows, :] = dz.astype(BF16)
        return carry[0] + fold(dz), carry[1] + fold(dz * centred)

    got = loop(a2_ref.shape[1], last, zeros8(width))
    out_ref[0, 0:1, :] = down(got[0])
    out_ref[0, 1:2, :] = down(got[1]) * rstd


def lower_second_kernel(
    inv_ref, stats2_ref, grads2_ref, param2_ref,
    a2_ref, a2_up_ref, a2_down_ref, dz_ref, dz_up_ref, dz_down_ref, mask_ref, cat_ref, shift_ref, pad_ref,
):
    inv = inv_ref[pl.program_id(0)]
    pixels, width = a2_ref.shape[1:]
    columns = pad_ref.shape[1] - 2 * PAD

    @pl.when(pl.program_id(0) == 0)
    def _():
        clear_pads(pad_ref)

    mean, scale, base, slope = lower_consts(stats2_ref, grads2_ref, inv, param2_ref[0:1, :])

    def lowered(k, a, dz, rows):
        d = dz.astype(F32) - (base + (a.astype(F32) - mean) * slope)
        return d * scale * wide(mask_ref[k, 0, rows, :], width)

    for k, a_ref, d_ref, place in ((0, a2_up_ref, dz_up_ref, 2), (2, a2_down_ref, dz_down_ref, 0)):
        def step(rows, carry):
            d = lowered(k, a_ref[0, rows, :], d_ref[0, rows, :], rows)
            cat_ref[0, rows, place * width : (place + 1) * width] = d.astype(BF16)
            return carry

        loop(pixels, step, 0)

    def own_step(row, carry):
        for start in range(0, columns, CHUNK):
            rows = pl.ds(pl.multiple_of(row * columns + start, CHUNK), CHUNK)
            d = lowered(1, a2_ref[0, rows, :], dz_ref[0, rows, :], rows)
            low = d.astype(BF16)
            cat_ref[0, rows, width : 2 * width] = low
            shift_ref[0, rows, width : 2 * width] = low
            pad_ref[row, PAD + start : PAD + start + CHUNK, :] = d
        for start in range(0, columns, CHUNK):
            rows = pl.ds(pl.multiple_of(row * columns + start, CHUNK), CHUNK)
            for tx in (-1, 1):
                at = PAD + start - tx * DILATION_SIZE
                moved = pad_ref[row, at : at + CHUNK, :].astype(BF16)
                shift_ref[0, rows, (tx + 1) * width : (tx + 2) * width] = moved
        return carry

    lax.fori_loop(0, pixels // columns, own_step, 0)


def back_second_kernel(
    inv_ref, stats1_ref, param1_ref, cat_ref, a1_ref, mask_ref, w_ref, after_ref, wide_ref, out_ref, part_ref
):
    inv = inv_ref[pl.program_id(0)]
    pixels, width = a1_ref.shape[1:]
    columns = part_ref.shape[2] - 2 * PAD

    @pl.when(pl.program_id(0) == 0)
    def _():
        clear_pads(part_ref)

    for tx in range(3):
        taps = [w_ref[(3 * ty + tx) * width : (3 * ty + tx + 1) * width, :] for ty in range(3)]
        product = dot(cat_ref[0], jnp.concatenate(taps, axis=1), NT)
        part_ref[tx, :, PAD : PAD + columns, :] = product.reshape(-1, columns, width)

    mean1, rstd1, scale1 = norm_stats(stats1_ref, inv, param1_ref[0:1, :])
    shift1 = param1_ref[1:2, :]

    def row_step(row, carry):
        for start in range(0, columns, CHUNK):
            rows = pl.ds(pl.multiple_of(row * columns + start, CHUNK), CHUNK)
            centred = a1_ref[0, rows, :] - mean1
            gate = sigmoid(centred * scale1 + shift1) * wide(mask_ref[0, 0, rows, :], width)
            dz = shifted_sum(part_ref, row, start, CHUNK, 1) * gate
            wide_ref[0, rows, :] = dz
            carry = carry[0] + fold(dz), carry[1] + fold(dz * centred)
        return carry

    got = lax.fori_loop(0, pixels // columns, row_step, zeros8(width))
    out_ref[0, 0:1, :] = down(got[0])
    out_ref[0, 1:2, :] = down(got[1]) * rstd1


def grads_kernel(spread, h_ref, d_ref, d3_ref, h2_ref, place_ref, core_ref, *refs):
    outs, product = refs[:-1], refs[-1]
    width = h_ref.shape[-1]
    step = pl.program_id(0)

    @pl.when(step < 3)
    def _():
        for tx in range(3):
            rows = pl.ds(pl.multiple_of((3 * step + tx) * width, width), width)
            product[rows, :] = dot(h_ref[0], d_ref[:, tx * width : (tx + 1) * width], TN)

    @pl.when(step == 2)
    def _():
        spread.emit(0, product, 0, product.shape[0], place_ref, core_ref, outs)

    @pl.when(step >= 3)
    def _():
        rows = d3_ref.shape[1]
        product[0:rows, :] = dot(d3_ref[...], h2_ref[...], TN)
        spread.emit(1, product, pl.multiple_of((step - 3) * rows, rows), rows, place_ref, core_ref, outs)


def first_back_kernel(
    spread, inv_ref, stats_ref, grads_ref, param_ref, dz_ref, a_ref, mask_ref, x_ref, place_ref, core_ref, *refs
):
    d_ref, outs, product = refs[0], refs[1:-1], refs[-1]
    pixels, width = dz_ref.shape[1:]

    @pl.when(pl.program_id(0) == 0)
    def _():
        for micro in range(dz_ref.shape[0]):
            inv = inv_ref[micro]
            mean, scale, base, slope = lower_consts(
                stats_ref.at[micro : micro + 1], grads_ref.at[micro : micro + 1], inv, param_ref[0:1, :]
            )

            def step(rows, carry):
                d = dz_ref[micro, rows, :] - (base + (a_ref[micro, rows, :] - mean) * slope)
                d = d * scale * wide(mask_ref[0, micro, rows, :], width)
                d_ref[micro, rows, :] = d.astype(BF16)
                return carry

            loop(pixels, step, 0)

    product[...] = dot(x_ref[...], d_ref[...].reshape(-1, width), TN)
    rows = product.shape[0]
    spread.emit(0, product, pl.multiple_of(pl.program_id(0) * rows, rows), rows, place_ref, core_ref, outs)


def input_grad_kernel(d_ref, w_ref, du_ref, out_ref):
    out_ref[...] = (dot(d_ref[...], w_ref[...], NT) + du_ref[...]).astype(BF16)


def adamw(weight, first, second, grad, rate, decay):
    new_first = BETA_ONE * first + (1.0 - BETA_ONE) * grad
    new_second = BETA_TWO * second + (1.0 - BETA_TWO) * grad * grad
    first_hat = new_first / (1.0 - BETA_ONE**STEP)
    second_hat = new_second / (1.0 - BETA_TWO**STEP)
    new_weight = weight - rate * (first_hat / (jnp.sqrt(second_hat) + ADAM_EPS) + decay * weight)
    return (new_weight, new_first, new_second)


def neighbours(x):
    count = lax.axis_size("rows")
    above = lax.ppermute(x, "rows", [(i, i + 1) for i in range(count - 1)])
    below = lax.ppermute(x, "rows", [(i + 1, i) for i in range(count - 1)])
    return above, below


def per_device(
    features, task_grads, row_counts, col_counts,
    weight_in, weight_mid, weight_out,
    first_in, first_mid, first_out,
    second_in, second_mid, second_out,
    norm_params, norm_first, norm_second,
):
    micros, _, row_span, columns, chan = features.shape
    inner = weight_in.shape[1]
    pixels = row_span * columns
    total_pixels = micros * pixels
    batch = lax.axis_index("batch")
    own_rows = lax.dynamic_index_in_dim(row_counts, batch, 1, keepdims=False)
    own_cols = lax.dynamic_index_in_dim(col_counts, batch, 1, keepdims=False)
    base = lax.axis_index("rows") * row_span + jnp.arange(-1, 2, dtype=jnp.int32) * row_span
    row_ids = base[:, None] + jnp.arange(row_span, dtype=jnp.int32)
    col_ids = jnp.arange(columns, dtype=jnp.int32)
    in_rows = (row_ids[:, None] >= 0) & (row_ids[:, None] < own_rows[None, :, None])
    in_cols = col_ids < own_cols[:, None]
    masks = (in_rows[:, :, :, None] & in_cols[None, :, None, :]).astype(F32)
    masks = jnp.broadcast_to(masks.reshape(3, micros, pixels, 1), (3, micros, pixels, 128))
    inverse = 1.0 / jnp.sum(row_counts * col_counts, axis=1).astype(F32)

    w_mid = lax.all_gather(weight_mid.astype(BF16), ("batch", "rows"), axis=0, tiled=True)
    grams = []
    for micro in range(micros):
        grams.append(call(
            gram_kernel, (row_span,),
            [
                (task_grads, block((3, 1, 1, 1, columns, chan), functools.partial(lambda m, r: (0, m, 0, r, 0, 0), micro))),
                (masks, block((1, 1, columns, 128), functools.partial(lambda m, r: (1, m, r, 0), micro))),
            ],
            [out((8, 128), F32, (8, 128), lambda r: (0, 0))],
            flops=6 * total_pixels * chan, nbytes=3 * total_pixels * chan,
        ))
    x = features.reshape(micros, pixels, chan)
    params = [norm_params[:, :inner], norm_params[:, inner : 2 * inner], norm_params[:, 2 * inner :]]

    def per_micro(array):
        return (array, block((1,) + array.shape[1:], lambda m, *_: (m,) + (0,) * (len(array.shape) - 1)))

    def out_micro(width, dtype, rows=pixels):
        return out((micros, rows, width), dtype, (1, rows, width), lambda m: (m, 0, 0))

    own_mask = (masks, block((1, 1, pixels, 128), lambda m, *_: (1, m, 0, 0)))
    all_masks = (masks, block((3, 1, pixels, 128), lambda m: (0, m, 0, 0)))
    row_mask = (masks, block((1, 1, columns, 128), lambda m, r: (1, m, r, 0)))
    task_rows = (
        task_grads, block((3, 1, 1, 1, columns, chan), lambda m, r: (0, m, 0, r, 0, 0))
    )
    big = total_pixels * chan
    small = total_pixels * inner
    part_rows = weight_in.shape[0]
    both = jnp.concatenate([weight_in.astype(BF16), weight_out.T.astype(BF16)], axis=0)
    if part_rows % 16:
        full = gather_shards(both).reshape(-1, 2, part_rows, inner)
        zero = jnp.zeros(1, jnp.int32)
        ins_in, ins_out = [Assembly([(full[:, k].reshape(1, -1, inner), zero)], 0, chan) for k in range(2)]
    else:
        pieces = gather_pieces(both, lambda got: joined(got, grams[0]))
        ins_in, ins_out = [Assembly(pieces, k * part_rows, part_rows) for k in range(2)]
    whole_weight = out((chan, inner), BF16, (chan, inner), lambda *_: (0, 0))
    a_one, a_one_low, part, w_in = call(
        functools.partial(first_kernel, ins_in), (micros,),
        [per_micro(x), own_mask, per_micro(jnp.stack(grams)), *ins_in.ins],
        [out_micro(inner, F32), out_micro(inner, BF16), out_micro(inner, F32, 4), whole_weight],
        flops=2 * big * inner, nbytes=2 * big + 8 * small,
    )
    a_one_up, a_one_down = neighbours(a_one_low)
    stats_one = all_sum(part)
    w_out = call(
        functools.partial(assemble_kernel, ins_out), (1,), ins_out.ins, [whole_weight], nbytes=8 * chan * inner
    )
    upstream = call(
        upstream_kernel, (micros, row_span),
        [whole(stats_one), task_rows, row_mask],
        [out((micros, pixels, chan), F32, (1, columns, chan), lambda m, r: (m, r, 0))],
        [pltpu.VMEM((3, 8, 128), F32)],
        flops=8 * big, nbytes=10 * big,
    )
    padded = (3, row_span, columns + 2 * PAD, inner)
    taps = [pltpu.VMEM((pixels, 3 * inner), BF16), pltpu.VMEM(padded, F32)]
    h_one, a_two, a_two_low, part = call(
        second_kernel, (micros,),
        [
            smem(inverse), per_micro(stats_one), whole(params[0]), per_micro(a_one),
            per_micro(a_one_up), per_micro(a_one_down), all_masks,
            whole(w_mid), anywhere(upstream),
        ],
        [
            out((3, micros, pixels, inner), BF16, (3, 1, pixels, inner), lambda m: (0, m, 0, 0)),
            out_micro(inner, F32), out_micro(inner, BF16), out_micro(inner, F32, 2),
        ],
        taps,
        flops=18 * small * inner, nbytes=20 * small + 18 * inner * inner,
    )
    a_two_up, a_two_down = neighbours(a_two_low)
    stats_two = all_sum(part)
    h_two, a_three, part = call(
        third_kernel, (micros,),
        [
            smem(inverse), per_micro(stats_two), whole(params[1]), per_micro(a_two), own_mask,
            whole(w_out),
        ],
        [out_micro(inner, BF16), out_micro(chan, F32), out_micro(chan, F32, 2)],
        flops=2 * big * inner, nbytes=4 * big + 8 * small,
    )
    stats_three = all_sum(part)
    tile = 512

    def tiled(array):
        return (array, block((1, array.shape[1], tile), lambda m, c: (m, 0, c)))

    def out_tiled(dtype, rows=pixels):
        return out((micros, rows, chan), dtype, (1, rows, tile), lambda m, c: (m, 0, c))

    block_out, d_resid, part = call(
        peak_kernel, (micros, chan // tile),
        [
            smem(inverse), tiled(stats_three), (params[2], block((2, tile), lambda m, c: (0, c))),
            tiled(a_three), tiled(x), tiled(upstream), own_mask, anywhere(a_two_up), anywhere(a_two_down),
        ],
        [out_tiled(BF16), out_tiled(F32), out_tiled(F32, 2)],
        flops=40 * big, nbytes=16 * big,
    )
    grads_three = all_sum(part)
    d_three, dz_two, dz_two_low, part = call(
        back_third_kernel, (micros,),
        [
            smem(inverse), per_micro(stats_three), per_micro(grads_three), per_micro(stats_two),
            whole(params[2]), whole(params[1]), per_micro(a_three), per_micro(d_resid),
            per_micro(a_two), own_mask, whole(w_out),
        ],
        [out_micro(chan, BF16), out_micro(inner, F32), out_micro(inner, BF16), out_micro(inner, F32, 2)],
        flops=2 * big * inner, nbytes=10 * big,
    )
    dz_two_up, dz_two_down = neighbours(dz_two_low)
    grads_two = all_sum(part)
    d_two_cat, d_two = call(
        lower_second_kernel, (micros,),
        [
            smem(inverse), per_micro(stats_two), per_micro(grads_two), whole(params[1]),
            per_micro(a_two), per_micro(a_two_up), per_micro(a_two_down),
            per_micro(dz_two), per_micro(dz_two_up), per_micro(dz_two_down), all_masks,
        ],
        [out_micro(3 * inner, BF16), out_micro(3 * inner, BF16)],
        [pltpu.VMEM(padded[1:], F32)],
        flops=60 * small, nbytes=28 * small,
    )
    spread = Spread(inner, 9 * inner, chan)
    grads = call(
        functools.partial(grads_kernel, spread), (3 + chan // tile,),
        [
            (
                h_one.reshape(3, total_pixels, inner),
                block((1, total_pixels, inner), lambda t: (jnp.minimum(t, 2), 0, 0)),
            ),
            whole(d_two.reshape(total_pixels, 3 * inner)),
            (
                d_three.reshape(total_pixels, chan),
                block((total_pixels, tile), lambda t: (0, jnp.maximum(t - 3, 0))),
            ),
            whole(h_two.reshape(total_pixels, inner)), *spread.ins,
        ],
        spread.outs, [pltpu.VMEM((9 * inner, inner), F32)],
        flops=18 * small * inner + 2 * big * inner, nbytes=12 * small + 18 * inner * inner,
    )
    sums = Sums(spread, grads)
    dz_one, part = call(
        back_second_kernel, (micros,),
        [
            smem(inverse), per_micro(stats_one), whole(params[0]), per_micro(d_two_cat),
            per_micro(a_one), own_mask, whole(w_mid), anywhere(grads[0]),
        ],
        [out_micro(inner, F32), out_micro(inner, F32, 2)],
        [pltpu.VMEM(padded, F32)],
        flops=18 * small * inner, nbytes=30 * small + 18 * inner * inner,
    )
    chip_one = chip_sums(part)
    if sums.direct:
        chip_one, *sends = in_order(chip_one, *sums.send_far())
        sums.take_far(sends)
    grads_one = line_sums(chip_one)
    spread_in = Spread(inner, chan)
    d_one, *grad_in = call(
        functools.partial(first_back_kernel, spread_in), (chan // tile,),
        [
            smem(inverse), whole(stats_one), whole(grads_one), whole(params[0]), whole(dz_one), whole(a_one),
            (masks, block((1, micros, pixels, 128), lambda c: (1, 0, 0, 0))),
            (x.reshape(total_pixels, chan), block((total_pixels, tile), lambda c: (0, c))),
            *spread_in.ins,
        ],
        [out((micros, pixels, inner), BF16, (micros, pixels, inner), lambda c: (0, 0, 0)), *spread_in.outs],
        [pltpu.VMEM((tile, inner), F32)],
        flops=2 * big * inner, nbytes=4 * big,
    )
    if sums.direct:
        d_one, *rest = in_order(d_one, *grad_in, *sums.far)
        grad_in, sums.far = rest[:2], rest[2:]
    sums_in = Sums(spread_in, grad_in)
    if sums.direct:
        d_one, *sends = in_order(d_one, *sums.send_near())
        sums.take_near(sends)
    strip = total_pixels // 4
    input_grad = call(
        input_grad_kernel, (4,),
        [
            (d_one.reshape(total_pixels, inner), block((strip, inner), lambda s: (s, 0))),
            whole(w_in),
            (d_resid.reshape(total_pixels, chan), block((strip, chan), lambda s: (s, 0))),
        ],
        [out((total_pixels, chan), BF16, (strip, chan), lambda s: (s, 0))],
        flops=2 * big * inner, nbytes=8 * big,
    )
    if sums.direct:
        input_grad, *rest = in_order(input_grad, *sums.near, *sums_in.send_far())
        sums.near = rest[:2]
        sums_in.take_far(rest[2:])
        sums.take_line(sums.send_line())
        sums_in.take_near(sums_in.send_near())
        sums_in.take_line(sums_in.send_line())
    grad_in, grad_both = sums_in.total, sums.total
    grad_mid, grad_out = grad_both[: weight_mid.shape[0]], grad_both[weight_mid.shape[0] :]

    norm_total = jnp.concatenate([grads_one[:, :2], grads_two, grads_three], axis=2)
    norm_total = jnp.sum(norm_total, axis=0)[::-1]
    local_squares = (
        jnp.sum(grad_in * grad_in) + jnp.sum(grad_both * grad_both)
    )
    total = all_sum(local_squares.reshape(1, 1)) + jnp.sum(norm_total * norm_total)
    grad_norm = jnp.sqrt(total)
    scale = CLIP / jnp.maximum(grad_norm, CLIP)
    new_in = adamw(weight_in, first_in, second_in, grad_in * scale, RATE, DECAY)
    new_mid = adamw(weight_mid, first_mid, second_mid, grad_mid * scale, RATE, DECAY)
    new_out = adamw(weight_out, first_out, second_out, (grad_out * scale).T, RATE, DECAY)
    new_norm = adamw(norm_params, norm_first, norm_second, norm_total * scale, RATE_NORM, 0.0)
    shape = (micros, 1, row_span, columns, chan)
    return (
        block_out.reshape(shape),
        input_grad.reshape(shape),
        *[group[k] for k in range(3) for group in (new_in, new_mid, new_out)],
        *new_norm,
        grad_norm.reshape(1),
    )


def solution(mesh):
    acts = P(None, "batch", "rows", None, None)
    by_row, by_col = P(("batch", "rows"), None), P(None, ("batch", "rows"))
    weights = (by_row, by_row, by_col)
    return jax.shard_map(
        per_device,
        mesh=mesh,
        in_specs=(
            acts, P(None, None, "batch", "rows", None, None), P(), P(), *(weights * 3), P(), P(), P()
        ),
        out_specs=(acts, acts, *(weights * 3), P(), P(), P(), P()),
        check_vma=False,
    )
```

profile of v0, /device:TPU:0, one launch (start us, length us, event | category | flops | bytes accessed | tf_op | source)
XLA Modules:
  0.0 371.1 jit_solution(11745101845949148458)
XLA Ops:
  10.8 5.1 %collective-permute-start.2 = (bf16[1,128,512]{2,1,0:T(8,128)(2,1)S(1)}, bf16[1,128,512]{2,1,0:T(8,128)(2,1)S(1)}, u32[]{:S(2)}, u32[]{:S(2)}) collective-permute-start(bf16[1,128,512]{2,1,0:T(8,128)(2,1)S(1)} %maximum_bitcast_fusion.refs_0_), channel_id=1, source_target_pairs={{0,6},{1,7},{2,4},{3,5},{4,2},{5,3},{6,0},{7,1},{8,14},{9,15},{10,... | collective-permute-start | bytes 393224 | tf_op jit(solution)/shard_map/ppermute | solution.py:28
  18.4 4.0 %shard_map.271.refs_4_ = f32[8,128]{1,0:T(8,128)S(1)} custom-call(bf16[3,2,1,4,96,2048]{5,4,3,2,1,0:T(8,128)(2,1)} %task_ref.5, f32[3,2,384,128]{3,2,1,0:T(8,128)S(1)} %broadcast_in_dim.4.mask_ref), custom_call_target="tpu_custom_call" | custom-call | flops 9437184 | bytes 4718592 | tf_op jit(solution)/shard_map/pallas_call | solution.py:317
  23.0 4.2 %collective-permute-done.1.refs_2_ = bf16[1,128,512]{2,1,0:T(8,128)(2,1)S(1)} collective-permute-done((bf16[1,128,512]{2,1,0:T(8,128)(2,1)S(1)}, bf16[1,128,512]{2,1,0:T(8,128)(2,1)S(1)}, u32[]{:S(2)}, u32[]{:S(2)}) %collective-permute-start.1) | collective-permute-done | bytes 131104 | tf_op jit(solution)/shard_map/ppermute | solution.py:28
  34.5 11.0 %collective-permute-done.6.refs_5_ = bf16[4,128,512]{2,1,0:T(8,128)(2,1)S(1)} collective-permute-done((bf16[4,128,512]{2,1,0:T(8,128)(2,1)}, bf16[4,128,512]{2,1,0:T(8,128)(2,1)S(1)}, u32[]{:S(2)}, u32[]{:S(2)}) %collective-permute-start.6) | collective-permute-done | bytes 524320 | tf_op jit(solution)/shard_map/ppermute | solution.py:28
  47.7 2.6 collective-permute-done.4.refs_3_
  51.5 4.0 %shard_map.272 = f32[8,128]{1,0:T(8,128)S(1)} custom-call(bf16[3,2,1,4,96,2048]{5,4,3,2,1,0:T(8,128)(2,1)} %task_ref.5, f32[3,2,384,128]{3,2,1,0:T(8,128)S(1)} %broadcast_in_dim.4.mask_ref), custom_call_target="tpu_custom_call" | custom-call | flops 9437184 | bytes 4718592 | tf_op jit(solution)/shard_map/pallas_call | solution.py:317
  60.1 6.6 %shard_map.274 = (f32[2,384,512]{2,1,0:T(8,128)}, bf16[2,384,512]{2,1,0:T(8,128)(2,1)S(1)}, f32[2,4,512]{2,1,0:T(4,128)S(1)}, bf16[2048,512]{1,0:T(8,128)(2,1)}) custom-call(bf16[2,384,2048]{2,1,0:T(8,128)(2,1)} %bitcast.122, f32[3,2,384,128]{3,2,1,0:T(8,128)S(1)} %broadcast_in_dim.4.mask_ref, f32[2,8,128]{2,1,0:T(8,128)S(1)} %pad_maximum_fusion.gram_ref, ...), custom_call_target="tpu_custom_call" | custom-call | flops 1610612736 | bytes 6291456 | tf_op jit(solution)/shard_map/pallas_call | solution.py:317
  69.7 3.1 collective-permute-start.19
  72.8 2.8 collective-permute-start.15
  80.0 3.0 collective-permute-start.18
  84.9 3.1 collective-permute-done.18
  88.1 9.4 %shard_map.275.refs_0_.up_ref = f32[2,384,2048]{2,1,0:T(8,128)} custom-call(f32[2,4,512]{2,1,0:T(4,128)S(1)} %bitcast.130, bf16[3,2,1,4,96,2048]{5,4,3,2,1,0:T(8,128)(2,1)} %task_ref.5, f32[3,2,384,128]{3,2,1,0:T(8,128)S(1)} %broadcast_in_dim.4.mask_ref), custom_call_target="tpu_custom_call" | custom-call | flops 12582912 | bytes 15728640 | tf_op jit(solution)/shard_map/pallas_call | solution.py:317
  102.8 11.9 %shard_map.276 = (bf16[3,2,384,512]{3,2,1,0:T(8,128)(2,1)}, f32[2,384,512]{2,1,0:T(8,128)S(1)}, bf16[2,384,512]{2,1,0:T(8,128)(2,1)S(1)}, f32[2,2,512]{2,1,0:T(2,128)S(1)}) custom-call(f32[2]{0:T(128)S(1)} %copy-done.15, f32[2,4,512]{2,1,0:T(4,128)S(1)} %bitcast.131, f32[2,512]{1,0:T(2,128)S(1)} %copy-done.13, ...), custom_call_target="tpu_custom_call" | custom-call | flops 3623878656 | bytes 12582912 | tf_op jit(solution)/shard_map/pallas_call | solution.py:317
  115.9 2.5 collective-permute-start.24
  125.3 2.2 collective-permute-start.25
  127.5 2.9 shard_map.277.w_ref
  132.0 7.9 %shard_map.278 = (bf16[2,384,512]{2,1,0:T(8,128)(2,1)S(1)}, f32[2,384,2048]{2,1,0:T(8,128)}, f32[2,2,2048]{2,1,0:T(2,128)S(1)}) custom-call(f32[2]{0:T(128)S(1)} %copy-done.16, f32[2,2,512]{2,1,0:T(2,128)S(1)} %add_add_fusion.10.sums_ref.stats2_ref, f32[2,512]{1,0:T(2,128)S(1)} %copy-done.10, f32[2,384,512]{2,1,0:T(8,128)S(1)} %get-tuple-element.62.a_ref.a2_ref, ...), custom_call_target="tpu_custom_call" | custom-call | flops 1610612736 | bytes 9437184 | tf_op jit(solution)/shard_map/pallas_call | solution.py:317
  146.0 3.1 collective-permute-start.35
  151.4 2.2 collective-permute-start.32
  153.6 5.6 %collective-permute-done.34 = f32[2,2,2048]{2,1,0:T(2,128)S(1)} collective-permute-done((f32[2,2,2048]{2,1,0:T(2,128)S(1)}, f32[2,2,2048]{2,1,0:T(2,128)S(1)}, u32[]{:S(2)}, u32[]{:S(2)}) %collective-permute-start.34) | collective-permute-done | bytes 32800 | tf_op jit(solution)/shard_map/ppermute | solution.py:28
  160.5 13.1 %shard_map.279 = (bf16[2,384,2048]{2,1,0:T(8,128)(2,1)}, f32[2,384,2048]{2,1,0:T(8,128)}, f32[2,2,2048]{2,1,0:T(2,128)S(1)}) custom-call(f32[2]{0:T(128)S(1)} %copy-done.16, f32[2,2,2048]{2,1,0:T(2,128)S(1)} %add_add_fusion.2.sums_ref.stats3_ref, f32[2,2048]{1,0:T(2,128)S(1)} %slice.169.param_ref.param3_ref, f32[2,384,2048]{2,1,0:T(8,128)} %get-tuple-element.64.a_ref.a3_ref, ...), custom_call_target="tpu_custom_call" | custom-call | flops 62914560 | bytes 25165824 | tf_op jit(solution)/shard_map/pallas_call | solution.py:317
  180.6 3.8 %collective-permute-start.43 = (f32[2,2,2048]{2,1,0:T(2,128)S(1)}, f32[2,2,2048]{2,1,0:T(2,128)S(1)}, u32[]{:S(2)}, u32[]{:S(2)}) collective-permute-start(f32[2,2,2048]{2,1,0:T(2,128)S(1)} %add_add_fusion.1), channel_id=1, source_target_pairs={{0,6},{1,7},{2,4},{3,5},{4,2},{5,3},{6,0},{7,1},{8,14},{9,15},{10,... | collective-permute-start | bytes 98312 | tf_op jit(solution)/shard_map/ppermute | solution.py:28
  186.7 2.5 collective-permute-done.42
  189.2 9.5 %shard_map.280 = (bf16[2,384,2048]{2,1,0:T(8,128)(2,1)}, f32[2,384,512]{2,1,0:T(8,128)S(1)}, bf16[2,384,512]{2,1,0:T(8,128)(2,1)S(1)}, f32[2,2,512]{2,1,0:T(2,128)S(1)}) custom-call(f32[2]{0:T(128)S(1)} %copy-done.16, f32[2,2,2048]{2,1,0:T(2,128)S(1)} %add_add_fusion.2.sums_ref.stats3_ref, f32[2,2,2048]{2,1,0:T(2,128)S(1)} %add_add_fusion.grads3_ref, ...), custom_call_target="tpu_custom_call" | custom-call | flops 1610612736 | bytes 15728640 | tf_op jit(solution)/shard_map/pallas_call | solution.py:317
  201.2 3.3 collective-permute-start.51
  206.1 2.3 collective-permute-start.47
  219.6 4.7 %shard_map.281 = (bf16[2,384,1536]{2,1,0:T(8,128)(2,1)}, bf16[2,384,1536]{2,1,0:T(8,128)(2,1)}) custom-call(f32[2]{0:T(128)S(1)} %copy-done.16, f32[2,2,512]{2,1,0:T(2,128)S(1)} %add_add_fusion.10.sums_ref.stats2_ref, f32[2,2,512]{2,1,0:T(2,128)S(1)} %add_add_fusion.8.grads2_ref, f32[2,512]{1,0:T(2,128)S(1)} %copy-done.10, ...), custom_call_target="tpu_custom_call" | custom-call | flops 23592960 | bytes 11010048 | tf_op jit(solution)/shard_map/pallas_call | solution.py:317
  225.9 12.6 %shard_map.282 = (bf16[16,208,512]{2,1,0:T(8,128)(2,1)}, bf16[16,208,512]{2,1,0:T(8,128)(2,1)}) custom-call(bf16[3,768,512]{2,1,0:T(8,128)(2,1)S(1)} %bitcast.136, bf16[768,1536]{1,0:T(8,128)(2,1)S(1)} %bitcast.137, bf16[768,2048]{1,0:T(8,128)(2,1)} %bitcast.162, bf16[768,512]{1,0:T(8,128)(2,1)S(1)} %bitcast.138, s32[16]{0:T(128)S(1)} %fusion.25.place_ref, ...), custom_call_target="tpu_custom_call" | custom-call | flops 5234491392 | bytes 9437184 | tf_op jit(solution)/shard_map/pallas_call | solution.py:317
  238.6 8.1 %shard_map.283 = (f32[2,384,512]{2,1,0:T(8,128)S(1)}, f32[2,2,512]{2,1,0:T(2,128)S(1)}) custom-call(f32[2]{0:T(128)S(1)} %copy-done.16, f32[2,4,512]{2,1,0:T(4,128)S(1)} %bitcast.132, f32[2,512]{1,0:T(2,128)S(1)} %copy-done.14, bf16[2,384,1536]{2,1,0:T(8,128)(2,1)} %get-tuple-element.72.cat_ref, f32[2,384,512]{2,1,0:T(8,128)S(1)} %copy-done.2, ...), custom_call_target="tpu_custom_call" | custom-call | flops 3623878656 | bytes 16515072 | tf_op jit(solution)/shard_map/pallas_call | solution.py:317
  258.3 2.1 collective-permute-start.60
  265.0 5.5 %shard_map.284 = (bf16[2,384,512]{2,1,0:T(8,128)(2,1)S(1)}, bf16[16,64,512]{2,1,0:T(8,128)(2,1)S(1)}, bf16[16,64,512]{2,1,0:T(8,128)(2,1)S(1)}) custom-call(f32[2]{0:T(128)S(1)} %copy-done.16, f32[2,4,512]{2,1,0:T(4,128)S(1)} %bitcast.133, f32[2,2,512]{2,1,0:T(2,128)S(1)} %add_add_fusion.6.grads_ref, f32[2,512]{1,0:T(2,128)S(1)} %copy-done.14, ...), custom_call_target="tpu_custom_call" | custom-call | flops 1610612736 | bytes 6291456 | tf_op jit(solution)/shard_map/pallas_call | solution.py:317
  270.6 5.0 %collective-permute-done.61 = bf16[2,2,208,512]{3,2,1,0:T(8,128)(2,1)} collective-permute-done((bf16[2,2,208,512]{3,2,1,0:T(8,128)(2,1)}, bf16[2,2,208,512]{3,2,1,0:T(8,128)(2,1)}, u32[]{:S(2)}, u32[]{:S(2)}) %collective-permute-start.61) | collective-permute-done | bytes 852000 | tf_op jit(solution)/shard_map/ppermute | solution.py:28
  280.1 6.7 %shard_map.285 = bf16[768,2048]{1,0:T(8,128)(2,1)} custom-call(bf16[768,512]{1,0:T(8,128)(2,1)S(1)} %bitcast.129, bf16[2048,512]{1,0:T(8,128)(2,1)S(1)} %copy-done.4, f32[768,2048]{1,0:T(8,128)} %bitcast.139), custom_call_target="tpu_custom_call" | custom-call | flops 1610612736 | bytes 12582912 | tf_op jit(solution)/shard_map/pallas_call | solution.py:317
  287.7 2.7 collective-permute-done.63
  294.5 3.9 %collective-permute-done.66 = bf16[2,2,64,512]{3,2,1,0:T(8,128)(2,1)S(1)} collective-permute-done((bf16[2,2,64,512]{3,2,1,0:T(8,128)(2,1)S(1)}, bf16[2,2,64,512]{3,2,1,0:T(8,128)(2,1)S(1)}, u32[]{:S(2)}, u32[]{:S(2)}) %collective-permute-start.66) | collective-permute-done | bytes 262176 | tf_op jit(solution)/shard_map/ppermute | solution.py:28
  300.5 2.4 fusion.4
  307.3 2.3 collective-permute-start.75
  309.9 2.1 collective-permute-start.71
  312.6 2.7 collective-permute-start.72
  315.3 10.0 %collective-permute-done.74 = bf16[1,208,512]{2,1,0:T(8,128)(2,1)S(1)} collective-permute-done((bf16[1,208,512]{2,1,0:T(8,128)(2,1)S(1)}, bf16[1,208,512]{2,1,0:T(8,128)(2,1)S(1)}, u32[]{:S(2)}, u32[]{:S(2)}) %collective-permute-start.74) | collective-permute-done | bytes 213024 | tf_op jit(solution)/shard_map/ppermute | solution.py:28
  326.0 4.2 %collective-permute-done.71 = bf16[1,64,512]{2,1,0:T(8,128)(2,1)S(1)} collective-permute-done((bf16[1,64,512]{2,1,0:T(8,128)(2,1)S(1)}, bf16[1,64,512]{2,1,0:T(8,128)(2,1)S(1)}, u32[]{:S(2)}, u32[]{:S(2)}) %collective-permute-start.71) | collective-permute-done | bytes 65568 | tf_op jit(solution)/shard_map/ppermute | solution.py:28
  334.1 2.6 collective-permute-start.79
  336.7 2.5 collective-permute-start.78
  339.2 2.3 collective-permute-start.77
  344.5 3.1 collective-permute-start.82
  347.7 2.2 collective-permute-start.81
  349.9 3.0 collective-permute-start.80
  359.2 2.1 multiply_subtract_fusion
  (276 shorter events, 124.6 us)
Async XLA Ops:
  7.2 92.0 %all-gather.2.cloned.1.call-start = ((), (), s32[]{:S(2)}) async-start(), calls=%async_computation | async-start | bytes 4866048 | tf_op jit(solution)/shard_map/all_gather | solution.py:778
  10.8 12.2 %collective-permute-start.2 = (bf16[1,128,512]{2,1,0:T(8,128)(2,1)S(1)}, bf16[1,128,512]{2,1,0:T(8,128)(2,1)S(1)}, u32[]{:S(2)}, u32[]{:S(2)}) collective-permute-start(bf16[1,128,512]{2,1,0:T(8,128)(2,1)S(1)} %maximum_bitcast_fusion.refs_0_), channel_id=1, source_target_pairs={{0,6},{1,7},{2,4},{3,5},{4,2},{5,3},{6,0},{7,1},{8,14},{9,15},{10,... | collective-permute-start | bytes 393224 | tf_op jit(solution)/shard_map/ppermute | solution.py:28
  15.9 11.3 %collective-permute-start.1 = (bf16[1,128,512]{2,1,0:T(8,128)(2,1)S(1)}, bf16[1,128,512]{2,1,0:T(8,128)(2,1)S(1)}, u32[]{:S(2)}, u32[]{:S(2)}) collective-permute-start(bf16[1,128,512]{2,1,0:T(8,128)(2,1)S(1)} %maximum_bitcast_fusion.refs_0_), channel_id=1, source_target_pairs={{0,4},{1,5},{2,6},{3,7},{4,0},{5,1},{6,2},{7,3},{8,12},{9,13},{10,... | collective-permute-start | bytes 393224 | tf_op jit(solution)/shard_map/ppermute | solution.py:28
  15.9 11.3 %collective-permute-start = (bf16[1,128,512]{2,1,0:T(8,128)(2,1)S(1)}, bf16[1,128,512]{2,1,0:T(8,128)(2,1)S(1)}, u32[]{:S(2)}, u32[]{:S(2)}) collective-permute-start(bf16[1,128,512]{2,1,0:T(8,128)(2,1)S(1)} %maximum_bitcast_fusion.refs_0_), channel_id=1, source_target_pairs={{0,2},{1,3},{2,0},{3,1},{4,6},{5,7},{6,4},{7,5},{8,10},{9,11},{10,... | collective-permute-start | bytes 393224 | tf_op jit(solution)/shard_map/ppermute | solution.py:28
  30.4 15.1 %collective-permute-start.6 = (bf16[4,128,512]{2,1,0:T(8,128)(2,1)}, bf16[4,128,512]{2,1,0:T(8,128)(2,1)S(1)}, u32[]{:S(2)}, u32[]{:S(2)}) collective-permute-start(bf16[4,128,512]{2,1,0:T(8,128)(2,1)} %shard_map.273.refs_1_), channel_id=1, source_target_pairs={{0,16},{8,24},{16,0},{24,8},{1,17},{9,25},{17,1},{25,9},{2,18},{10... | collective-permute-start | bytes 1572872 | tf_op jit(solution)/shard_map/ppermute | solution.py:28
  31.9 18.3 %collective-permute-start.4 = (bf16[4,128,512]{2,1,0:T(8,128)(2,1)}, bf16[4,128,512]{2,1,0:T(8,128)(2,1)S(1)}, u32[]{:S(2)}, u32[]{:S(2)}) collective-permute-start(bf16[4,128,512]{2,1,0:T(8,128)(2,1)} %shard_map.273.refs_1_), channel_id=1, source_target_pairs={{0,8},{8,0},{16,24},{24,16},{1,9},{9,1},{17,25},{25,17},{2,10},{10... | collective-permute-start | bytes 1572872 | tf_op jit(solution)/shard_map/ppermute | solution.py:28
  46.2 10.6 %collective-permute-start.10 = (bf16[2,128,512]{2,1,0:T(8,128)(2,1)}, bf16[2,128,512]{2,1,0:T(8,128)(2,1)S(1)}, u32[]{:S(2)}, u32[]{:S(2)}) collective-permute-start(bf16[2,128,512]{2,1,0:T(8,128)(2,1)} %slice.213), channel_id=1, source_target_pairs={{0,8},{8,0},{16,24},{24,16},{1,9},{9,1},{17,25},{25,17},{2,10},{10... | collective-permute-start | bytes 786440 | tf_op jit(solution)/shard_map/ppermute | solution.py:28
  51.0 6.7 %collective-permute-start.8 = (bf16[2,128,512]{2,1,0:T(8,128)(2,1)}, bf16[2,128,512]{2,1,0:T(8,128)(2,1)}, u32[]{:S(2)}, u32[]{:S(2)}) collective-permute-start(bf16[2,128,512]{2,1,0:T(8,128)(2,1)} %slice.212), channel_id=1, source_target_pairs={{0,16},{8,24},{16,0},{24,8},{1,17},{9,25},{17,1},{25,9},{2,18},{10... | collective-permute-start | bytes 786440 | tf_op jit(solution)/shard_map/ppermute | solution.py:28
  66.7 6.1 %collective-permute-start.12 = (f32[2,4,512]{2,1,0:T(4,128)S(1)}, f32[2,4,512]{2,1,0:T(4,128)S(1)}, u32[]{:S(2)}, u32[]{:S(2)}) collective-permute-start(f32[2,4,512]{2,1,0:T(4,128)S(1)} %get-tuple-element.58), channel_id=1, source_target_pairs={{0,1},{1,0},{2,3},{3,2},{4,5},{5,4},{6,7},{7,6},{8,9},{9,8},{10,11... | collective-permute-start | bytes 49160 | tf_op jit(solution)/shard_map/ppermute | solution.py:28
  68.4 29.0 %collective-permute-start.20 = (bf16[2,384,512]{2,1,0:T(8,128)(2,1)S(1)}, bf16[2,384,512]{2,1,0:T(8,128)(2,1)S(1)}, u32[]{:S(2)}, u32[]{:S(2)}) collective-permute-start(bf16[2,384,512]{2,1,0:T(8,128)(2,1)S(1)} %get-tuple-element.60), channel_id=1, source_target_pairs={{1,0},{2,1},{3,2},{4,3},{5,4},{6,5},{7,6},{9,8},{10,9},{11,10},{12... | collective-permute-start | bytes 2359304 | tf_op jit(solution)/shard_map/ppermute | solution.py:751
  69.7 28.6 %collective-permute-start.19 = (bf16[2,384,512]{2,1,0:T(8,128)(2,1)S(1)}, bf16[2,384,512]{2,1,0:T(8,128)(2,1)S(1)}, u32[]{:S(2)}, u32[]{:S(2)}) collective-permute-start(bf16[2,384,512]{2,1,0:T(8,128)(2,1)S(1)} %get-tuple-element.60), channel_id=1, source_target_pairs={{0,1},{1,2},{2,3},{3,4},{4,5},{5,6},{6,7},{8,9},{9,10},{10,11},{11... | collective-permute-start | bytes 2359304 | tf_op jit(solution)/shard_map/ppermute | solution.py:750
  80.0 8.1 %collective-permute-start.18 = (f32[2,4,512]{2,1,0:T(4,128)S(1)}, f32[2,4,512]{2,1,0:T(4,128)S(1)}, u32[]{:S(2)}, u32[]{:S(2)}) collective-permute-start(f32[2,4,512]{2,1,0:T(4,128)S(1)} %bitcast.151), channel_id=1, source_target_pairs={{0,6},{1,7},{2,4},{3,5},{4,2},{5,3},{6,0},{7,1},{8,14},{9,15},{10,... | collective-permute-start | bytes 49160 | tf_op jit(solution)/shard_map/ppermute | solution.py:28
  83.0 5.1 %collective-permute-start.17 = (f32[2,4,512]{2,1,0:T(4,128)S(1)}, f32[2,4,512]{2,1,0:T(4,128)S(1)}, u32[]{:S(2)}, u32[]{:S(2)}) collective-permute-start(f32[2,4,512]{2,1,0:T(4,128)S(1)} %bitcast.152), channel_id=1, source_target_pairs={{0,4},{1,5},{2,6},{3,7},{4,0},{5,1},{6,2},{7,3},{8,12},{9,13},{10,... | collective-permute-start | bytes 49160 | tf_op jit(solution)/shard_map/ppermute | solution.py:28
  123.0 7.3 %collective-permute-start.27 = (f32[2,2,512]{2,1,0:T(2,128)S(1)}, f32[2,2,512]{2,1,0:T(2,128)S(1)}, u32[]{:S(2)}, u32[]{:S(2)}) collective-permute-start(f32[2,2,512]{2,1,0:T(2,128)S(1)} %add_add_fusion.11), channel_id=1, source_target_pairs={{0,6},{1,7},{2,4},{3,5},{4,2},{5,3},{6,0},{7,1},{8,14},{9,15},{10,... | collective-permute-start | bytes 24584 | tf_op jit(solution)/shard_map/ppermute | solution.py:28
  124.0 6.3 %collective-permute-start.26 = (f32[2,2,512]{2,1,0:T(2,128)S(1)}, f32[2,2,512]{2,1,0:T(2,128)S(1)}, u32[]{:S(2)}, u32[]{:S(2)}) collective-permute-start(f32[2,2,512]{2,1,0:T(2,128)S(1)} %add_add_fusion.11), channel_id=1, source_target_pairs={{0,4},{1,5},{2,6},{3,7},{4,0},{5,1},{6,2},{7,3},{8,12},{9,13},{10,... | collective-permute-start | bytes 24584 | tf_op jit(solution)/shard_map/ppermute | solution.py:28
  125.3 5.1 %collective-permute-start.25 = (f32[2,2,512]{2,1,0:T(2,128)S(1)}, f32[2,2,512]{2,1,0:T(2,128)S(1)}, u32[]{:S(2)}, u32[]{:S(2)}) collective-permute-start(f32[2,2,512]{2,1,0:T(2,128)S(1)} %add_add_fusion.11), channel_id=1, source_target_pairs={{0,2},{1,3},{2,0},{3,1},{4,6},{5,7},{6,4},{7,5},{8,10},{9,11},{10,... | collective-permute-start | bytes 24584 | tf_op jit(solution)/shard_map/ppermute | solution.py:28
  141.1 7.9 %collective-permute-start.31 = (f32[2,2,2048]{2,1,0:T(2,128)S(1)}, f32[2,2,2048]{2,1,0:T(2,128)S(1)}, u32[]{:S(2)}, u32[]{:S(2)}) collective-permute-start(f32[2,2,2048]{2,1,0:T(2,128)S(1)} %add.534), channel_id=1, source_target_pairs={{0,24},{8,16},{16,8},{24,0},{1,25},{9,17},{17,9},{25,1},{2,26},{10... | collective-permute-start | bytes 98312 | tf_op jit(solution)/shard_map/ppermute | solution.py:28
  142.6 6.5 %collective-permute-start.30 = (f32[2,2,2048]{2,1,0:T(2,128)S(1)}, f32[2,2,2048]{2,1,0:T(2,128)S(1)}, u32[]{:S(2)}, u32[]{:S(2)}) collective-permute-start(f32[2,2,2048]{2,1,0:T(2,128)S(1)} %add.534), channel_id=1, source_target_pairs={{0,16},{8,24},{16,0},{24,8},{1,17},{9,25},{17,1},{25,9},{2,18},{10... | collective-permute-start | bytes 98312 | tf_op jit(solution)/shard_map/ppermute | solution.py:28
  142.7 6.4 %collective-permute-start.29 = (f32[2,2,2048]{2,1,0:T(2,128)S(1)}, f32[2,2,2048]{2,1,0:T(2,128)S(1)}, u32[]{:S(2)}, u32[]{:S(2)}) collective-permute-start(f32[2,2,2048]{2,1,0:T(2,128)S(1)} %add.534), channel_id=1, source_target_pairs={{0,8},{8,0},{16,24},{24,16},{1,9},{9,1},{17,25},{25,17},{2,10},{10... | collective-permute-start | bytes 98312 | tf_op jit(solution)/shard_map/ppermute | solution.py:28
  144.7 15.8 %collective-permute-start.36 = (bf16[2,384,512]{2,1,0:T(8,128)(2,1)S(1)}, bf16[2,384,512]{2,1,0:T(8,128)(2,1)S(1)}, u32[]{:S(2)}, u32[]{:S(2)}) collective-permute-start(bf16[2,384,512]{2,1,0:T(8,128)(2,1)S(1)} %get-tuple-element.65), channel_id=1, source_target_pairs={{1,0},{2,1},{3,2},{4,3},{5,4},{6,5},{7,6},{9,8},{10,9},{11,10},{12... | collective-permute-start | bytes 2359304 | tf_op jit(solution)/shard_map/ppermute | solution.py:751
  146.0 14.5 %collective-permute-start.35 = (bf16[2,384,512]{2,1,0:T(8,128)(2,1)S(1)}, bf16[2,384,512]{2,1,0:T(8,128)(2,1)S(1)}, u32[]{:S(2)}, u32[]{:S(2)}) collective-permute-start(bf16[2,384,512]{2,1,0:T(8,128)(2,1)S(1)} %get-tuple-element.65), channel_id=1, source_target_pairs={{0,1},{1,2},{2,3},{3,4},{4,5},{5,6},{6,7},{8,9},{9,10},{10,11},{11... | collective-permute-start | bytes 2359304 | tf_op jit(solution)/shard_map/ppermute | solution.py:750
  149.1 10.0 %collective-permute-start.34 = (f32[2,2,2048]{2,1,0:T(2,128)S(1)}, f32[2,2,2048]{2,1,0:T(2,128)S(1)}, u32[]{:S(2)}, u32[]{:S(2)}) collective-permute-start(f32[2,2,2048]{2,1,0:T(2,128)S(1)} %add_add_fusion.3), channel_id=1, source_target_pairs={{0,6},{1,7},{2,4},{3,5},{4,2},{5,3},{6,0},{7,1},{8,14},{9,15},{10,... | collective-permute-start | bytes 98312 | tf_op jit(solution)/shard_map/ppermute | solution.py:28
  150.3 10.2 %collective-permute-start.33 = (f32[2,2,2048]{2,1,0:T(2,128)S(1)}, f32[2,2,2048]{2,1,0:T(2,128)S(1)}, u32[]{:S(2)}, u32[]{:S(2)}) collective-permute-start(f32[2,2,2048]{2,1,0:T(2,128)S(1)} %add_add_fusion.3), channel_id=1, source_target_pairs={{0,4},{1,5},{2,6},{3,7},{4,0},{5,1},{6,2},{7,3},{8,12},{9,13},{10,... | collective-permute-start | bytes 98312 | tf_op jit(solution)/shard_map/ppermute | solution.py:28
  151.4 9.1 %collective-permute-start.32 = (f32[2,2,2048]{2,1,0:T(2,128)S(1)}, f32[2,2,2048]{2,1,0:T(2,128)S(1)}, u32[]{:S(2)}, u32[]{:S(2)}) collective-permute-start(f32[2,2,2048]{2,1,0:T(2,128)S(1)} %add_add_fusion.3), channel_id=1, source_target_pairs={{0,2},{1,3},{2,0},{3,1},{4,6},{5,7},{6,4},{7,5},{8,10},{9,11},{10,... | collective-permute-start | bytes 98312 | tf_op jit(solution)/shard_map/ppermute | solution.py:28
  180.6 6.1 %collective-permute-start.43 = (f32[2,2,2048]{2,1,0:T(2,128)S(1)}, f32[2,2,2048]{2,1,0:T(2,128)S(1)}, u32[]{:S(2)}, u32[]{:S(2)}) collective-permute-start(f32[2,2,2048]{2,1,0:T(2,128)S(1)} %add_add_fusion.1), channel_id=1, source_target_pairs={{0,6},{1,7},{2,4},{3,5},{4,2},{5,3},{6,0},{7,1},{8,14},{9,15},{10,... | collective-permute-start | bytes 98312 | tf_op jit(solution)/shard_map/ppermute | solution.py:28
  199.9 19.7 %collective-permute-start.52 = (bf16[2,384,512]{2,1,0:T(8,128)(2,1)S(1)}, bf16[2,384,512]{2,1,0:T(8,128)(2,1)S(1)}, u32[]{:S(2)}, u32[]{:S(2)}) collective-permute-start(bf16[2,384,512]{2,1,0:T(8,128)(2,1)S(1)} %get-tuple-element.71), channel_id=1, source_target_pairs={{1,0},{2,1},{3,2},{4,3},{5,4},{6,5},{7,6},{9,8},{10,9},{11,10},{12... | collective-permute-start | bytes 2359304 | tf_op jit(solution)/shard_map/ppermute | solution.py:751
  201.2 18.4 %collective-permute-start.51 = (bf16[2,384,512]{2,1,0:T(8,128)(2,1)S(1)}, bf16[2,384,512]{2,1,0:T(8,128)(2,1)S(1)}, u32[]{:S(2)}, u32[]{:S(2)}) collective-permute-start(bf16[2,384,512]{2,1,0:T(8,128)(2,1)S(1)} %get-tuple-element.71), channel_id=1, source_target_pairs={{0,1},{1,2},{2,3},{3,4},{4,5},{5,6},{6,7},{8,9},{9,10},{10,11},{11... | collective-permute-start | bytes 2359304 | tf_op jit(solution)/shard_map/ppermute | solution.py:750
  213.0 5.5 %collective-permute-start.50 = (f32[2,2,512]{2,1,0:T(2,128)S(1)}, f32[2,2,512]{2,1,0:T(2,128)S(1)}, u32[]{:S(2)}, u32[]{:S(2)}) collective-permute-start(f32[2,2,512]{2,1,0:T(2,128)S(1)} %add_add_fusion.9), channel_id=1, source_target_pairs={{0,6},{1,7},{2,4},{3,5},{4,2},{5,3},{6,0},{7,1},{8,14},{9,15},{10,... | collective-permute-start | bytes 24584 | tf_op jit(solution)/shard_map/ppermute | solution.py:28
  238.5 14.9 %collective-permute-start.57 = (bf16[16,208,512]{2,1,0:T(8,128)(2,1)}, bf16[16,208,512]{2,1,0:T(8,128)(2,1)S(1)}, u32[]{:S(2)}, u32[]{:S(2)}) collective-permute-start(bf16[16,208,512]{2,1,0:T(8,128)(2,1)} %get-tuple-element.77.after_ref), channel_id=1, source_target_pairs={{0,1},{1,0},{2,3},{3,2},{4,5},{5,4},{6,7},{7,6},{8,9},{9,8},{10,11... | collective-permute-start | bytes 10223624 | tf_op jit(solution)/shard_map/ppermute | solution.py:28
  255.4 20.2 %collective-permute-start.61 = (bf16[2,2,208,512]{3,2,1,0:T(8,128)(2,1)}, bf16[2,2,208,512]{3,2,1,0:T(8,128)(2,1)}, u32[]{:S(2)}, u32[]{:S(2)}) collective-permute-start(bf16[2,2,208,512]{3,2,1,0:T(8,128)(2,1)} %get-tuple-element.85), channel_id=1, source_target_pairs={{0,8},{8,0},{16,24},{24,16},{1,9},{9,1},{17,25},{25,17},{2,10},{10... | collective-permute-start | bytes 2555912 | tf_op jit(solution)/shard_map/ppermute | solution.py:28
  257.2 19.3 %collective-permute-start.62 = (bf16[2,2,208,512]{3,2,1,0:T(8,128)(2,1)S(1)}, bf16[2,2,208,512]{3,2,1,0:T(8,128)(2,1)}, u32[]{:S(2)}, u32[]{:S(2)}) collective-permute-start(bf16[2,2,208,512]{3,2,1,0:T(8,128)(2,1)S(1)} %get-tuple-element.86), channel_id=1, source_target_pairs={{0,16},{8,24},{16,0},{24,8},{1,17},{9,25},{17,1},{25,9},{2,18},{10... | collective-permute-start | bytes 2555912 | tf_op jit(solution)/shard_map/ppermute | solution.py:28
  258.3 5.4 %collective-permute-start.60 = (f32[2,2,512]{2,1,0:T(2,128)S(1)}, f32[2,2,512]{2,1,0:T(2,128)S(1)}, u32[]{:S(2)}, u32[]{:S(2)}) collective-permute-start(f32[2,2,512]{2,1,0:T(2,128)S(1)} %add_add_fusion.7), channel_id=1, source_target_pairs={{0,6},{1,7},{2,4},{3,5},{4,2},{5,3},{6,0},{7,1},{8,14},{9,15},{10,... | collective-permute-start | bytes 24584 | tf_op jit(solution)/shard_map/ppermute | solution.py:28
  276.5 10.3 %collective-permute-start.65 = (bf16[16,64,512]{2,1,0:T(8,128)(2,1)S(1)}, bf16[16,64,512]{2,1,0:T(8,128)(2,1)S(1)}, u32[]{:S(2)}, u32[]{:S(2)}) collective-permute-start(bf16[16,64,512]{2,1,0:T(8,128)(2,1)S(1)} %get-tuple-element.95), channel_id=1, source_target_pairs={{0,1},{1,0},{2,3},{3,2},{4,5},{5,4},{6,7},{7,6},{8,9},{9,8},{10,11... | collective-permute-start | bytes 3145736 | tf_op jit(solution)/shard_map/ppermute | solution.py:28
  278.0 12.4 %collective-permute-start.63 = (bf16[2,208,512]{2,1,0:T(8,128)(2,1)S(1)}, bf16[2,208,512]{2,1,0:T(8,128)(2,1)}, u32[]{:S(2)}, u32[]{:S(2)}) collective-permute-start(bf16[2,208,512]{2,1,0:T(8,128)(2,1)S(1)} %get-tuple-element.92), channel_id=1, source_target_pairs={{0,8},{8,0},{16,24},{24,16},{1,9},{9,1},{17,25},{25,17},{2,10},{10... | collective-permute-start | bytes 1277960 | tf_op jit(solution)/shard_map/ppermute | solution.py:28
  278.7 12.1 %collective-permute-start.64 = (bf16[2,208,512]{2,1,0:T(8,128)(2,1)S(1)}, bf16[2,208,512]{2,1,0:T(8,128)(2,1)}, u32[]{:S(2)}, u32[]{:S(2)}) collective-permute-start(bf16[2,208,512]{2,1,0:T(8,128)(2,1)S(1)} %get-tuple-element.93), channel_id=1, source_target_pairs={{0,16},{8,24},{16,0},{24,8},{1,17},{9,25},{17,1},{25,9},{2,18},{10... | collective-permute-start | bytes 1277960 | tf_op jit(solution)/shard_map/ppermute | solution.py:28
  290.7 7.6 %collective-permute-start.66 = (bf16[2,2,64,512]{3,2,1,0:T(8,128)(2,1)S(1)}, bf16[2,2,64,512]{3,2,1,0:T(8,128)(2,1)S(1)}, u32[]{:S(2)}, u32[]{:S(2)}) collective-permute-start(bf16[2,2,64,512]{3,2,1,0:T(8,128)(2,1)S(1)} %get-tuple-element.97), channel_id=1, source_target_pairs={{0,8},{8,0},{16,24},{24,16},{1,9},{9,1},{17,25},{25,17},{2,10},{10... | collective-permute-start | bytes 786440 | tf_op jit(solution)/shard_map/ppermute | solution.py:28
  293.4 11.2 %collective-permute-start.69 = (bf16[2,2,64,512]{3,2,1,0:T(8,128)(2,1)}, bf16[2,2,64,512]{3,2,1,0:T(8,128)(2,1)S(1)}, u32[]{:S(2)}, u32[]{:S(2)}) collective-permute-start(bf16[2,2,64,512]{3,2,1,0:T(8,128)(2,1)} %get-tuple-element.98), channel_id=1, source_target_pairs={{0,16},{8,24},{16,0},{24,8},{1,17},{9,25},{17,1},{25,9},{2,18},{10... | collective-permute-start | bytes 786440 | tf_op jit(solution)/shard_map/ppermute | solution.py:28
  299.1 5.5 %collective-permute-start.67 = (bf16[2,64,512]{2,1,0:T(8,128)(2,1)S(1)}, bf16[2,64,512]{2,1,0:T(8,128)(2,1)S(1)}, u32[]{:S(2)}, u32[]{:S(2)}) collective-permute-start(bf16[2,64,512]{2,1,0:T(8,128)(2,1)S(1)} %fusion.16), channel_id=1, source_target_pairs={{0,16},{8,24},{16,0},{24,8},{1,17},{9,25},{17,1},{25,9},{2,18},{10... | collective-permute-start | bytes 393224 | tf_op jit(solution)/shard_map/ppermute | solution.py:28
  303.0 9.6 %collective-permute-start.73 = (bf16[1,208,512]{2,1,0:T(8,128)(2,1)S(1)}, bf16[1,208,512]{2,1,0:T(8,128)(2,1)S(1)}, u32[]{:S(2)}, u32[]{:S(2)}) collective-permute-start(bf16[1,208,512]{2,1,0:T(8,128)(2,1)S(1)} %slice.318), channel_id=1, source_target_pairs={{0,2},{1,3},{2,0},{3,1},{4,6},{5,7},{6,4},{7,5},{8,10},{9,11},{10,... | collective-permute-start | bytes 638984 | tf_op jit(solution)/shard_map/ppermute | solution.py:28
  305.9 19.4 %collective-permute-start.74 = (bf16[1,208,512]{2,1,0:T(8,128)(2,1)S(1)}, bf16[1,208,512]{2,1,0:T(8,128)(2,1)S(1)}, u32[]{:S(2)}, u32[]{:S(2)}) collective-permute-start(bf16[1,208,512]{2,1,0:T(8,128)(2,1)S(1)} %get-tuple-element.157), channel_id=1, source_target_pairs={{0,4},{1,5},{2,6},{3,7},{4,0},{5,1},{6,2},{7,3},{8,12},{9,13},{10,... | collective-permute-start | bytes 638984 | tf_op jit(solution)/shard_map/ppermute | solution.py:28
  307.3 18.0 %collective-permute-start.75 = (bf16[1,208,512]{2,1,0:T(8,128)(2,1)S(1)}, bf16[1,208,512]{2,1,0:T(8,128)(2,1)S(1)}, u32[]{:S(2)}, u32[]{:S(2)}) collective-permute-start(bf16[1,208,512]{2,1,0:T(8,128)(2,1)S(1)} %get-tuple-element.158), channel_id=1, source_target_pairs={{0,6},{1,7},{2,4},{3,5},{4,2},{5,3},{6,0},{7,1},{8,14},{9,15},{10,... | collective-permute-start | bytes 638984 | tf_op jit(solution)/shard_map/ppermute | solution.py:28
  309.7 16.4 %collective-permute-start.68 = (bf16[1,64,512]{2,1,0:T(8,128)(2,1)S(1)}, bf16[1,64,512]{2,1,0:T(8,128)(2,1)S(1)}, u32[]{:S(2)}, u32[]{:S(2)}) collective-permute-start(bf16[1,64,512]{2,1,0:T(8,128)(2,1)S(1)} %slice.319), channel_id=1, source_target_pairs={{0,2},{1,3},{2,0},{3,1},{4,6},{5,7},{6,4},{7,5},{8,10},{9,11},{10,... | collective-permute-start | bytes 196616 | tf_op jit(solution)/shard_map/ppermute | solution.py:28
  309.9 20.4 %collective-permute-start.71 = (bf16[1,64,512]{2,1,0:T(8,128)(2,1)S(1)}, bf16[1,64,512]{2,1,0:T(8,128)(2,1)S(1)}, u32[]{:S(2)}, u32[]{:S(2)}) collective-permute-start(bf16[1,64,512]{2,1,0:T(8,128)(2,1)S(1)} %get-tuple-element.159), channel_id=1, source_target_pairs={{0,4},{1,5},{2,6},{3,7},{4,0},{5,1},{6,2},{7,3},{8,12},{9,13},{10,... | collective-permute-start | bytes 196616 | tf_op jit(solution)/shard_map/ppermute | solution.py:28
  312.6 17.7 %collective-permute-start.72 = (bf16[1,64,512]{2,1,0:T(8,128)(2,1)S(1)}, bf16[1,64,512]{2,1,0:T(8,128)(2,1)S(1)}, u32[]{:S(2)}, u32[]{:S(2)}) collective-permute-start(bf16[1,64,512]{2,1,0:T(8,128)(2,1)S(1)} %get-tuple-element.160), channel_id=1, source_target_pairs={{0,6},{1,7},{2,4},{3,5},{4,2},{5,3},{6,0},{7,1},{8,14},{9,15},{10,... | collective-permute-start | bytes 196616 | tf_op jit(solution)/shard_map/ppermute | solution.py:28
  334.1 9.2 %collective-permute-start.79 = (f32[1,1]{1,0:T(1,128)}, f32[1,1]{1,0:T(1,128)}, u32[]{:S(2)}, u32[]{:S(2)}) collective-permute-start(f32[1,1]{1,0:T(1,128)} %add.605), channel_id=1, source_target_pairs={{0,24},{8,16},{16,8},{24,0},{1,25},{9,17},{17,9},{25,1},{2,26},{10... | collective-permute-start | bytes 20 | tf_op jit(solution)/shard_map/ppermute | solution.py:28
  336.7 6.7 %collective-permute-start.78 = (f32[1,1]{1,0:T(1,128)}, f32[1,1]{1,0:T(1,128)}, u32[]{:S(2)}, u32[]{:S(2)}) collective-permute-start(f32[1,1]{1,0:T(1,128)} %add.605), channel_id=1, source_target_pairs={{0,16},{8,24},{16,0},{24,8},{1,17},{9,25},{17,1},{25,9},{2,18},{10... | collective-permute-start | bytes 20 | tf_op jit(solution)/shard_map/ppermute | solution.py:28
  344.5 9.5 %collective-permute-start.82 = (f32[1,1]{1,0:T(1,128)}, f32[1,1]{1,0:T(1,128)}, u32[]{:S(2)}, u32[]{:S(2)}) collective-permute-start(f32[1,1]{1,0:T(1,128)} %add.608), channel_id=1, source_target_pairs={{0,6},{1,7},{2,4},{3,5},{4,2},{5,3},{6,0},{7,1},{8,14},{9,15},{10,... | collective-permute-start | bytes 20 | tf_op jit(solution)/shard_map/ppermute | solution.py:28
  347.7 6.4 %collective-permute-start.81 = (f32[1,1]{1,0:T(1,128)}, f32[1,1]{1,0:T(1,128)}, u32[]{:S(2)}, u32[]{:S(2)}) collective-permute-start(f32[1,1]{1,0:T(1,128)} %add.608), channel_id=1, source_target_pairs={{0,4},{1,5},{2,6},{3,7},{4,0},{5,1},{6,2},{7,3},{8,12},{9,13},{10,... | collective-permute-start | bytes 20 | tf_op jit(solution)/shard_map/ppermute | solution.py:28
  (71 other events, 545.2 us)
Sparse Core Ops, SparseCore 0:
  11.6 70.0 all-gather.1
where the time goes:
time: 373 us; the launch traced here: 371 us
  starting transfers between devices  111 us (30%)
  Pallas kernels  109 us (29%)
  waiting for transfers between devices  87.3 us (23%)
  other arithmetic  23.6 us (6%)
  between operations  22 us (6%)
  local copies, waits for them, and re-layouts  18.7 us (5%)
    pallas_call x14, Pallas kernels, call(): pl.pallas_call(kernel, grid=grid, in_specs=[spec for _, spec in ins], out...  107 us
    ppermute x77, starting transfers between devices, swap(): lax.ppermute(x, axis, [(i, i ^ mask) for i in range(lax.axis_size(axis))])  97.5 us
    ppermute x77, waiting for transfers between devices, swap(): lax.ppermute(x, axis, [(i, i ^ mask) for i in range(lax.axis_size(axis))])  87.3 us
    unnamed x70, local copies, waits for them, and re-layouts  12.4 us
    ppermute x3, starting transfers between devices, neighbours(): above = lax.ppermute(x, 'rows', [(i, i + 1) for i in range(count - 1)])  9.42 us
  transfers between devices with their start and end apart: 84, of which 48 were waited for; matrix products, arithmetic and copies ran while one was open for 5% of the time, Pallas kernels for 13%

commit v1 on v0

--- a/solution.py
+++ b/solution.py
@@ -146,22 +146,36 @@
     return chip * 2 + ((mine & 1) ^ core_mask)
 
 
-def gather_pieces(shard, join):
-    line = lax.axis_size("rows") // 2
-    block = shard[None]
-    for bit, size in row_groups():
-        block = join([block] + [swap(block, "rows", m << bit) for m in range(1, size)])
-    half = line // 2
-    from_x = swap(block, "batch", 1)
-    from_y = swap(block, "batch", 2)
-    far_low = swap(from_x[:half], "batch", 2)
-    far_high = swap(from_y[half:], "batch", 1)
-    pieces = []
-    for piece, mask, first in ((block, 0, 0), (from_x, 1, 0), (from_y, 2, 0), (far_low, 3, 0), (far_high, 3, half)):
-        place = first + jnp.arange(piece.shape[0], dtype=jnp.int32)
-        for array, core in ((piece, 0), (swap(piece, "rows", 1), 1)):
-            pieces.append((array, owners(mask, core, place)))
-    return pieces
+class Gather:
+    def along_line(self, shard):
+        blocks = [shard[None]]
+        for bit, size in row_groups():
+            block = jnp.concatenate(blocks, axis=0)
+            blocks = [block] + [swap(block, "rows", m << bit) for m in range(1, size)]
+        return blocks
+
+    def near(self, block):
+        self.block = block
+        return swap(block, "batch", 1), swap(block, "batch", 2)
+
+    def far(self, from_x, from_y):
+        self.from_x, self.from_y = from_x, from_y
+        half = from_x.shape[0] // 2
+        return swap(from_x[:half], "batch", 2), swap(from_y[half:], "batch", 1)
+
+    def pieces(self, far_low, far_high):
+        got = []
+        half = far_low.shape[0]
+        parts = ((self.block, 0, 0), (self.from_x, 1, 0), (self.from_y, 2, 0), (far_low, 3, 0), (far_high, 3, half))
+        for piece, mask, first in parts:
+            place = first + jnp.arange(piece.shape[0], dtype=jnp.int32)
+            for array, core in ((piece, 0), (swap(piece, "rows", 1), 1)):
+                got.append((array, owners(mask, core, place)))
+        return got
+
+
+def in_order(*values):
+    return lax.optimization_barrier(values)
 
 
 class Assembly:
@@ -200,7 +214,7 @@
         shapes = [(r, width) for r in rows]
         if self.direct:
             shapes = [(self.chips, sum(self.sizes), width)] * 2
-        self.outs = [out(shape, BF16, shape, lambda *_, n=len(shape): (0,) * n) for shape in shapes]
+        self.outs = [constant(shape, BF16) for shape in shapes]
 
     def emit(self, weight, product, base, rows, place_ref, core_ref, outs):
         if not self.direct:
@@ -217,10 +231,6 @@
                 ref[to, low : low + size, :] = product[pl.ds(start, size), :].astype(BF16)
 
 
-def in_order(*values):
-    return lax.optimization_barrier(values)
-
-
 class Sums:
     def __init__(self, spread, outs):
         self.direct = spread.direct
@@ -257,13 +267,18 @@
         return jnp.concatenate([low, high], axis=0)
 
     def take_line(self, own):
+        self.parts = []
         for bit, size in reversed(row_groups()):
+            if self.parts:
+                own = sum(part.astype(F32) for part in self.parts)
             own = own.reshape((size, -1) + own.shape[1:])
-            total = own[0]
-            for m in range(1, size):
-                total = total + swap(own[m].astype(BF16), "rows", m << bit).astype(F32)
-            own = total
-        self.total = own.reshape(own.shape[-2:])
+            self.parts = [own[0]] + [swap(own[m].astype(BF16), "rows", m << bit) for m in range(1, size)]
+
+    def finish(self):
+        if self.direct:
+            own = sum(part.astype(F32) for part in self.parts)
+            self.total = own.reshape(own.shape[-2:])
+        return self.total
 
 
 CHUNK = 16
@@ -350,6 +365,11 @@
     return (array, pl.BlockSpec(memory_space=pl.ANY))
 
 
+def constant(shape, dtype):
+    spec = pl.BlockSpec(shape, lambda *_: (0,) * len(shape), pipeline_mode=pl.Buffered(1))
+    return (jax.ShapeDtypeStruct(shape, dtype), spec)
+
+
 def out(shape, dtype, spec_shape, index):
     return (jax.ShapeDtypeStruct(shape, dtype), pl.BlockSpec(spec_shape, index))
 
@@ -468,9 +488,9 @@
 
 
 def second_kernel(
-    inv_ref, sums_ref, param_ref, own_ref, up_ref, down_ref, mask_ref, w_ref, *refs
+    assembly, inv_ref, sums_ref, param_ref, own_ref, up_ref, down_ref, mask_ref, *refs
 ):
-    h_ref, wide_ref, low_ref, out_ref, cat_ref, part_ref = refs[-6:]
+    h_ref, wide_ref, low_ref, out_ref, cat_ref, part_ref, w_ref = refs[-7:]
     micro = pl.program_id(0)
     width = own_ref.shape[-1]
     pixels = own_ref.shape[1]
@@ -478,6 +498,7 @@
 
     @pl.when(micro == 0)
     def _():
+        assembly.run(refs[: assembly.count], w_ref)
         clear_pads(part_ref)
 
     mean, rstd, scale = norm_stats(sums_ref, inv_ref[micro], param_ref[0:1, :])
@@ -540,7 +561,7 @@
 
 
 def peak_kernel(
-    inv_ref, sums_ref, param_ref, a_ref, x_ref, up_ref, mask_ref, after_ref, late_ref, block_ref, du_ref, out_ref
+    inv_ref, sums_ref, param_ref, a_ref, x_ref, up_ref, mask_ref, block_ref, du_ref, out_ref
 ):
     width = a_ref.shape[-1]
     mean, rstd, scale = norm_stats(sums_ref, inv_ref[pl.program_id(0)], param_ref[0:1, :])
@@ -650,14 +671,16 @@
 
 
 def back_second_kernel(
-    inv_ref, stats1_ref, param1_ref, cat_ref, a1_ref, mask_ref, w_ref, after_ref, wide_ref, out_ref, part_ref
+    assembly, inv_ref, stats1_ref, param1_ref, cat_ref, a1_ref, mask_ref, *refs
 ):
+    wide_ref, out_ref, part_ref, w_ref = refs[-4:]
     inv = inv_ref[pl.program_id(0)]
     pixels, width = a1_ref.shape[1:]
     columns = part_ref.shape[2] - 2 * PAD
 
     @pl.when(pl.program_id(0) == 0)
     def _():
+        assembly.run(refs[: assembly.count], w_ref)
         clear_pads(part_ref)
 
     for tx in range(3):
@@ -692,7 +715,7 @@
     def _():
         for tx in range(3):
             rows = pl.ds(pl.multiple_of((3 * step + tx) * width, width), width)
-            product[rows, :] = dot(h_ref[0], d_ref[:, tx * width : (tx + 1) * width], TN)
+            product[rows, :] = dot(h_ref[0], d_ref[:, tx * width : (tx + 1) * width], TN).astype(BF16)
 
     @pl.when(step == 2)
     def _():
@@ -701,7 +724,7 @@
     @pl.when(step >= 3)
     def _():
         rows = d3_ref.shape[1]
-        product[0:rows, :] = dot(d3_ref[...], h2_ref[...], TN)
+        product[0:rows, :] = dot(d3_ref[...], h2_ref[...], TN).astype(BF16)
         spread.emit(1, product, pl.multiple_of((step - 3) * rows, rows), rows, place_ref, core_ref, outs)
 
 
@@ -775,7 +798,6 @@
     masks = jnp.broadcast_to(masks.reshape(3, micros, pixels, 1), (3, micros, pixels, 128))
     inverse = 1.0 / jnp.sum(row_counts * col_counts, axis=1).astype(F32)
 
-    w_mid = lax.all_gather(weight_mid.astype(BF16), ("batch", "rows"), axis=0, tiled=True)
     grams = []
     for micro in range(micros):
         grams.append(call(
@@ -785,7 +807,7 @@
                 (masks, block((1, 1, columns, 128), functools.partial(lambda m, r: (1, m, r, 0), micro))),
             ],
             [out((8, 128), F32, (8, 128), lambda r: (0, 0))],
-            flops=6 * total_pixels * chan, nbytes=3 * total_pixels * chan,
+            flops=6 * total_pixels * chan, nbytes=3 * total_pixels * chan, vmem=10,
         ))
     x = features.reshape(micros, pixels, chan)
     params = [norm_params[:, :inner], norm_params[:, inner : 2 * inner], norm_params[:, 2 * inner :]]
@@ -805,50 +827,75 @@
     big = total_pixels * chan
     small = total_pixels * inner
     part_rows = weight_in.shape[0]
+    mid_rows = weight_mid.shape[0]
+    low_mid = weight_mid.astype(BF16)
     both = jnp.concatenate([weight_in.astype(BF16), weight_out.T.astype(BF16)], axis=0)
-    if part_rows % 16:
+    direct = part_rows % 16 == 0 and mid_rows % 16 == 0
+    zero = jnp.zeros(1, jnp.int32)
+    if direct:
+        gather_both, gather_mid = Gather(), Gather()
+        line_both = gather_both.along_line(both)
+        near_both, low_mid = in_order(joined(line_both, *grams), low_mid)
+        from_both = gather_both.near(near_both)
+        line_mid = gather_mid.along_line(low_mid)
+        far_both = gather_both.far(*from_both)
+        pieces = gather_both.pieces(*far_both)
+        line_mid = in_order(*line_mid, *far_both)[: len(line_mid)]
+        near_mid, *arrays = in_order(joined(line_mid), *[array for array, _ in pieces])
+        from_mid = gather_mid.near(near_mid)
+        pieces = [(array, owner) for array, (_, owner) in zip(arrays, pieces)]
+        ins_in, ins_out = [Assembly(pieces, k * part_rows, part_rows) for k in range(2)]
+    else:
         full = gather_shards(both).reshape(-1, 2, part_rows, inner)
-        zero = jnp.zeros(1, jnp.int32)
         ins_in, ins_out = [Assembly([(full[:, k].reshape(1, -1, inner), zero)], 0, chan) for k in range(2)]
-    else:
-        pieces = gather_pieces(both, lambda got: joined(got, grams[0]))
-        ins_in, ins_out = [Assembly(pieces, k * part_rows, part_rows) for k in range(2)]
-    whole_weight = out((chan, inner), BF16, (chan, inner), lambda *_: (0, 0))
+        ins_mid = Assembly([(gather_shards(low_mid).reshape(1, -1, inner), zero)], 0, 9 * inner)
+    whole_weight = constant((chan, inner), BF16)
     a_one, a_one_low, part, w_in = call(
         functools.partial(first_kernel, ins_in), (micros,),
         [per_micro(x), own_mask, per_micro(jnp.stack(grams)), *ins_in.ins],
         [out_micro(inner, F32), out_micro(inner, BF16), out_micro(inner, F32, 4), whole_weight],
-        flops=2 * big * inner, nbytes=2 * big + 8 * small,
+        flops=2 * big * inner, nbytes=2 * big + 8 * small, vmem=18,
     )
     a_one_up, a_one_down = neighbours(a_one_low)
-    stats_one = all_sum(part)
-    w_out = call(
-        functools.partial(assemble_kernel, ins_out), (1,), ins_out.ins, [whole_weight], nbytes=8 * chan * inner
-    )
+    core_one = group_sum(part, "rows", 0, 2)
+    if direct:
+        core_one, *from_mid = in_order(core_one, *from_mid)
+    chip_one = group_sum(core_one, "batch", 0, lax.axis_size("batch"))
+    chip_one, a_one_up, a_one_down = in_order(chip_one, a_one_up, a_one_down)
+    if direct:
+        chip_one, *from_mid = in_order(chip_one, *from_mid)
+        far_mid = gather_mid.far(*from_mid)
+    stats_one = line_sums(chip_one)
     upstream = call(
         upstream_kernel, (micros, row_span),
         [whole(stats_one), task_rows, row_mask],
         [out((micros, pixels, chan), F32, (1, columns, chan), lambda m, r: (m, r, 0))],
         [pltpu.VMEM((3, 8, 128), F32)],
-        flops=8 * big, nbytes=10 * big,
-    )
+        flops=8 * big, nbytes=10 * big, vmem=10,
+    )
+    if direct:
+        upstream, *far_mid = in_order(upstream, *far_mid)
+        ins_mid = Assembly(gather_mid.pieces(*far_mid), 0, mid_rows)
     padded = (3, row_span, columns + 2 * PAD, inner)
-    taps = [pltpu.VMEM((pixels, 3 * inner), BF16), pltpu.VMEM(padded, F32)]
+    held = pltpu.VMEM((9 * inner, inner), BF16)
+    taps = [pltpu.VMEM((pixels, 3 * inner), BF16), pltpu.VMEM(padded, F32), held]
     h_one, a_two, a_two_low, part = call(
-        second_kernel, (micros,),
+        functools.partial(second_kernel, ins_mid), (micros,),
         [
             smem(inverse), per_micro(stats_one), whole(params[0]), per_micro(a_one),
             per_micro(a_one_up), per_micro(a_one_down), all_masks,
-            whole(w_mid), anywhere(upstream),
+            *ins_mid.ins, anywhere(upstream),
         ],
         [
             out((3, micros, pixels, inner), BF16, (3, 1, pixels, inner), lambda m: (0, m, 0, 0)),
             out_micro(inner, F32), out_micro(inner, BF16), out_micro(inner, F32, 2),
         ],
         taps,
-        flops=18 * small * inner, nbytes=20 * small + 18 * inner * inner,
-    )
-    a_two_up, a_two_down = neighbours(a_two_low)
+        flops=18 * small * inner, nbytes=20 * small + 18 * inner * inner, vmem=32,
+    )
+    w_out = call(
+        functools.partial(assemble_kernel, ins_out), (1,), ins_out.ins, [whole_weight], nbytes=8 * chan * inner, vmem=16
+    )
     stats_two = all_sum(part)
     h_two, a_three, part = call(
         third_kernel, (micros,),
@@ -857,9 +904,11 @@
             whole(w_out),
         ],
         [out_micro(inner, BF16), out_micro(chan, F32), out_micro(chan, F32, 2)],
-        flops=2 * big * inner, nbytes=4 * big + 8 * small,
+        flops=2 * big * inner, nbytes=4 * big + 8 * small, vmem=20,
     )
     stats_three = all_sum(part)
+    stats_three, a_two_low = in_order(stats_three, a_two_low)
+    a_two_up, a_two_down = neighbours(a_two_low)
     tile = 512
 
     def tiled(array):
@@ -872,11 +921,12 @@
         peak_kernel, (micros, chan // tile),
         [
             smem(inverse), tiled(stats_three), (params[2], block((2, tile), lambda m, c: (0, c))),
-            tiled(a_three), tiled(x), tiled(upstream), own_mask, anywhere(a_two_up), anywhere(a_two_down),
+            tiled(a_three), tiled(x), tiled(upstream), own_mask,
         ],
         [out_tiled(BF16), out_tiled(F32), out_tiled(F32, 2)],
-        flops=40 * big, nbytes=16 * big,
-    )
+        flops=40 * big, nbytes=16 * big, vmem=14,
+    )
+    part, a_two_up, a_two_down = in_order(part, a_two_up, a_two_down)
     grads_three = all_sum(part)
     d_three, dz_two, dz_two_low, part = call(
         back_third_kernel, (micros,),
@@ -886,7 +936,7 @@
             per_micro(a_two), own_mask, whole(w_out),
         ],
         [out_micro(chan, BF16), out_micro(inner, F32), out_micro(inner, BF16), out_micro(inner, F32, 2)],
-        flops=2 * big * inner, nbytes=10 * big,
+        flops=2 * big * inner, nbytes=10 * big, vmem=26,
     )
     dz_two_up, dz_two_down = neighbours(dz_two_low)
     grads_two = all_sum(part)
@@ -899,7 +949,7 @@
         ],
         [out_micro(3 * inner, BF16), out_micro(3 * inner, BF16)],
         [pltpu.VMEM(padded[1:], F32)],
-        flops=60 * small, nbytes=28 * small,
+        flops=60 * small, nbytes=28 * small, vmem=20,
     )
     spread = Spread(inner, 9 * inner, chan)
     grads = call(
@@ -916,19 +966,19 @@
             ),
             whole(h_two.reshape(total_pixels, inner)), *spread.ins,
         ],
-        spread.outs, [pltpu.VMEM((9 * inner, inner), F32)],
-        flops=18 * small * inner + 2 * big * inner, nbytes=12 * small + 18 * inner * inner,
+        spread.outs, [pltpu.VMEM((9 * inner, inner), BF16)],
+        flops=18 * small * inner + 2 * big * inner, nbytes=12 * small + 18 * inner * inner, vmem=30,
     )
     sums = Sums(spread, grads)
     dz_one, part = call(
-        back_second_kernel, (micros,),
+        functools.partial(back_second_kernel, ins_mid), (micros,),
         [
             smem(inverse), per_micro(stats_one), whole(params[0]), per_micro(d_two_cat),
-            per_micro(a_one), own_mask, whole(w_mid), anywhere(grads[0]),
+            per_micro(a_one), own_mask, *ins_mid.ins, anywhere(grads[0]),
         ],
         [out_micro(inner, F32), out_micro(inner, F32, 2)],
-        [pltpu.VMEM(padded, F32)],
-        flops=18 * small * inner, nbytes=30 * small + 18 * inner * inner,
+        [pltpu.VMEM(padded, F32), held],
+        flops=18 * small * inner, nbytes=30 * small + 18 * inner * inner, vmem=26,
     )
     chip_one = chip_sums(part)
     if sums.direct:
@@ -946,7 +996,7 @@
         ],
         [out((micros, pixels, inner), BF16, (micros, pixels, inner), lambda c: (0, 0, 0)), *spread_in.outs],
         [pltpu.VMEM((tile, inner), F32)],
-        flops=2 * big * inner, nbytes=4 * big,
+        flops=2 * big * inner, nbytes=4 * big, vmem=20,
     )
     if sums.direct:
         d_one, *rest = in_order(d_one, *grad_in, *sums.far)
@@ -964,24 +1014,24 @@
             (d_resid.reshape(total_pixels, chan), block((strip, chan), lambda s: (s, 0))),
         ],
         [out((total_pixels, chan), BF16, (strip, chan), lambda s: (s, 0))],
-        flops=2 * big * inner, nbytes=8 * big,
+        flops=2 * big * inner, nbytes=8 * big, vmem=16,
     )
     if sums.direct:
-        input_grad, *rest = in_order(input_grad, *sums.near, *sums_in.send_far())
-        sums.near = rest[:2]
-        sums_in.take_far(rest[2:])
-        sums.take_line(sums.send_line())
+        input_grad, *sums.near = in_order(input_grad, *sums.near)
+        line, *sends = in_order(sums.send_line(), *sums_in.send_far())
+        sums.take_line(line)
+        sums_in.take_far(sends)
+        sums.parts[1], *sums_in.far = in_order(sums.parts[1], *sums_in.far)
         sums_in.take_near(sums_in.send_near())
         sums_in.take_line(sums_in.send_line())
-    grad_in, grad_both = sums_in.total, sums.total
+    grad_in, grad_both = sums_in.finish(), sums.finish()
     grad_mid, grad_out = grad_both[: weight_mid.shape[0]], grad_both[weight_mid.shape[0] :]
 
     norm_total = jnp.concatenate([grads_one[:, :2], grads_two, grads_three], axis=2)
     norm_total = jnp.sum(norm_total, axis=0)[::-1]
-    local_squares = (
-        jnp.sum(grad_in * grad_in) + jnp.sum(grad_both * grad_both)
-    )
-    total = all_sum(local_squares.reshape(1, 1)) + jnp.sum(norm_total * norm_total)
+    squares = jnp.sum(grad_in * grad_in, axis=0) + jnp.sum(grad_both * grad_both, axis=0)
+    squares = all_sum(squares.reshape(-1, 128))
+    total = jnp.sum(squares).reshape(1, 1) + jnp.sum(norm_total * norm_total)
     grad_norm = jnp.sqrt(total)
     scale = CLIP / jnp.maximum(grad_norm, CLIP)
     new_in = adamw(weight_in, first_in, second_in, grad_in * scale, RATE, DECAY)

time: 373 us -> 324 us (0.87)
  Pallas kernels: 109 us -> 74.9 us
  between operations: 22 us -> 4.07 us
  waiting for transfers between devices: 87.3 us -> 99 us
  local copies, waits for them, and re-layouts: 18.7 us -> 27.9 us
  other arithmetic: 23.6 us -> 14.5 us
  starting transfers between devices: 111 us -> 103 us
    pallas_call x14, Pallas kernels: 107 us -> 71 us  [call(): pl.pallas_call(kernel, grid=grid, in_specs=[spec for _, spec in ins], out...]
    ppermute x77 -> x89, waiting for transfers between devices: 87.3 us -> 99 us  [swap(): lax.ppermute(x, axis, [(i, i ^ mask) for i in range(lax.axis_size(axis))])]
    unnamed x70 -> x82, local copies, waits for them, and re-layouts: 12.4 us -> 22.9 us
    ppermute x3, starting transfers between devices: 9.42 us -> 4.57 us  [neighbours(): above = lax.ppermute(x, 'rows', [(i, i + 1) for i in range(count - 1)])]
    sub x4, other arithmetic: 7.14 us -> 3.39 us  [adamw(): weight - rate * (first_hat / (jnp.sqrt(second_hat) + ADAM_EPS) + decay *...]
    ppermute x77 -> x89, starting transfers between devices: 97.5 us -> 94.8 us  [swap(): lax.ppermute(x, axis, [(i, i ^ mask) for i in range(lax.axis_size(axis))])]
  transfers between devices with their start and end apart: 84 -> 95, of which waited for: 48 -> 57; matrix products, arithmetic and copies ran while one was open for 5% -> 4% of each run, Pallas kernels for 13% -> 12%
where the time goes in v1:
time: 324 us
  starting transfers between devices  103 us (32%)
  waiting for transfers between devices  99 us (31%)
  Pallas kernels  74.9 us (23%)
  local copies, waits for them, and re-layouts  27.9 us (9%)
  other arithmetic  14.5 us (4%)
  between operations  4.07 us (1%)
    ppermute x89, waiting for transfers between devices, swap(): lax.ppermute(x, axis, [(i, i ^ mask) for i in range(lax.axis_size(axis))])  99 us
    ppermute x89, starting transfers between devices, swap(): lax.ppermute(x, axis, [(i, i ^ mask) for i in range(lax.axis_size(axis))])  94.8 us
    pallas_call x14, Pallas kernels, call(): pl.pallas_call(kernel, grid=grid, in_specs=[spec for _, spec in ins], out...  71 us
    unnamed x82, local copies, waits for them, and re-layouts  22.9 us
  transfers between devices with their start and end apart: 95, of which 57 were waited for; matrix products, arithmetic and copies ran while one was open for 4% of the time, Pallas kernels for 12%

profile of v1, /device:TPU:0, one launch (start us, length us, event | category | flops | bytes accessed | tf_op | source)
XLA Modules:
  0.0 323.8 jit_solution(12111893771618134569)
XLA Ops:
  2.5 3.1 collective-permute-start
  5.6 2.6 collective-permute-start.1
  11.7 3.7 %copy-done = bf16[3,2,1,4,96,2048]{5,4,3,2,1,0:T(8,128)(2,1)S(1)} copy-done((bf16[3,2,1,4,96,2048]{5,4,3,2,1,0:T(8,128)(2,1)S(1)}, bf16[3,2,1,4,96,2048]{5,4,3,2,1,0:T(8,128)(2,1)}, u32[]{:S(2)}) %copy-start) | copy-done | bytes 9437208
  15.4 2.1 shard_map.272.refs_5_
  18.1 2.1 shard_map.271.refs_4_
  22.2 1.9 shard_map.273.refs_1_
  28.6 3.5 %collective-permute-start.4 = (bf16[1,144,512]{2,1,0:T(8,128)(2,1)}, bf16[1,144,512]{2,1,0:T(8,128)(2,1)}, u32[]{:S(2)}, u32[]{:S(2)}) collective-permute-start(bf16[1,144,512]{2,1,0:T(8,128)(2,1)} %bitcast.5.refs_0_), channel_id=1, source_target_pairs={{0,4},{1,5},{2,6},{3,7},{4,0},{5,1},{6,2},{7,3},{8,12},{9,13},{10,... | collective-permute-start | bytes 442376 | tf_op jit(solution)/shard_map/ppermute | solution.py:28
  32.8 4.7 %collective-permute-done.6.refs_3_ = bf16[4,128,512]{2,1,0:T(8,128)(2,1)S(1)} collective-permute-done((bf16[4,128,512]{2,1,0:T(8,128)(2,1)}, bf16[4,128,512]{2,1,0:T(8,128)(2,1)S(1)}, u32[]{:S(2)}, u32[]{:S(2)}) %collective-permute-start.6) | collective-permute-done | bytes 524320 | tf_op jit(solution)/shard_map/ppermute | solution.py:28
  45.1 2.1 collective-permute-done.9.refs_9_
  49.7 2.0 shard_map.274.refs_1_
  55.6 4.1 %shard_map.275 = (f32[2,384,512]{2,1,0:T(8,128)S(1)}, bf16[2,384,512]{2,1,0:T(8,128)(2,1)S(1)}, f32[2,4,512]{2,1,0:T(4,128)S(1)}, bf16[2048,512]{1,0:T(8,128)(2,1)S(1)}) custom-call(bf16[2,384,2048]{2,1,0:T(8,128)(2,1)S(1)} %bitcast.116, f32[3,2,384,128]{3,2,1,0:T(8,128)S(1)} %broadcast_in_dim.6.mask_ref, f32[2,8,128]{2,1,0:T(8,128)S(1)} %pad_maximum_fusion.1.gram_ref, ...), custom_call_target="tpu_custom_call" | custom-call | flops 1610612736 | bytes 6291456 | tf_op jit(solution)/shard_map/pallas_call | solution.py:332
  59.8 1.9 collective-permute-start.21
  76.5 1.9 collective-permute-start.25
  83.4 3.7 %copy-done.1 = bf16[3,2,1,4,96,2048]{5,4,3,2,1,0:T(8,128)(2,1)S(1)} copy-done((bf16[3,2,1,4,96,2048]{5,4,3,2,1,0:T(8,128)(2,1)S(1)}, bf16[3,2,1,4,96,2048]{5,4,3,2,1,0:T(8,128)(2,1)}, u32[]{:S(2)}) %copy-start.1) | copy-done | bytes 9437208
  87.1 2.9 shard_map.276.refs_11_.up_ref
  92.3 9.3 %shard_map.277 = (bf16[3,2,384,512]{3,2,1,0:T(8,128)(2,1)S(1)}, f32[2,384,512]{2,1,0:T(8,128)S(1)}, bf16[2,384,512]{2,1,0:T(8,128)(2,1)S(1)}, f32[2,2,512]{2,1,0:T(2,128)S(1)}) custom-call(f32[2]{0:T(128)S(1)} %convert_divide_fusion.inv_ref, f32[2,4,512]{2,1,0:T(4,128)S(1)} %bitcast.131, f32[2,512]{1,0:T(2,128)S(1)} %get-tuple-element.254.param_ref.param1_ref, ...), custom_call_target="tpu_custom_call" | custom-call | flops 3623878656 | bytes 12582912 | tf_op jit(solution)/shard_map/pallas_call | solution.py:332
  106.6 2.4 collective-permute-done.36
  109.0 2.2 collective-permute-start.38
  114.2 2.5 collective-permute-done.39
  116.7 6.3 %shard_map.279 = (bf16[2,384,512]{2,1,0:T(8,128)(2,1)S(1)}, f32[2,384,2048]{2,1,0:T(8,128)S(1)}, f32[2,2,2048]{2,1,0:T(2,128)S(1)}) custom-call(f32[2]{0:T(128)S(1)} %convert_divide_fusion.inv_ref, f32[2,2,512]{2,1,0:T(2,128)S(1)} %add_add_fusion.10.sums_ref.stats2_ref, f32[2,512]{1,0:T(2,128)S(1)} %get-tuple-element.253.param_ref.param2_ref, ...), custom_call_target="tpu_custom_call" | custom-call | flops 1610612736 | bytes 9437184 | tf_op jit(solution)/shard_map/pallas_call | solution.py:332
  123.0 2.7 copy-done.5
  138.9 1.9 collective-permute-done.46
  143.5 2.8 copy-done.6
  146.3 10.3 %shard_map.280 = (bf16[2,384,2048]{2,1,0:T(8,128)(2,1)}, f32[2,384,2048]{2,1,0:T(8,128)S(1)}, f32[2,2,2048]{2,1,0:T(2,128)S(1)}) custom-call(f32[2]{0:T(128)S(1)} %convert_divide_fusion.inv_ref, f32[2,2,2048]{2,1,0:T(2,128)S(1)} %add_add_fusion.2.sums_ref.stats3_ref, f32[2,2048]{1,0:T(2,128)S(1)} %slice.173.param_ref.param3_ref, ...), custom_call_target="tpu_custom_call" | custom-call | flops 62914560 | bytes 25165824 | tf_op jit(solution)/shard_map/pallas_call | solution.py:332
  156.6 1.9 collective-permute-start.49
  160.4 2.0 collective-permute-start.52
  163.4 2.0 collective-permute-done.52
  166.4 2.6 collective-permute-start.54
  171.3 3.5 %collective-permute-done.55 = f32[2,2,2048]{2,1,0:T(2,128)S(1)} collective-permute-done((f32[2,2,2048]{2,1,0:T(2,128)S(1)}, f32[2,2,2048]{2,1,0:T(2,128)S(1)}, u32[]{:S(2)}, u32[]{:S(2)}) %collective-permute-start.55) | collective-permute-done | bytes 32800 | tf_op jit(solution)/shard_map/ppermute | solution.py:28
  175.1 2.8 copy-done.7
  177.9 5.4 %shard_map.281 = (bf16[2,384,2048]{2,1,0:T(8,128)(2,1)S(1)}, f32[2,384,512]{2,1,0:T(8,128)S(1)}, bf16[2,384,512]{2,1,0:T(8,128)(2,1)S(1)}, f32[2,2,512]{2,1,0:T(2,128)S(1)}) custom-call(f32[2]{0:T(128)S(1)} %convert_divide_fusion.inv_ref, f32[2,2,2048]{2,1,0:T(2,128)S(1)} %add_add_fusion.2.sums_ref.stats3_ref, f32[2,2,2048]{2,1,0:T(2,128)S(1)} %add_add_fusion.grads3_ref, ...), custom_call_target="tpu_custom_call" | custom-call | flops 1610612736 | bytes 15728640 | tf_op jit(solution)/shard_map/pallas_call | solution.py:332
  196.4 2.4 collective-permute-start.61
  201.4 2.9 collective-permute-done.62
  204.3 2.6 shard_map.282
  207.1 9.9 %shard_map.283 = (bf16[16,208,512]{2,1,0:T(8,128)(2,1)}, bf16[16,208,512]{2,1,0:T(8,128)(2,1)S(1)}) custom-call(bf16[3,768,512]{2,1,0:T(8,128)(2,1)S(1)} %bitcast.137, bf16[768,1536]{1,0:T(8,128)(2,1)S(1)} %bitcast.138, bf16[768,2048]{1,0:T(8,128)(2,1)S(1)} %bitcast.136, bf16[768,512]{1,0:T(8,128)(2,1)S(1)} %bitcast.139, s32[16]{0:T(128)S(1)} %fusion.22.place_ref, ...), custom_call_target="tpu_custom_call" | custom-call | flops 5234491392 | bytes 9437184 | tf_op jit(solution)/shard_map/pallas_call | solution.py:332
  216.9 6.0 %shard_map.284 = (f32[2,384,512]{2,1,0:T(8,128)S(1)}, f32[2,2,512]{2,1,0:T(2,128)S(1)}) custom-call(f32[2]{0:T(128)S(1)} %convert_divide_fusion.inv_ref, f32[2,4,512]{2,1,0:T(4,128)S(1)} %bitcast.132, f32[2,512]{1,0:T(2,128)S(1)} %get-tuple-element.254.param_ref.param1_ref, bf16[2,384,1536]{2,1,0:T(8,128)(2,1)S(1)} %get-tuple-element.144.cat_ref, ...), custom_call_target="tpu_custom_call" | custom-call | flops 3623878656 | bytes 16515072 | tf_op jit(solution)/shard_map/pallas_call | solution.py:332
  225.3 2.0 collective-permute-start.68
  239.5 4.0 %shard_map.285 = (bf16[2,384,512]{2,1,0:T(8,128)(2,1)S(1)}, bf16[16,64,512]{2,1,0:T(8,128)(2,1)S(1)}, bf16[16,64,512]{2,1,0:T(8,128)(2,1)S(1)}) custom-call(f32[2]{0:T(128)S(1)} %convert_divide_fusion.inv_ref, f32[2,4,512]{2,1,0:T(4,128)S(1)} %bitcast.133, f32[2,2,512]{2,1,0:T(2,128)S(1)} %add_add_fusion.6.grads_ref, ...), custom_call_target="tpu_custom_call" | custom-call | flops 1610612736 | bytes 6291456 | tf_op jit(solution)/shard_map/pallas_call | solution.py:332
  243.4 7.9 %collective-permute-done.73 = bf16[2,2,208,512]{3,2,1,0:T(8,128)(2,1)S(1)} collective-permute-done((bf16[2,2,208,512]{3,2,1,0:T(8,128)(2,1)S(1)}, bf16[2,2,208,512]{3,2,1,0:T(8,128)(2,1)S(1)}, u32[]{:S(2)}, u32[]{:S(2)}) %collective-permute-start.73) | collective-permute-done | bytes 852000 | tf_op jit(solution)/shard_map/ppermute | solution.py:28
  254.3 4.3 %shard_map.286 = bf16[768,2048]{1,0:T(8,128)(2,1)} custom-call(bf16[768,512]{1,0:T(8,128)(2,1)S(1)} %bitcast.129, bf16[2048,512]{1,0:T(8,128)(2,1)S(1)} %get-tuple-element.163.w_ref, f32[768,2048]{1,0:T(8,128)S(1)} %bitcast.121), custom_call_target="tpu_custom_call" | custom-call | flops 1610612736 | bytes 12582912 | tf_op jit(solution)/shard_map/pallas_call | solution.py:332
  258.6 5.5 %collective-permute-done.75 = bf16[2,208,512]{2,1,0:T(8,128)(2,1)S(1)} collective-permute-done((bf16[2,208,512]{2,1,0:T(8,128)(2,1)S(1)}, bf16[2,208,512]{2,1,0:T(8,128)(2,1)S(1)}, u32[]{:S(2)}, u32[]{:S(2)}) %collective-permute-start.75) | collective-permute-done | bytes 426016 | tf_op jit(solution)/shard_map/ppermute | solution.py:28
  268.0 6.0 %collective-permute-done.78 = bf16[1,208,512]{2,1,0:T(8,128)(2,1)S(1)} collective-permute-done((bf16[1,208,512]{2,1,0:T(8,128)(2,1)S(1)}, bf16[1,208,512]{2,1,0:T(8,128)(2,1)S(1)}, u32[]{:S(2)}, u32[]{:S(2)}) %collective-permute-start.78) | collective-permute-done | bytes 213024 | tf_op jit(solution)/shard_map/ppermute | solution.py:28
  275.4 4.1 %collective-permute-done.81 = bf16[2,64,512]{2,1,0:T(8,128)(2,1)S(1)} collective-permute-done((bf16[2,64,512]{2,1,0:T(8,128)(2,1)S(1)}, bf16[2,64,512]{2,1,0:T(8,128)(2,1)S(1)}, u32[]{:S(2)}, u32[]{:S(2)}) %collective-permute-start.81) | collective-permute-done | bytes 131104 | tf_op jit(solution)/shard_map/ppermute | solution.py:28
  281.1 2.0 collective-permute-start.87
  283.2 2.4 collective-permute-start.82
  285.7 2.1 collective-permute-start.85
  287.9 3.2 collective-permute-done.87
  291.1 11.4 %collective-permute-done.86 = bf16[1,208,512]{2,1,0:T(8,128)(2,1)S(1)} collective-permute-done((bf16[1,208,512]{2,1,0:T(8,128)(2,1)S(1)}, bf16[1,208,512]{2,1,0:T(8,128)(2,1)S(1)}, u32[]{:S(2)}, u32[]{:S(2)}) %collective-permute-start.86) | collective-permute-done | bytes 213024 | tf_op jit(solution)/shard_map/ppermute | solution.py:28
  (318 shorter events, 138.2 us)
Async XLA Ops:
  2.5 18.4 %collective-permute-start = (bf16[1,128,512]{2,1,0:T(8,128)(2,1)S(1)}, bf16[1,128,512]{2,1,0:T(8,128)(2,1)S(1)}, u32[]{:S(2)}, u32[]{:S(2)}) collective-permute-start(bf16[1,128,512]{2,1,0:T(8,128)(2,1)S(1)} %maximum_bitcast_fusion.refs_0_), channel_id=1, source_target_pairs={{0,2},{1,3},{2,0},{3,1},{4,6},{5,7},{6,4},{7,5},{8,10},{9,11},{10,... | collective-permute-start | bytes 393224 | tf_op jit(solution)/shard_map/ppermute | solution.py:28
  5.6 15.3 %collective-permute-start.1 = (bf16[1,128,512]{2,1,0:T(8,128)(2,1)S(1)}, bf16[1,128,512]{2,1,0:T(8,128)(2,1)S(1)}, u32[]{:S(2)}, u32[]{:S(2)}) collective-permute-start(bf16[1,128,512]{2,1,0:T(8,128)(2,1)S(1)} %maximum_bitcast_fusion.refs_0_), channel_id=1, source_target_pairs={{0,4},{1,5},{2,6},{3,7},{4,0},{5,1},{6,2},{7,3},{8,12},{9,13},{10,... | collective-permute-start | bytes 393224 | tf_op jit(solution)/shard_map/ppermute | solution.py:28
  8.2 12.7 %collective-permute-start.2 = (bf16[1,128,512]{2,1,0:T(8,128)(2,1)S(1)}, bf16[1,128,512]{2,1,0:T(8,128)(2,1)S(1)}, u32[]{:S(2)}, u32[]{:S(2)}) collective-permute-start(bf16[1,128,512]{2,1,0:T(8,128)(2,1)S(1)} %maximum_bitcast_fusion.refs_0_), channel_id=1, source_target_pairs={{0,6},{1,7},{2,4},{3,5},{4,2},{5,3},{6,0},{7,1},{8,14},{9,15},{10,... | collective-permute-start | bytes 393224 | tf_op jit(solution)/shard_map/ppermute | solution.py:28
  24.2 13.3 %collective-permute-start.6 = (bf16[4,128,512]{2,1,0:T(8,128)(2,1)}, bf16[4,128,512]{2,1,0:T(8,128)(2,1)S(1)}, u32[]{:S(2)}, u32[]{:S(2)}) collective-permute-start(bf16[4,128,512]{2,1,0:T(8,128)(2,1)} %shard_map.273.refs_1_), channel_id=1, source_target_pairs={{0,8},{8,0},{16,24},{24,16},{1,9},{9,1},{17,25},{25,17},{2,10},{10... | collective-permute-start | bytes 1572872 | tf_op jit(solution)/shard_map/ppermute | solution.py:28
  25.9 13.8 %collective-permute-start.8 = (bf16[4,128,512]{2,1,0:T(8,128)(2,1)}, bf16[4,128,512]{2,1,0:T(8,128)(2,1)S(1)}, u32[]{:S(2)}, u32[]{:S(2)}) collective-permute-start(bf16[4,128,512]{2,1,0:T(8,128)(2,1)} %shard_map.273.refs_1_), channel_id=1, source_target_pairs={{0,16},{8,24},{16,0},{24,8},{1,17},{9,25},{17,1},{25,9},{2,18},{10... | collective-permute-start | bytes 1572872 | tf_op jit(solution)/shard_map/ppermute | solution.py:28
  27.9 14.0 %collective-permute-start.3 = (bf16[1,144,512]{2,1,0:T(8,128)(2,1)}, bf16[1,144,512]{2,1,0:T(8,128)(2,1)}, u32[]{:S(2)}, u32[]{:S(2)}) collective-permute-start(bf16[1,144,512]{2,1,0:T(8,128)(2,1)} %bitcast.5.refs_0_), channel_id=1, source_target_pairs={{0,2},{1,3},{2,0},{3,1},{4,6},{5,7},{6,4},{7,5},{8,10},{9,11},{10,... | collective-permute-start | bytes 442376 | tf_op jit(solution)/shard_map/ppermute | solution.py:28
  28.6 13.9 %collective-permute-start.4 = (bf16[1,144,512]{2,1,0:T(8,128)(2,1)}, bf16[1,144,512]{2,1,0:T(8,128)(2,1)}, u32[]{:S(2)}, u32[]{:S(2)}) collective-permute-start(bf16[1,144,512]{2,1,0:T(8,128)(2,1)} %bitcast.5.refs_0_), channel_id=1, source_target_pairs={{0,4},{1,5},{2,6},{3,7},{4,0},{5,1},{6,2},{7,3},{8,12},{9,13},{10,... | collective-permute-start | bytes 442376 | tf_op jit(solution)/shard_map/ppermute | solution.py:28
  32.1 10.4 %collective-permute-start.5 = (bf16[1,144,512]{2,1,0:T(8,128)(2,1)}, bf16[1,144,512]{2,1,0:T(8,128)(2,1)}, u32[]{:S(2)}, u32[]{:S(2)}) collective-permute-start(bf16[1,144,512]{2,1,0:T(8,128)(2,1)} %bitcast.5.refs_0_), channel_id=1, source_target_pairs={{0,6},{1,7},{2,4},{3,5},{4,2},{5,3},{6,0},{7,1},{8,14},{9,15},{10,... | collective-permute-start | bytes 442376 | tf_op jit(solution)/shard_map/ppermute | solution.py:28
  38.2 6.9 %collective-permute-start.7 = (bf16[2,128,512]{2,1,0:T(8,128)(2,1)}, bf16[2,128,512]{2,1,0:T(8,128)(2,1)S(1)}, u32[]{:S(2)}, u32[]{:S(2)}) collective-permute-start(bf16[2,128,512]{2,1,0:T(8,128)(2,1)} %slice.216), channel_id=1, source_target_pairs={{0,16},{8,24},{16,0},{24,8},{1,17},{9,25},{17,1},{25,9},{2,18},{10... | collective-permute-start | bytes 786440 | tf_op jit(solution)/shard_map/ppermute | solution.py:28
  40.4 6.7 %collective-permute-start.9 = (bf16[2,128,512]{2,1,0:T(8,128)(2,1)}, bf16[2,128,512]{2,1,0:T(8,128)(2,1)}, u32[]{:S(2)}, u32[]{:S(2)}) collective-permute-start(bf16[2,128,512]{2,1,0:T(8,128)(2,1)} %slice.217), channel_id=1, source_target_pairs={{0,8},{8,0},{16,24},{24,16},{1,9},{9,1},{17,25},{25,17},{2,10},{10... | collective-permute-start | bytes 786440 | tf_op jit(solution)/shard_map/ppermute | solution.py:28
  41.9 9.7 %collective-permute-start.10 = (bf16[4,128,512]{2,1,0:T(8,128)(2,1)}, bf16[4,128,512]{2,1,0:T(8,128)(2,1)S(1)}, u32[]{:S(2)}, u32[]{:S(2)}) collective-permute-start(bf16[4,128,512]{2,1,0:T(8,128)(2,1)} %shard_map.273.refs_1_), channel_id=1, source_target_pairs={{0,1},{1,0},{2,3},{3,2},{4,5},{5,4},{6,7},{7,6},{8,9},{9,8},{10,11... | collective-permute-start | bytes 1572872 | tf_op jit(solution)/shard_map/ppermute | solution.py:28
  42.5 9.2 %collective-permute-start.11 = (bf16[4,128,512]{2,1,0:T(8,128)(2,1)S(1)}, bf16[4,128,512]{2,1,0:T(8,128)(2,1)}, u32[]{:S(2)}, u32[]{:S(2)}) collective-permute-start(bf16[4,128,512]{2,1,0:T(8,128)(2,1)S(1)} %collective-permute-done.6.refs_3_), channel_id=1, source_target_pairs={{0,1},{1,0},{2,3},{3,2},{4,5},{5,4},{6,7},{7,6},{8,9},{9,8},{10,11... | collective-permute-start | bytes 1572872 | tf_op jit(solution)/shard_map/ppermute | solution.py:28
  42.5 9.1 %collective-permute-start.12 = (bf16[4,128,512]{2,1,0:T(8,128)(2,1)S(1)}, bf16[4,128,512]{2,1,0:T(8,128)(2,1)}, u32[]{:S(2)}, u32[]{:S(2)}) collective-permute-start(bf16[4,128,512]{2,1,0:T(8,128)(2,1)S(1)} %collective-permute-done.8.refs_5_), channel_id=1, source_target_pairs={{0,1},{1,0},{2,3},{3,2},{4,5},{5,4},{6,7},{7,6},{8,9},{9,8},{10,11... | collective-permute-start | bytes 1572872 | tf_op jit(solution)/shard_map/ppermute | solution.py:28
  45.1 6.6 %collective-permute-start.13 = (bf16[2,128,512]{2,1,0:T(8,128)(2,1)S(1)}, bf16[2,128,512]{2,1,0:T(8,128)(2,1)}, u32[]{:S(2)}, u32[]{:S(2)}) collective-permute-start(bf16[2,128,512]{2,1,0:T(8,128)(2,1)S(1)} %collective-permute-done.7.refs_7_), channel_id=1, source_target_pairs={{0,1},{1,0},{2,3},{3,2},{4,5},{5,4},{6,7},{7,6},{8,9},{9,8},{10,11... | collective-permute-start | bytes 786440 | tf_op jit(solution)/shard_map/ppermute | solution.py:28
  51.7 16.0 %collective-permute-start.16 = (bf16[4,144,512]{2,1,0:T(8,128)(2,1)}, bf16[4,144,512]{2,1,0:T(8,128)(2,1)S(1)}, u32[]{:S(2)}, u32[]{:S(2)}) collective-permute-start(bf16[4,144,512]{2,1,0:T(8,128)(2,1)} %shard_map.274.refs_1_), channel_id=1, source_target_pairs={{0,8},{8,0},{16,24},{24,16},{1,9},{9,1},{17,25},{25,17},{2,10},{10... | collective-permute-start | bytes 1769480 | tf_op jit(solution)/shard_map/ppermute | solution.py:28
  53.2 15.7 %collective-permute-start.17 = (bf16[4,144,512]{2,1,0:T(8,128)(2,1)}, bf16[4,144,512]{2,1,0:T(8,128)(2,1)S(1)}, u32[]{:S(2)}, u32[]{:S(2)}) collective-permute-start(bf16[4,144,512]{2,1,0:T(8,128)(2,1)} %shard_map.274.refs_1_), channel_id=1, source_target_pairs={{0,16},{8,24},{16,0},{24,8},{1,17},{9,25},{17,1},{25,9},{2,18},{10... | collective-permute-start | bytes 1769480 | tf_op jit(solution)/shard_map/ppermute | solution.py:28
  59.8 14.9 %collective-permute-start.21 = (bf16[2,384,512]{2,1,0:T(8,128)(2,1)S(1)}, bf16[2,384,512]{2,1,0:T(8,128)(2,1)S(1)}, u32[]{:S(2)}, u32[]{:S(2)}) collective-permute-start(bf16[2,384,512]{2,1,0:T(8,128)(2,1)S(1)} %get-tuple-element.115), channel_id=1, source_target_pairs={{0,1},{1,2},{2,3},{3,4},{4,5},{5,6},{6,7},{8,9},{9,10},{10,11},{11... | collective-permute-start | bytes 2359304 | tf_op jit(solution)/shard_map/ppermute | solution.py:773
  61.7 13.0 %collective-permute-start.22 = (bf16[2,384,512]{2,1,0:T(8,128)(2,1)S(1)}, bf16[2,384,512]{2,1,0:T(8,128)(2,1)S(1)}, u32[]{:S(2)}, u32[]{:S(2)}) collective-permute-start(bf16[2,384,512]{2,1,0:T(8,128)(2,1)S(1)} %get-tuple-element.115), channel_id=1, source_target_pairs={{1,0},{2,1},{3,2},{4,3},{5,4},{6,5},{7,6},{9,8},{10,9},{11,10},{12... | collective-permute-start | bytes 2359304 | tf_op jit(solution)/shard_map/ppermute | solution.py:774
  74.7 6.6 %collective-permute-start.24 = (f32[2,4,512]{2,1,0:T(4,128)S(1)}, f32[2,4,512]{2,1,0:T(4,128)S(1)}, u32[]{:S(2)}, u32[]{:S(2)}) collective-permute-start(f32[2,4,512]{2,1,0:T(4,128)S(1)} %bitcast.148), channel_id=1, source_target_pairs={{0,4},{1,5},{2,6},{3,7},{4,0},{5,1},{6,2},{7,3},{8,12},{9,13},{10,... | collective-permute-start | bytes 49160 | tf_op jit(solution)/shard_map/ppermute | solution.py:28
  76.5 5.6 %collective-permute-start.25 = (f32[2,4,512]{2,1,0:T(4,128)S(1)}, f32[2,4,512]{2,1,0:T(4,128)S(1)}, u32[]{:S(2)}, u32[]{:S(2)}) collective-permute-start(f32[2,4,512]{2,1,0:T(4,128)S(1)} %bitcast.149), channel_id=1, source_target_pairs={{0,6},{1,7},{2,4},{3,5},{4,2},{5,3},{6,0},{7,1},{8,14},{9,15},{10,... | collective-permute-start | bytes 49160 | tf_op jit(solution)/shard_map/ppermute | solution.py:28
  79.0 11.1 %collective-permute-start.29 = (bf16[2,144,512]{2,1,0:T(8,128)(2,1)S(1)}, bf16[2,144,512]{2,1,0:T(8,128)(2,1)S(1)}, u32[]{:S(2)}, u32[]{:S(2)}) collective-permute-start(bf16[2,144,512]{2,1,0:T(8,128)(2,1)S(1)} %slice.170), channel_id=1, source_target_pairs={{0,16},{8,24},{16,0},{24,8},{1,17},{9,25},{17,1},{25,9},{2,18},{10... | collective-permute-start | bytes 884744 | tf_op jit(solution)/shard_map/ppermute | solution.py:28
  80.6 9.5 %collective-permute-start.30 = (bf16[2,144,512]{2,1,0:T(8,128)(2,1)S(1)}, bf16[2,144,512]{2,1,0:T(8,128)(2,1)S(1)}, u32[]{:S(2)}, u32[]{:S(2)}) collective-permute-start(bf16[2,144,512]{2,1,0:T(8,128)(2,1)S(1)} %slice.171), channel_id=1, source_target_pairs={{0,8},{8,0},{16,24},{24,16},{1,9},{9,1},{17,25},{25,17},{2,10},{10... | collective-permute-start | bytes 884744 | tf_op jit(solution)/shard_map/ppermute | solution.py:28
  81.3 9.5 %collective-permute-start.26 = (bf16[4,144,512]{2,1,0:T(8,128)(2,1)S(1)}, bf16[4,144,512]{2,1,0:T(8,128)(2,1)S(1)}, u32[]{:S(2)}, u32[]{:S(2)}) collective-permute-start(bf16[4,144,512]{2,1,0:T(8,128)(2,1)S(1)} %copy-done.11), channel_id=1, source_target_pairs={{0,1},{1,0},{2,3},{3,2},{4,5},{5,4},{6,7},{7,6},{8,9},{9,8},{10,11... | collective-permute-start | bytes 1769480 | tf_op jit(solution)/shard_map/ppermute | solution.py:28
  82.0 10.2 %collective-permute-start.27 = (bf16[4,144,512]{2,1,0:T(8,128)(2,1)S(1)}, bf16[4,144,512]{2,1,0:T(8,128)(2,1)S(1)}, u32[]{:S(2)}, u32[]{:S(2)}) collective-permute-start(bf16[4,144,512]{2,1,0:T(8,128)(2,1)S(1)} %collective-permute-done.16.refs_3_), channel_id=1, source_target_pairs={{0,1},{1,0},{2,3},{3,2},{4,5},{5,4},{6,7},{7,6},{8,9},{9,8},{10,11... | collective-permute-start | bytes 1769480 | tf_op jit(solution)/shard_map/ppermute | solution.py:28
  83.4 8.9 %collective-permute-start.28 = (bf16[4,144,512]{2,1,0:T(8,128)(2,1)S(1)}, bf16[4,144,512]{2,1,0:T(8,128)(2,1)S(1)}, u32[]{:S(2)}, u32[]{:S(2)}) collective-permute-start(bf16[4,144,512]{2,1,0:T(8,128)(2,1)S(1)} %collective-permute-done.17.refs_5_), channel_id=1, source_target_pairs={{0,1},{1,0},{2,3},{3,2},{4,5},{5,4},{6,7},{7,6},{8,9},{9,8},{10,11... | collective-permute-start | bytes 1769480 | tf_op jit(solution)/shard_map/ppermute | solution.py:28
  135.1 5.7 %collective-permute-start.46 = (f32[2,2,2048]{2,1,0:T(2,128)S(1)}, f32[2,2,2048]{2,1,0:T(2,128)S(1)}, u32[]{:S(2)}, u32[]{:S(2)}) collective-permute-start(f32[2,2,2048]{2,1,0:T(2,128)S(1)} %add_add_fusion.3), channel_id=1, source_target_pairs={{0,6},{1,7},{2,4},{3,5},{4,2},{5,3},{6,0},{7,1},{8,14},{9,15},{10,... | collective-permute-start | bytes 98312 | tf_op jit(solution)/shard_map/ppermute | solution.py:28
  140.8 15.8 %collective-permute-start.47 = (bf16[2,384,512]{2,1,0:T(8,128)(2,1)S(1)}, bf16[2,384,512]{2,1,0:T(8,128)(2,1)S(1)}, u32[]{:S(2)}, u32[]{:S(2)}) collective-permute-start(bf16[2,384,512]{2,1,0:T(8,128)(2,1)S(1)} %get-tuple-element.136), channel_id=1, source_target_pairs={{0,1},{1,2},{2,3},{3,4},{4,5},{5,6},{6,7},{8,9},{9,10},{10,11},{11... | collective-permute-start | bytes 2359304 | tf_op jit(solution)/shard_map/ppermute | solution.py:773
  142.2 14.5 %collective-permute-start.48 = (bf16[2,384,512]{2,1,0:T(8,128)(2,1)S(1)}, bf16[2,384,512]{2,1,0:T(8,128)(2,1)S(1)}, u32[]{:S(2)}, u32[]{:S(2)}) collective-permute-start(bf16[2,384,512]{2,1,0:T(8,128)(2,1)S(1)} %get-tuple-element.136), channel_id=1, source_target_pairs={{1,0},{2,1},{3,2},{4,3},{5,4},{6,5},{7,6},{9,8},{10,9},{11,10},{12... | collective-permute-start | bytes 2359304 | tf_op jit(solution)/shard_map/ppermute | solution.py:774
  169.0 5.7 %collective-permute-start.55 = (f32[2,2,2048]{2,1,0:T(2,128)S(1)}, f32[2,2,2048]{2,1,0:T(2,128)S(1)}, u32[]{:S(2)}, u32[]{:S(2)}) collective-permute-start(f32[2,2,2048]{2,1,0:T(2,128)S(1)} %add_add_fusion.1), channel_id=1, source_target_pairs={{0,6},{1,7},{2,4},{3,5},{4,2},{5,3},{6,0},{7,1},{8,14},{9,15},{10,... | collective-permute-start | bytes 98312 | tf_op jit(solution)/shard_map/ppermute | solution.py:28
  185.0 19.3 %collective-permute-start.63 = (bf16[2,384,512]{2,1,0:T(8,128)(2,1)S(1)}, bf16[2,384,512]{2,1,0:T(8,128)(2,1)S(1)}, u32[]{:S(2)}, u32[]{:S(2)}) collective-permute-start(bf16[2,384,512]{2,1,0:T(8,128)(2,1)S(1)} %get-tuple-element.143), channel_id=1, source_target_pairs={{0,1},{1,2},{2,3},{3,4},{4,5},{5,6},{6,7},{8,9},{9,10},{10,11},{11... | collective-permute-start | bytes 2359304 | tf_op jit(solution)/shard_map/ppermute | solution.py:773
  186.3 18.0 %collective-permute-start.64 = (bf16[2,384,512]{2,1,0:T(8,128)(2,1)S(1)}, bf16[2,384,512]{2,1,0:T(8,128)(2,1)S(1)}, u32[]{:S(2)}, u32[]{:S(2)}) collective-permute-start(bf16[2,384,512]{2,1,0:T(8,128)(2,1)S(1)} %get-tuple-element.143), channel_id=1, source_target_pairs={{1,0},{2,1},{3,2},{4,3},{5,4},{6,5},{7,6},{9,8},{10,9},{11,10},{12... | collective-permute-start | bytes 2359304 | tf_op jit(solution)/shard_map/ppermute | solution.py:774
  198.8 5.4 %collective-permute-start.62 = (f32[2,2,512]{2,1,0:T(2,128)S(1)}, f32[2,2,512]{2,1,0:T(2,128)S(1)}, u32[]{:S(2)}, u32[]{:S(2)}) collective-permute-start(f32[2,2,512]{2,1,0:T(2,128)S(1)} %add_add_fusion.9), channel_id=1, source_target_pairs={{0,6},{1,7},{2,4},{3,5},{4,2},{5,3},{6,0},{7,1},{8,14},{9,15},{10,... | collective-permute-start | bytes 24584 | tf_op jit(solution)/shard_map/ppermute | solution.py:28
  216.9 14.1 %collective-permute-start.69 = (bf16[16,208,512]{2,1,0:T(8,128)(2,1)}, bf16[16,208,512]{2,1,0:T(8,128)(2,1)S(1)}, u32[]{:S(2)}, u32[]{:S(2)}) collective-permute-start(bf16[16,208,512]{2,1,0:T(8,128)(2,1)} %get-tuple-element.149.refs_11_), channel_id=1, source_target_pairs={{0,1},{1,0},{2,3},{3,2},{4,5},{5,4},{6,7},{7,6},{8,9},{9,8},{10,11... | collective-permute-start | bytes 10223624 | tf_op jit(solution)/shard_map/ppermute | solution.py:28
  231.5 19.8 %collective-permute-start.73 = (bf16[2,2,208,512]{3,2,1,0:T(8,128)(2,1)S(1)}, bf16[2,2,208,512]{3,2,1,0:T(8,128)(2,1)S(1)}, u32[]{:S(2)}, u32[]{:S(2)}) collective-permute-start(bf16[2,2,208,512]{3,2,1,0:T(8,128)(2,1)S(1)} %get-tuple-element.157), channel_id=1, source_target_pairs={{0,8},{8,0},{16,24},{24,16},{1,9},{9,1},{17,25},{25,17},{2,10},{10... | collective-permute-start | bytes 2555912 | tf_op jit(solution)/shard_map/ppermute | solution.py:28
  232.2 19.3 %collective-permute-start.74 = (bf16[2,2,208,512]{3,2,1,0:T(8,128)(2,1)S(1)}, bf16[2,2,208,512]{3,2,1,0:T(8,128)(2,1)S(1)}, u32[]{:S(2)}, u32[]{:S(2)}) collective-permute-start(bf16[2,2,208,512]{3,2,1,0:T(8,128)(2,1)S(1)} %get-tuple-element.158), channel_id=1, source_target_pairs={{0,16},{8,24},{16,0},{24,8},{1,17},{9,25},{17,1},{25,9},{2,18},{10... | collective-permute-start | bytes 2555912 | tf_op jit(solution)/shard_map/ppermute | solution.py:28
  234.0 5.4 %collective-permute-start.72 = (f32[2,2,512]{2,1,0:T(2,128)S(1)}, f32[2,2,512]{2,1,0:T(2,128)S(1)}, u32[]{:S(2)}, u32[]{:S(2)}) collective-permute-start(f32[2,2,512]{2,1,0:T(2,128)S(1)} %add_add_fusion.7), channel_id=1, source_target_pairs={{0,6},{1,7},{2,4},{3,5},{4,2},{5,3},{6,0},{7,1},{8,14},{9,15},{10,... | collective-permute-start | bytes 24584 | tf_op jit(solution)/shard_map/ppermute | solution.py:28
  251.5 14.7 %collective-permute-start.77 = (bf16[16,64,512]{2,1,0:T(8,128)(2,1)S(1)}, bf16[16,64,512]{2,1,0:T(8,128)(2,1)S(1)}, u32[]{:S(2)}, u32[]{:S(2)}) collective-permute-start(bf16[16,64,512]{2,1,0:T(8,128)(2,1)S(1)} %get-tuple-element.168), channel_id=1, source_target_pairs={{0,1},{1,0},{2,3},{3,2},{4,5},{5,4},{6,7},{7,6},{8,9},{9,8},{10,11... | collective-permute-start | bytes 3145736 | tf_op jit(solution)/shard_map/ppermute | solution.py:28
  251.8 12.3 %collective-permute-start.75 = (bf16[2,208,512]{2,1,0:T(8,128)(2,1)S(1)}, bf16[2,208,512]{2,1,0:T(8,128)(2,1)S(1)}, u32[]{:S(2)}, u32[]{:S(2)}) collective-permute-start(bf16[2,208,512]{2,1,0:T(8,128)(2,1)S(1)} %get-tuple-element.164), channel_id=1, source_target_pairs={{0,8},{8,0},{16,24},{24,16},{1,9},{9,1},{17,25},{25,17},{2,10},{10... | collective-permute-start | bytes 1277960 | tf_op jit(solution)/shard_map/ppermute | solution.py:28
  253.6 11.9 %collective-permute-start.76 = (bf16[2,208,512]{2,1,0:T(8,128)(2,1)S(1)}, bf16[2,208,512]{2,1,0:T(8,128)(2,1)S(1)}, u32[]{:S(2)}, u32[]{:S(2)}) collective-permute-start(bf16[2,208,512]{2,1,0:T(8,128)(2,1)S(1)} %get-tuple-element.165), channel_id=1, source_target_pairs={{0,16},{8,24},{16,0},{24,8},{1,17},{9,25},{17,1},{25,9},{2,18},{10... | collective-permute-start | bytes 1277960 | tf_op jit(solution)/shard_map/ppermute | solution.py:28
  266.4 7.7 %collective-permute-start.79 = (bf16[2,2,64,512]{3,2,1,0:T(8,128)(2,1)S(1)}, bf16[2,2,64,512]{3,2,1,0:T(8,128)(2,1)S(1)}, u32[]{:S(2)}, u32[]{:S(2)}) collective-permute-start(bf16[2,2,64,512]{3,2,1,0:T(8,128)(2,1)S(1)} %get-tuple-element.172), channel_id=1, source_target_pairs={{0,8},{8,0},{16,24},{24,16},{1,9},{9,1},{17,25},{25,17},{2,10},{10... | collective-permute-start | bytes 786440 | tf_op jit(solution)/shard_map/ppermute | solution.py:28
  266.8 7.6 %collective-permute-start.80 = (bf16[2,2,64,512]{3,2,1,0:T(8,128)(2,1)S(1)}, bf16[2,2,64,512]{3,2,1,0:T(8,128)(2,1)S(1)}, u32[]{:S(2)}, u32[]{:S(2)}) collective-permute-start(bf16[2,2,64,512]{3,2,1,0:T(8,128)(2,1)S(1)} %get-tuple-element.173), channel_id=1, source_target_pairs={{0,16},{8,24},{16,0},{24,8},{1,17},{9,25},{17,1},{25,9},{2,18},{10... | collective-permute-start | bytes 786440 | tf_op jit(solution)/shard_map/ppermute | solution.py:28
  268.0 6.1 %collective-permute-start.78 = (bf16[1,208,512]{2,1,0:T(8,128)(2,1)S(1)}, bf16[1,208,512]{2,1,0:T(8,128)(2,1)S(1)}, u32[]{:S(2)}, u32[]{:S(2)}) collective-permute-start(bf16[1,208,512]{2,1,0:T(8,128)(2,1)S(1)} %get-tuple-element.250), channel_id=1, source_target_pairs={{0,2},{1,3},{2,0},{3,1},{4,6},{5,7},{6,4},{7,5},{8,10},{9,11},{10,... | collective-permute-start | bytes 638984 | tf_op jit(solution)/shard_map/ppermute | solution.py:28
  279.7 6.0 %collective-permute-start.83 = (bf16[2,64,512]{2,1,0:T(8,128)(2,1)S(1)}, bf16[2,64,512]{2,1,0:T(8,128)(2,1)S(1)}, u32[]{:S(2)}, u32[]{:S(2)}) collective-permute-start(bf16[2,64,512]{2,1,0:T(8,128)(2,1)S(1)} %get-tuple-element.245), channel_id=1, source_target_pairs={{0,8},{8,0},{16,24},{24,16},{1,9},{9,1},{17,25},{25,17},{2,10},{10... | collective-permute-start | bytes 393224 | tf_op jit(solution)/shard_map/ppermute | solution.py:28
  281.1 10.0 %collective-permute-start.87 = (bf16[1,208,512]{2,1,0:T(8,128)(2,1)S(1)}, bf16[1,208,512]{2,1,0:T(8,128)(2,1)S(1)}, u32[]{:S(2)}, u32[]{:S(2)}) collective-permute-start(bf16[1,208,512]{2,1,0:T(8,128)(2,1)S(1)} %get-tuple-element.249), channel_id=1, source_target_pairs={{0,6},{1,7},{2,4},{3,5},{4,2},{5,3},{6,0},{7,1},{8,14},{9,15},{10,... | collective-permute-start | bytes 638984 | tf_op jit(solution)/shard_map/ppermute | solution.py:28
  283.2 19.4 %collective-permute-start.86 = (bf16[1,208,512]{2,1,0:T(8,128)(2,1)S(1)}, bf16[1,208,512]{2,1,0:T(8,128)(2,1)S(1)}, u32[]{:S(2)}, u32[]{:S(2)}) collective-permute-start(bf16[1,208,512]{2,1,0:T(8,128)(2,1)S(1)} %get-tuple-element.248), channel_id=1, source_target_pairs={{0,4},{1,5},{2,6},{3,7},{4,0},{5,1},{6,2},{7,3},{8,12},{9,13},{10,... | collective-permute-start | bytes 638984 | tf_op jit(solution)/shard_map/ppermute | solution.py:28
  283.2 19.5 %collective-permute-start.82 = (bf16[1,64,512]{2,1,0:T(8,128)(2,1)S(1)}, bf16[1,64,512]{2,1,0:T(8,128)(2,1)S(1)}, u32[]{:S(2)}, u32[]{:S(2)}) collective-permute-start(bf16[1,64,512]{2,1,0:T(8,128)(2,1)S(1)} %slice.304), channel_id=1, source_target_pairs={{0,2},{1,3},{2,0},{3,1},{4,6},{5,7},{6,4},{7,5},{8,10},{9,11},{10,... | collective-permute-start | bytes 196616 | tf_op jit(solution)/shard_map/ppermute | solution.py:28
  285.7 16.9 %collective-permute-start.85 = (bf16[1,64,512]{2,1,0:T(8,128)(2,1)S(1)}, bf16[1,64,512]{2,1,0:T(8,128)(2,1)S(1)}, u32[]{:S(2)}, u32[]{:S(2)}) collective-permute-start(bf16[1,64,512]{2,1,0:T(8,128)(2,1)S(1)} %get-tuple-element.252), channel_id=1, source_target_pairs={{0,6},{1,7},{2,4},{3,5},{4,2},{5,3},{6,0},{7,1},{8,14},{9,15},{10,... | collective-permute-start | bytes 196616 | tf_op jit(solution)/shard_map/ppermute | solution.py:28
  287.9 16.1 %collective-permute-start.84 = (bf16[1,64,512]{2,1,0:T(8,128)(2,1)S(1)}, bf16[1,64,512]{2,1,0:T(8,128)(2,1)S(1)}, u32[]{:S(2)}, u32[]{:S(2)}) collective-permute-start(bf16[1,64,512]{2,1,0:T(8,128)(2,1)S(1)} %get-tuple-element.251), channel_id=1, source_target_pairs={{0,4},{1,5},{2,6},{3,7},{4,0},{5,1},{6,2},{7,3},{8,12},{9,13},{10,... | collective-permute-start | bytes 196616 | tf_op jit(solution)/shard_map/ppermute | solution.py:28
  (88 other events, 926.1 us)

commit v2 on v1

--- a/solution.py
+++ b/solution.py
@@ -2,6 +2,7 @@
 
 import jax
 import jax.numpy as jnp
+import numpy as np
 from jax import lax
 from jax.experimental import pallas as pl
 from jax.experimental.pallas import tpu as pltpu
@@ -140,10 +141,10 @@
     )(*pieces, *after)
 
 
-def owners(batch_mask, core_mask, line):
+def owners(table):
     mine, batch = lax.axis_index("rows"), lax.axis_index("batch")
-    chip = (batch ^ batch_mask) * (lax.axis_size("rows") // 2) + ((mine >> 1) ^ line)
-    return chip * 2 + ((mine & 1) ^ core_mask)
+    far, near, core = np.array(table, np.int32).T
+    return ((batch ^ far) * (lax.axis_size("rows") // 2) + ((mine >> 1) ^ near)) * 2 + ((mine & 1) ^ core)
 
 
 class Gather:
@@ -164,14 +165,14 @@
         return swap(from_x[:half], "batch", 2), swap(from_y[half:], "batch", 1)
 
     def pieces(self, far_low, far_high):
-        got = []
+        got, table = [], []
         half = far_low.shape[0]
         parts = ((self.block, 0, 0), (self.from_x, 1, 0), (self.from_y, 2, 0), (far_low, 3, 0), (far_high, 3, half))
         for piece, mask, first in parts:
-            place = first + jnp.arange(piece.shape[0], dtype=jnp.int32)
             for array, core in ((piece, 0), (swap(piece, "rows", 1), 1)):
-                got.append((array, owners(mask, core, place)))
-        return got
+                got.append(array)
+                table += [(mask, first + j, core) for j in range(piece.shape[0])]
+        return got, table
 
 
 def in_order(*values):
@@ -179,10 +180,10 @@
 
 
 class Assembly:
-    def __init__(self, pieces, first, size):
+    def __init__(self, arrays, table, first, size):
         self.first, self.size = first, size
-        owner = jnp.concatenate([owner for _, owner in pieces]).astype(jnp.int32)
-        self.ins = [smem(owner * size)] + [whole(array) for array, _ in pieces]
+        starts = owners(table) * size if table else jnp.zeros(1, jnp.int32)
+        self.ins = [smem(starts)] + [whole(array) for array in arrays]
         self.count = len(self.ins)
 
     def run(self, refs, held):
@@ -464,7 +465,7 @@
         for col in range(task_ref.shape[-1] // lanes):
             cols = pl.ds(col * lanes, lanes)
             t = [task_ref[k, 0, 0, 0, rows, cols].astype(F32) for k in range(3)]
-            out_ref[0, rows, cols] = c[0] * t[0] + c[1] * t[1] + c[2] * t[2]
+            out_ref[0, rows, cols] = (c[0] * t[0] + c[1] * t[1] + c[2] * t[2]).astype(BF16)
         return carry
 
     loop(task_ref.shape[4], step, 0, unroll=1)
@@ -572,8 +573,8 @@
         u = centred * scale + (shift + x_ref[0, rows, :].astype(F32))
         mask = wide(mask_ref[0, 0, rows, :], width)
         block_ref[0, rows, :] = (softplus(u) * mask).astype(BF16)
-        du = up_ref[0, rows, :] * sigmoid(u)
-        du_ref[0, rows, :] = du
+        du = up_ref[0, rows, :].astype(F32) * sigmoid(u)
+        du_ref[0, rows, :] = du.astype(BF16)
         return carry[0] + fold(du), carry[1] + fold(du * centred)
 
     got = loop(a_ref.shape[1], step, zeros8(width))
@@ -602,7 +603,7 @@
         slope = grads3_ref[0, 1:2, cols] * inv * rstd
 
         def step(rows, carry):
-            d = du_ref[0, rows, cols] - (base + (a3_ref[0, rows, cols] - mean) * slope)
+            d = du_ref[0, rows, cols].astype(F32) - (base + (a3_ref[0, rows, cols] - mean) * slope)
             d_ref[0, rows, cols] = (d * scale * wide(mask_ref[0, 0, rows, :], tile)).astype(BF16)
             return carry
 
@@ -756,7 +757,7 @@
 
 
 def input_grad_kernel(d_ref, w_ref, du_ref, out_ref):
-    out_ref[...] = (dot(d_ref[...], w_ref[...], NT) + du_ref[...]).astype(BF16)
+    out_ref[...] = (dot(d_ref[...], w_ref[...], NT) + du_ref[...].astype(F32)).astype(BF16)
 
 
 def adamw(weight, first, second, grad, rate, decay):
@@ -807,7 +808,7 @@
                 (masks, block((1, 1, columns, 128), functools.partial(lambda m, r: (1, m, r, 0), micro))),
             ],
             [out((8, 128), F32, (8, 128), lambda r: (0, 0))],
-            flops=6 * total_pixels * chan, nbytes=3 * total_pixels * chan, vmem=10,
+            flops=6 * total_pixels * chan, nbytes=3 * total_pixels * chan, vmem=4,
         ))
     x = features.reshape(micros, pixels, chan)
     params = [norm_params[:, :inner], norm_params[:, inner : 2 * inner], norm_params[:, 2 * inner :]]
@@ -831,7 +832,6 @@
     low_mid = weight_mid.astype(BF16)
     both = jnp.concatenate([weight_in.astype(BF16), weight_out.T.astype(BF16)], axis=0)
     direct = part_rows % 16 == 0 and mid_rows % 16 == 0
-    zero = jnp.zeros(1, jnp.int32)
     if direct:
         gather_both, gather_mid = Gather(), Gather()
         line_both = gather_both.along_line(both)
@@ -839,22 +839,21 @@
         from_both = gather_both.near(near_both)
         line_mid = gather_mid.along_line(low_mid)
         far_both = gather_both.far(*from_both)
-        pieces = gather_both.pieces(*far_both)
+        arrays, table = gather_both.pieces(*far_both)
         line_mid = in_order(*line_mid, *far_both)[: len(line_mid)]
-        near_mid, *arrays = in_order(joined(line_mid), *[array for array, _ in pieces])
+        near_mid, *arrays = in_order(joined(line_mid), *arrays)
         from_mid = gather_mid.near(near_mid)
-        pieces = [(array, owner) for array, (_, owner) in zip(arrays, pieces)]
-        ins_in, ins_out = [Assembly(pieces, k * part_rows, part_rows) for k in range(2)]
+        ins_in, ins_out = [Assembly(arrays, table, k * part_rows, part_rows) for k in range(2)]
     else:
         full = gather_shards(both).reshape(-1, 2, part_rows, inner)
-        ins_in, ins_out = [Assembly([(full[:, k].reshape(1, -1, inner), zero)], 0, chan) for k in range(2)]
-        ins_mid = Assembly([(gather_shards(low_mid).reshape(1, -1, inner), zero)], 0, 9 * inner)
+        ins_in, ins_out = [Assembly([full[:, k].reshape(1, -1, inner)], (), 0, chan) for k in range(2)]
+        ins_mid = Assembly([gather_shards(low_mid).reshape(1, -1, inner)], (), 0, 9 * inner)
     whole_weight = constant((chan, inner), BF16)
     a_one, a_one_low, part, w_in = call(
         functools.partial(first_kernel, ins_in), (micros,),
         [per_micro(x), own_mask, per_micro(jnp.stack(grams)), *ins_in.ins],
         [out_micro(inner, F32), out_micro(inner, BF16), out_micro(inner, F32, 4), whole_weight],
-        flops=2 * big * inner, nbytes=2 * big + 8 * small, vmem=18,
+        flops=2 * big * inner, nbytes=2 * big + 8 * small, vmem=12,
     )
     a_one_up, a_one_down = neighbours(a_one_low)
     core_one = group_sum(part, "rows", 0, 2)
@@ -869,13 +868,13 @@
     upstream = call(
         upstream_kernel, (micros, row_span),
         [whole(stats_one), task_rows, row_mask],
-        [out((micros, pixels, chan), F32, (1, columns, chan), lambda m, r: (m, r, 0))],
+        [out((micros, pixels, chan), BF16, (1, columns, chan), lambda m, r: (m, r, 0))],
         [pltpu.VMEM((3, 8, 128), F32)],
-        flops=8 * big, nbytes=10 * big, vmem=10,
+        flops=8 * big, nbytes=10 * big, vmem=6,
     )
     if direct:
         upstream, *far_mid = in_order(upstream, *far_mid)
-        ins_mid = Assembly(gather_mid.pieces(*far_mid), 0, mid_rows)
+        ins_mid = Assembly(*gather_mid.pieces(*far_mid), 0, mid_rows)
     padded = (3, row_span, columns + 2 * PAD, inner)
     held = pltpu.VMEM((9 * inner, inner), BF16)
     taps = [pltpu.VMEM((pixels, 3 * inner), BF16), pltpu.VMEM(padded, F32), held]
@@ -891,10 +890,10 @@
             out_micro(inner, F32), out_micro(inner, BF16), out_micro(inner, F32, 2),
         ],
         taps,
-        flops=18 * small * inner, nbytes=20 * small + 18 * inner * inner, vmem=32,
+        flops=18 * small * inner, nbytes=20 * small + 18 * inner * inner, vmem=27,
     )
     w_out = call(
-        functools.partial(assemble_kernel, ins_out), (1,), ins_out.ins, [whole_weight], nbytes=8 * chan * inner, vmem=16
+        functools.partial(assemble_kernel, ins_out), (1,), ins_out.ins, [whole_weight], nbytes=8 * chan * inner, vmem=9
     )
     stats_two = all_sum(part)
     h_two, a_three, part = call(
@@ -904,7 +903,7 @@
             whole(w_out),
         ],
         [out_micro(inner, BF16), out_micro(chan, F32), out_micro(chan, F32, 2)],
-        flops=2 * big * inner, nbytes=4 * big + 8 * small, vmem=20,
+        flops=2 * big * inner, nbytes=4 * big + 8 * small, vmem=13,
     )
     stats_three = all_sum(part)
     stats_three, a_two_low = in_order(stats_three, a_two_low)
@@ -923,8 +922,8 @@
             smem(inverse), tiled(stats_three), (params[2], block((2, tile), lambda m, c: (0, c))),
             tiled(a_three), tiled(x), tiled(upstream), own_mask,
         ],
-        [out_tiled(BF16), out_tiled(F32), out_tiled(F32, 2)],
-        flops=40 * big, nbytes=16 * big, vmem=14,
+        [out_tiled(BF16), out_tiled(BF16), out_tiled(F32, 2)],
+        flops=40 * big, nbytes=16 * big, vmem=9,
     )
     part, a_two_up, a_two_down = in_order(part, a_two_up, a_two_down)
     grads_three = all_sum(part)
@@ -936,7 +935,7 @@
             per_micro(a_two), own_mask, whole(w_out),
         ],
         [out_micro(chan, BF16), out_micro(inner, F32), out_micro(inner, BF16), out_micro(inner, F32, 2)],
-        flops=2 * big * inner, nbytes=10 * big, vmem=26,
+        flops=2 * big * inner, nbytes=10 * big, vmem=20,
     )
     dz_two_up, dz_two_down = neighbours(dz_two_low)
     grads_two = all_sum(part)
@@ -949,7 +948,7 @@
         ],
         [out_micro(3 * inner, BF16), out_micro(3 * inner, BF16)],
         [pltpu.VMEM(padded[1:], F32)],
-        flops=60 * small, nbytes=28 * small, vmem=20,
+        flops=60 * small, nbytes=28 * small, vmem=16,
     )
     spread = Spread(inner, 9 * inner, chan)
     grads = call(
@@ -967,7 +966,7 @@
             whole(h_two.reshape(total_pixels, inner)), *spread.ins,
         ],
         spread.outs, [pltpu.VMEM((9 * inner, inner), BF16)],
-        flops=18 * small * inner + 2 * big * inner, nbytes=12 * small + 18 * inner * inner, vmem=30,
+        flops=18 * small * inner + 2 * big * inner, nbytes=12 * small + 18 * inner * inner, vmem=21,
     )
     sums = Sums(spread, grads)
     dz_one, part = call(
@@ -978,7 +977,7 @@
         ],
         [out_micro(inner, F32), out_micro(inner, F32, 2)],
         [pltpu.VMEM(padded, F32), held],
-        flops=18 * small * inner, nbytes=30 * small + 18 * inner * inner, vmem=26,
+        flops=18 * small * inner, nbytes=30 * small + 18 * inner * inner, vmem=21,
     )
     chip_one = chip_sums(part)
     if sums.direct:
@@ -996,7 +995,7 @@
         ],
         [out((micros, pixels, inner), BF16, (micros, pixels, inner), lambda c: (0, 0, 0)), *spread_in.outs],
         [pltpu.VMEM((tile, inner), F32)],
-        flops=2 * big * inner, nbytes=4 * big, vmem=20,
+        flops=2 * big * inner, nbytes=4 * big, vmem=14,
     )
     if sums.direct:
         d_one, *rest = in_order(d_one, *grad_in, *sums.far)
@@ -1014,14 +1013,14 @@
             (d_resid.reshape(total_pixels, chan), block((strip, chan), lambda s: (s, 0))),
         ],
         [out((total_pixels, chan), BF16, (strip, chan), lambda s: (s, 0))],
-        flops=2 * big * inner, nbytes=8 * big, vmem=16,
+        flops=2 * big * inner, nbytes=8 * big, vmem=11,
     )
     if sums.direct:
         input_grad, *sums.near = in_order(input_grad, *sums.near)
         line, *sends = in_order(sums.send_line(), *sums_in.send_far())
         sums.take_line(line)
         sums_in.take_far(sends)
-        sums.parts[1], *sums_in.far = in_order(sums.parts[1], *sums_in.far)
+        sums.parts[1], sums.parts[2], *sums_in.far = in_order(*sums.parts[1:3], *sums_in.far)
         sums_in.take_near(sums_in.send_near())
         sums_in.take_line(sums_in.send_line())
     grad_in, grad_both = sums_in.finish(), sums.finish()

time: 324 us -> 305 us (0.941)
  local copies, waits for them, and re-layouts: 27.9 us -> 15 us
  waiting for transfers between devices: 99 us -> 87.7 us
  starting transfers between devices: 103 us -> 112 us
    unnamed x82 -> x64, local copies, waits for them, and re-layouts: 22.9 us -> 11.3 us
    ppermute x89, waiting for transfers between devices: 99 us -> 87.7 us  [swap(): lax.ppermute(x, axis, [(i, i ^ mask) for i in range(lax.axis_size(axis))])]
    ppermute x3, starting transfers between devices: 4.57 us -> 9.24 us  [neighbours(): above = lax.ppermute(x, 'rows', [(i, i + 1) for i in range(count - 1)])]
    ppermute x89, starting transfers between devices: 94.8 us -> 99 us  [swap(): lax.ppermute(x, axis, [(i, i ^ mask) for i in range(lax.axis_size(axis))])]
  transfers between devices with their start and end apart: 95 -> 95, of which waited for: 57 -> 59; matrix products, arithmetic and copies ran while one was open for 4% -> 3% of each run, Pallas kernels for 12% -> 13%
where the time goes in v2:
time: 305 us; the launch traced here: 304 us
  starting transfers between devices  112 us (37%)
  waiting for transfers between devices  87.7 us (29%)
  Pallas kernels  73.6 us (24%)
  local copies, waits for them, and re-layouts  15 us (5%)
  other arithmetic  11.7 us (4%)
  between operations  3.99 us (1%)
    ppermute x89, starting transfers between devices, swap(): lax.ppermute(x, axis, [(i, i ^ mask) for i in range(lax.axis_size(axis))])  99 us
    ppermute x89, waiting for transfers between devices, swap(): lax.ppermute(x, axis, [(i, i ^ mask) for i in range(lax.axis_size(axis))])  87.7 us
    pallas_call x14, Pallas kernels, call(): pl.pallas_call(kernel, grid=grid, in_specs=[spec for _, spec in ins], out...  69.7 us
    unnamed x64, local copies, waits for them, and re-layouts  11.3 us
    ppermute x3, starting transfers between devices, neighbours(): above = lax.ppermute(x, 'rows', [(i, i + 1) for i in range(count - 1)])  9.24 us
  transfers between devices with their start and end apart: 95, of which 59 were waited for; matrix products, arithmetic and copies ran while one was open for 3% of the time, Pallas kernels for 13%

profile of v2, /device:TPU:0, one launch (start us, length us, event | category | flops | bytes accessed | tf_op | source)
XLA Modules:
  0.0 304.3 jit_solution(5629041979895910508)
XLA Ops:
  2.5 5.1 %collective-permute-start.2 = (bf16[1,128,512]{2,1,0:T(8,128)(2,1)S(1)}, bf16[1,128,512]{2,1,0:T(8,128)(2,1)S(1)}, u32[]{:S(2)}, u32[]{:S(2)}) collective-permute-start(bf16[1,128,512]{2,1,0:T(8,128)(2,1)S(1)} %maximum_bitcast_fusion.refs_0_), channel_id=1, source_target_pairs={{0,6},{1,7},{2,4},{3,5},{4,2},{5,3},{6,0},{7,1},{8,14},{9,15},{10,... | collective-permute-start | bytes 393224 | tf_op jit(solution)/shard_map/ppermute | solution.py:29
  11.8 3.7 %copy-done = bf16[3,2,1,4,96,2048]{5,4,3,2,1,0:T(8,128)(2,1)S(1)} copy-done((bf16[3,2,1,4,96,2048]{5,4,3,2,1,0:T(8,128)(2,1)S(1)}, bf16[3,2,1,4,96,2048]{5,4,3,2,1,0:T(8,128)(2,1)}, u32[]{:S(2)}) %copy-start) | copy-done | bytes 9437208
  15.5 2.1 shard_map.353.refs_5_
  17.7 2.1 shard_map.352.refs_4_
  21.8 1.9 shard_map.354.refs_1_
  23.7 1.7 collective-permute-start.8
  26.9 3.6 %collective-permute-start.5 = (bf16[1,144,512]{2,1,0:T(8,128)(2,1)}, bf16[1,144,512]{2,1,0:T(8,128)(2,1)}, u32[]{:S(2)}, u32[]{:S(2)}) collective-permute-start(bf16[1,144,512]{2,1,0:T(8,128)(2,1)} %bitcast.5.refs_0_), channel_id=1, source_target_pairs={{0,6},{1,7},{2,4},{3,5},{4,2},{5,3},{6,0},{7,1},{8,14},{9,15},{10,... | collective-permute-start | bytes 442376 | tf_op jit(solution)/shard_map/ppermute | solution.py:29
  31.2 5.8 %collective-permute-done.8.refs_5_ = bf16[4,128,512]{2,1,0:T(8,128)(2,1)S(1)} collective-permute-done((bf16[4,128,512]{2,1,0:T(8,128)(2,1)}, bf16[4,128,512]{2,1,0:T(8,128)(2,1)S(1)}, u32[]{:S(2)}, u32[]{:S(2)}) %collective-permute-start.8) | collective-permute-done | bytes 524320 | tf_op jit(solution)/shard_map/ppermute | solution.py:29
  42.3 2.3 collective-permute-done.9.refs_9_
  44.6 2.0 collective-permute-done.7.refs_7_
  47.3 2.0 shard_map.355.refs_1_
  51.5 1.9 copy-done.2
  53.4 4.1 %shard_map.356 = (f32[2,384,512]{2,1,0:T(8,128)S(1)}, bf16[2,384,512]{2,1,0:T(8,128)(2,1)S(1)}, f32[2,4,512]{2,1,0:T(4,128)S(1)}, bf16[2048,512]{1,0:T(8,128)(2,1)S(1)}) custom-call(bf16[2,384,2048]{2,1,0:T(8,128)(2,1)S(1)} %bitcast.116, f32[3,2,384,128]{3,2,1,0:T(8,128)S(1)} %broadcast_in_dim.6.mask_ref, f32[2,8,128]{2,1,0:T(8,128)S(1)} %pad_maximum_fusion.1.gram_ref, ...), custom_call_target="tpu_custom_call" | custom-call | flops 1610612736 | bytes 6291456 | tf_op jit(solution)/shard_map/pallas_call | solution.py:333
  58.8 3.1 %collective-permute-start.21 = (bf16[2,384,512]{2,1,0:T(8,128)(2,1)S(1)}, bf16[2,384,512]{2,1,0:T(8,128)(2,1)S(1)}, u32[]{:S(2)}, u32[]{:S(2)}) collective-permute-start(bf16[2,384,512]{2,1,0:T(8,128)(2,1)S(1)} %get-tuple-element.116), channel_id=1, source_target_pairs={{0,1},{1,2},{2,3},{3,4},{4,5},{5,6},{6,7},{8,9},{9,10},{10,11},{11... | collective-permute-start | bytes 2359304 | tf_op jit(solution)/shard_map/ppermute | solution.py:774
  72.4 3.8 %collective-permute-start.25 = (f32[2,4,512]{2,1,0:T(4,128)S(1)}, f32[2,4,512]{2,1,0:T(4,128)S(1)}, u32[]{:S(2)}, u32[]{:S(2)}) collective-permute-start(f32[2,4,512]{2,1,0:T(4,128)S(1)} %bitcast.146), channel_id=1, source_target_pairs={{0,6},{1,7},{2,4},{3,5},{4,2},{5,3},{6,0},{7,1},{8,14},{9,15},{10,... | collective-permute-start | bytes 49160 | tf_op jit(solution)/shard_map/ppermute | solution.py:29
  79.2 1.7 collective-permute-done.24
  81.4 3.7 %copy-done.1 = bf16[3,2,1,4,96,2048]{5,4,3,2,1,0:T(8,128)(2,1)S(1)} copy-done((bf16[3,2,1,4,96,2048]{5,4,3,2,1,0:T(8,128)(2,1)S(1)}, bf16[3,2,1,4,96,2048]{5,4,3,2,1,0:T(8,128)(2,1)}, u32[]{:S(2)}) %copy-start.1) | copy-done | bytes 9437208
  85.0 3.2 %shard_map.357.refs_11_.up_ref = bf16[2,384,2048]{2,1,0:T(8,128)(2,1)S(1)} custom-call(f32[2,4,512]{2,1,0:T(4,128)S(1)} %bitcast.128, bf16[3,2,1,4,96,2048]{5,4,3,2,1,0:T(8,128)(2,1)S(1)} %copy-done.1, f32[3,2,384,128]{3,2,1,0:T(8,128)S(1)} %broadcast_in_dim.6.mask_ref), custom_call_target="tpu_custom_call" | custom-call | flops 12582912 | bytes 15728640 | tf_op jit(solution)/shard_map/pallas_call | solution.py:333
  90.3 9.3 %shard_map.358 = (bf16[3,2,384,512]{3,2,1,0:T(8,128)(2,1)S(1)}, f32[2,384,512]{2,1,0:T(8,128)S(1)}, bf16[2,384,512]{2,1,0:T(8,128)(2,1)S(1)}, f32[2,2,512]{2,1,0:T(2,128)S(1)}) custom-call(f32[2]{0:T(128)S(1)} %convert_divide_fusion.inv_ref, f32[2,4,512]{2,1,0:T(4,128)S(1)} %bitcast.129, f32[2,512]{1,0:T(2,128)S(1)} %get-tuple-element.258.param_ref.param1_ref, ...), custom_call_target="tpu_custom_call" | custom-call | flops 3623878656 | bytes 12582912 | tf_op jit(solution)/shard_map/pallas_call | solution.py:333
  109.4 2.6 collective-permute-start.37
  113.6 6.3 %shard_map.360 = (bf16[2,384,512]{2,1,0:T(8,128)(2,1)S(1)}, f32[2,384,2048]{2,1,0:T(8,128)S(1)}, f32[2,2,2048]{2,1,0:T(2,128)S(1)}) custom-call(f32[2]{0:T(128)S(1)} %convert_divide_fusion.inv_ref, f32[2,2,512]{2,1,0:T(2,128)S(1)} %add_add_fusion.10.sums_ref.stats2_ref, f32[2,512]{1,0:T(2,128)S(1)} %get-tuple-element.257.param_ref.param2_ref, ...), custom_call_target="tpu_custom_call" | custom-call | flops 1610612736 | bytes 9437184 | tf_op jit(solution)/shard_map/pallas_call | solution.py:333
  121.2 2.3 collective-permute-start.43
  128.0 1.7 collective-permute-start.46
  130.8 1.7 collective-permute-start.44
  136.2 3.1 %collective-permute-start.47 = (bf16[2,384,512]{2,1,0:T(8,128)(2,1)S(1)}, bf16[2,384,512]{2,1,0:T(8,128)(2,1)S(1)}, u32[]{:S(2)}, u32[]{:S(2)}) collective-permute-start(bf16[2,384,512]{2,1,0:T(8,128)(2,1)S(1)} %get-tuple-element.137), channel_id=1, source_target_pairs={{0,1},{1,2},{2,3},{3,4},{4,5},{5,6},{6,7},{8,9},{9,10},{10,11},{11... | collective-permute-start | bytes 2359304 | tf_op jit(solution)/shard_map/ppermute | solution.py:774
  139.3 10.4 %shard_map.361 = (bf16[2,384,2048]{2,1,0:T(8,128)(2,1)}, bf16[2,384,2048]{2,1,0:T(8,128)(2,1)S(1)}, f32[2,2,2048]{2,1,0:T(2,128)S(1)}) custom-call(f32[2]{0:T(128)S(1)} %convert_divide_fusion.inv_ref, f32[2,2,2048]{2,1,0:T(2,128)S(1)} %add_add_fusion.2.sums_ref.stats3_ref, f32[2,2048]{1,0:T(2,128)S(1)} %slice.173.param_ref.param3_ref, ...), custom_call_target="tpu_custom_call" | custom-call | flops 62914560 | bytes 25165824 | tf_op jit(solution)/shard_map/pallas_call | solution.py:333
  157.9 2.0 collective-permute-start.55
  165.1 5.5 %shard_map.362 = (bf16[2,384,2048]{2,1,0:T(8,128)(2,1)S(1)}, f32[2,384,512]{2,1,0:T(8,128)S(1)}, bf16[2,384,512]{2,1,0:T(8,128)(2,1)S(1)}, f32[2,2,512]{2,1,0:T(2,128)S(1)}) custom-call(f32[2]{0:T(128)S(1)} %convert_divide_fusion.inv_ref, f32[2,2,2048]{2,1,0:T(2,128)S(1)} %add_add_fusion.2.sums_ref.stats3_ref, f32[2,2,2048]{2,1,0:T(2,128)S(1)} %add_add_fusion.grads3_ref, ...), custom_call_target="tpu_custom_call" | custom-call | flops 1610612736 | bytes 15728640 | tf_op jit(solution)/shard_map/pallas_call | solution.py:333
  172.2 3.1 %collective-permute-start.63 = (bf16[2,384,512]{2,1,0:T(8,128)(2,1)S(1)}, bf16[2,384,512]{2,1,0:T(8,128)(2,1)S(1)}, u32[]{:S(2)}, u32[]{:S(2)}) collective-permute-start(bf16[2,384,512]{2,1,0:T(8,128)(2,1)S(1)} %get-tuple-element.144), channel_id=1, source_target_pairs={{0,1},{1,2},{2,3},{3,4},{4,5},{5,6},{6,7},{8,9},{9,10},{10,11},{11... | collective-permute-start | bytes 2359304 | tf_op jit(solution)/shard_map/ppermute | solution.py:774
  177.1 2.1 collective-permute-start.59
  183.4 1.9 collective-permute-start.62
  190.0 2.6 shard_map.363
  192.6 8.1 %shard_map.364 = (bf16[16,208,512]{2,1,0:T(8,128)(2,1)S(1)}, bf16[16,208,512]{2,1,0:T(8,128)(2,1)S(1)}) custom-call(bf16[3,768,512]{2,1,0:T(8,128)(2,1)S(1)} %bitcast.136, bf16[768,1536]{1,0:T(8,128)(2,1)S(1)} %bitcast.135, bf16[768,2048]{1,0:T(8,128)(2,1)S(1)} %bitcast.134, bf16[768,512]{1,0:T(8,128)(2,1)S(1)} %bitcast.137, s32[16]{0:T(128)S(1)} %fusion.22.place_ref, ...), custom_call_target="tpu_custom_call" | custom-call | flops 5234491392 | bytes 9437184 | tf_op jit(solution)/shard_map/pallas_call | solution.py:333
  200.8 6.1 %shard_map.365 = (f32[2,384,512]{2,1,0:T(8,128)S(1)}, f32[2,2,512]{2,1,0:T(2,128)S(1)}) custom-call(f32[2]{0:T(128)S(1)} %convert_divide_fusion.inv_ref, f32[2,4,512]{2,1,0:T(4,128)S(1)} %bitcast.130, f32[2,512]{1,0:T(2,128)S(1)} %get-tuple-element.258.param_ref.param1_ref, bf16[2,384,1536]{2,1,0:T(8,128)(2,1)S(1)} %get-tuple-element.145.cat_ref, ...), custom_call_target="tpu_custom_call" | custom-call | flops 3623878656 | bytes 16515072 | tf_op jit(solution)/shard_map/pallas_call | solution.py:333
  217.6 1.9 collective-permute-start.72
  224.2 4.0 %shard_map.366 = (bf16[2,384,512]{2,1,0:T(8,128)(2,1)S(1)}, bf16[16,64,512]{2,1,0:T(8,128)(2,1)S(1)}, bf16[16,64,512]{2,1,0:T(8,128)(2,1)S(1)}) custom-call(f32[2]{0:T(128)S(1)} %convert_divide_fusion.inv_ref, f32[2,4,512]{2,1,0:T(4,128)S(1)} %bitcast.131, f32[2,2,512]{2,1,0:T(2,128)S(1)} %add_add_fusion.6.grads_ref, ...), custom_call_target="tpu_custom_call" | custom-call | flops 1610612736 | bytes 6291456 | tf_op jit(solution)/shard_map/pallas_call | solution.py:333
  228.2 6.4 %collective-permute-done.73 = bf16[2,2,208,512]{3,2,1,0:T(8,128)(2,1)S(1)} collective-permute-done((bf16[2,2,208,512]{3,2,1,0:T(8,128)(2,1)S(1)}, bf16[2,2,208,512]{3,2,1,0:T(8,128)(2,1)S(1)}, u32[]{:S(2)}, u32[]{:S(2)}) %collective-permute-start.73) | collective-permute-done | bytes 852000 | tf_op jit(solution)/shard_map/ppermute | solution.py:29
  238.0 4.3 %shard_map.367 = bf16[768,2048]{1,0:T(8,128)(2,1)} custom-call(bf16[768,512]{1,0:T(8,128)(2,1)S(1)} %bitcast.127, bf16[2048,512]{1,0:T(8,128)(2,1)S(1)} %get-tuple-element.164.w_ref, bf16[768,2048]{1,0:T(8,128)(2,1)S(1)} %bitcast.119), custom_call_target="tpu_custom_call" | custom-call | flops 1610612736 | bytes 12582912 | tf_op jit(solution)/shard_map/pallas_call | solution.py:333
  242.3 5.6 %collective-permute-done.75 = bf16[2,208,512]{2,1,0:T(8,128)(2,1)S(1)} collective-permute-done((bf16[2,208,512]{2,1,0:T(8,128)(2,1)S(1)}, bf16[2,208,512]{2,1,0:T(8,128)(2,1)S(1)}, u32[]{:S(2)}, u32[]{:S(2)}) %collective-permute-start.75) | collective-permute-done | bytes 426016 | tf_op jit(solution)/shard_map/ppermute | solution.py:29
  252.2 2.0 collective-permute-start.79
  254.7 9.0 %collective-permute-done.79 = bf16[1,208,512]{2,1,0:T(8,128)(2,1)S(1)} collective-permute-done((bf16[1,208,512]{2,1,0:T(8,128)(2,1)S(1)}, bf16[1,208,512]{2,1,0:T(8,128)(2,1)S(1)}, u32[]{:S(2)}, u32[]{:S(2)}) %collective-permute-start.79) | collective-permute-done | bytes 213024 | tf_op jit(solution)/shard_map/ppermute | solution.py:29
  264.4 4.5 %collective-permute-done.82 = bf16[2,64,512]{2,1,0:T(8,128)(2,1)S(1)} collective-permute-done((bf16[2,64,512]{2,1,0:T(8,128)(2,1)S(1)}, bf16[2,64,512]{2,1,0:T(8,128)(2,1)S(1)}, u32[]{:S(2)}, u32[]{:S(2)}) %collective-permute-start.82) | collective-permute-done | bytes 131104 | tf_op jit(solution)/shard_map/ppermute | solution.py:29
  269.9 2.0 collective-permute-start.87
  272.1 2.0 collective-permute-done.84
  275.8 1.9 collective-permute-start.86
  279.5 4.1 %collective-permute-done.85 = bf16[1,64,512]{2,1,0:T(8,128)(2,1)S(1)} collective-permute-done((bf16[1,64,512]{2,1,0:T(8,128)(2,1)S(1)}, bf16[1,64,512]{2,1,0:T(8,128)(2,1)S(1)}, u32[]{:S(2)}, u32[]{:S(2)}) %collective-permute-start.85) | collective-permute-done | bytes 65568 | tf_op jit(solution)/shard_map/ppermute | solution.py:29
  291.3 2.0 collective-permute-start.94
  294.0 1.7 collective-permute-start.92
  (294 shorter events, 126.6 us)
Async XLA Ops:
  2.5 17.9 %collective-permute-start.2 = (bf16[1,128,512]{2,1,0:T(8,128)(2,1)S(1)}, bf16[1,128,512]{2,1,0:T(8,128)(2,1)S(1)}, u32[]{:S(2)}, u32[]{:S(2)}) collective-permute-start(bf16[1,128,512]{2,1,0:T(8,128)(2,1)S(1)} %maximum_bitcast_fusion.refs_0_), channel_id=1, source_target_pairs={{0,6},{1,7},{2,4},{3,5},{4,2},{5,3},{6,0},{7,1},{8,14},{9,15},{10,... | collective-permute-start | bytes 393224 | tf_op jit(solution)/shard_map/ppermute | solution.py:29
  7.6 12.8 %collective-permute-start.1 = (bf16[1,128,512]{2,1,0:T(8,128)(2,1)S(1)}, bf16[1,128,512]{2,1,0:T(8,128)(2,1)S(1)}, u32[]{:S(2)}, u32[]{:S(2)}) collective-permute-start(bf16[1,128,512]{2,1,0:T(8,128)(2,1)S(1)} %maximum_bitcast_fusion.refs_0_), channel_id=1, source_target_pairs={{0,4},{1,5},{2,6},{3,7},{4,0},{5,1},{6,2},{7,3},{8,12},{9,13},{10,... | collective-permute-start | bytes 393224 | tf_op jit(solution)/shard_map/ppermute | solution.py:29
  7.6 12.8 %collective-permute-start = (bf16[1,128,512]{2,1,0:T(8,128)(2,1)S(1)}, bf16[1,128,512]{2,1,0:T(8,128)(2,1)S(1)}, u32[]{:S(2)}, u32[]{:S(2)}) collective-permute-start(bf16[1,128,512]{2,1,0:T(8,128)(2,1)S(1)} %maximum_bitcast_fusion.refs_0_), channel_id=1, source_target_pairs={{0,2},{1,3},{2,0},{3,1},{4,6},{5,7},{6,4},{7,5},{8,10},{9,11},{10,... | collective-permute-start | bytes 393224 | tf_op jit(solution)/shard_map/ppermute | solution.py:29
  23.7 13.3 %collective-permute-start.8 = (bf16[4,128,512]{2,1,0:T(8,128)(2,1)}, bf16[4,128,512]{2,1,0:T(8,128)(2,1)S(1)}, u32[]{:S(2)}, u32[]{:S(2)}) collective-permute-start(bf16[4,128,512]{2,1,0:T(8,128)(2,1)} %shard_map.354.refs_1_), channel_id=1, source_target_pairs={{0,16},{8,24},{16,0},{24,8},{1,17},{9,25},{17,1},{25,9},{2,18},{10... | collective-permute-start | bytes 1572872 | tf_op jit(solution)/shard_map/ppermute | solution.py:29
  25.4 13.9 %collective-permute-start.6 = (bf16[4,128,512]{2,1,0:T(8,128)(2,1)}, bf16[4,128,512]{2,1,0:T(8,128)(2,1)S(1)}, u32[]{:S(2)}, u32[]{:S(2)}) collective-permute-start(bf16[4,128,512]{2,1,0:T(8,128)(2,1)} %shard_map.354.refs_1_), channel_id=1, source_target_pairs={{0,8},{8,0},{16,24},{24,16},{1,9},{9,1},{17,25},{25,17},{2,10},{10... | collective-permute-start | bytes 1572872 | tf_op jit(solution)/shard_map/ppermute | solution.py:29
  26.9 14.6 %collective-permute-start.5 = (bf16[1,144,512]{2,1,0:T(8,128)(2,1)}, bf16[1,144,512]{2,1,0:T(8,128)(2,1)}, u32[]{:S(2)}, u32[]{:S(2)}) collective-permute-start(bf16[1,144,512]{2,1,0:T(8,128)(2,1)} %bitcast.5.refs_0_), channel_id=1, source_target_pairs={{0,6},{1,7},{2,4},{3,5},{4,2},{5,3},{6,0},{7,1},{8,14},{9,15},{10,... | collective-permute-start | bytes 442376 | tf_op jit(solution)/shard_map/ppermute | solution.py:29
  30.5 11.3 %collective-permute-start.4 = (bf16[1,144,512]{2,1,0:T(8,128)(2,1)}, bf16[1,144,512]{2,1,0:T(8,128)(2,1)}, u32[]{:S(2)}, u32[]{:S(2)}) collective-permute-start(bf16[1,144,512]{2,1,0:T(8,128)(2,1)} %bitcast.5.refs_0_), channel_id=1, source_target_pairs={{0,4},{1,5},{2,6},{3,7},{4,0},{5,1},{6,2},{7,3},{8,12},{9,13},{10,... | collective-permute-start | bytes 442376 | tf_op jit(solution)/shard_map/ppermute | solution.py:29
  30.5 11.5 %collective-permute-start.3 = (bf16[1,144,512]{2,1,0:T(8,128)(2,1)}, bf16[1,144,512]{2,1,0:T(8,128)(2,1)}, u32[]{:S(2)}, u32[]{:S(2)}) collective-permute-start(bf16[1,144,512]{2,1,0:T(8,128)(2,1)} %bitcast.5.refs_0_), channel_id=1, source_target_pairs={{0,2},{1,3},{2,0},{3,1},{4,6},{5,7},{6,4},{7,5},{8,10},{9,11},{10,... | collective-permute-start | bytes 442376 | tf_op jit(solution)/shard_map/ppermute | solution.py:29
  37.7 6.9 %collective-permute-start.9 = (bf16[2,128,512]{2,1,0:T(8,128)(2,1)}, bf16[2,128,512]{2,1,0:T(8,128)(2,1)S(1)}, u32[]{:S(2)}, u32[]{:S(2)}) collective-permute-start(bf16[2,128,512]{2,1,0:T(8,128)(2,1)} %slice.217), channel_id=1, source_target_pairs={{0,8},{8,0},{16,24},{24,16},{1,9},{9,1},{17,25},{25,17},{2,10},{10... | collective-permute-start | bytes 786440 | tf_op jit(solution)/shard_map/ppermute | solution.py:29
  39.9 6.7 %collective-permute-start.7 = (bf16[2,128,512]{2,1,0:T(8,128)(2,1)}, bf16[2,128,512]{2,1,0:T(8,128)(2,1)}, u32[]{:S(2)}, u32[]{:S(2)}) collective-permute-start(bf16[2,128,512]{2,1,0:T(8,128)(2,1)} %slice.216), channel_id=1, source_target_pairs={{0,16},{8,24},{16,0},{24,8},{1,17},{9,25},{17,1},{25,9},{2,18},{10... | collective-permute-start | bytes 786440 | tf_op jit(solution)/shard_map/ppermute | solution.py:29
  41.5 7.9 %collective-permute-start.10 = (bf16[4,128,512]{2,1,0:T(8,128)(2,1)}, bf16[4,128,512]{2,1,0:T(8,128)(2,1)S(1)}, u32[]{:S(2)}, u32[]{:S(2)}) collective-permute-start(bf16[4,128,512]{2,1,0:T(8,128)(2,1)} %shard_map.354.refs_1_), channel_id=1, source_target_pairs={{0,1},{1,0},{2,3},{3,2},{4,5},{5,4},{6,7},{7,6},{8,9},{9,8},{10,11... | collective-permute-start | bytes 1572872 | tf_op jit(solution)/shard_map/ppermute | solution.py:29
  41.8 7.5 %collective-permute-start.12 = (bf16[4,128,512]{2,1,0:T(8,128)(2,1)S(1)}, bf16[4,128,512]{2,1,0:T(8,128)(2,1)}, u32[]{:S(2)}, u32[]{:S(2)}) collective-permute-start(bf16[4,128,512]{2,1,0:T(8,128)(2,1)S(1)} %collective-permute-done.8.refs_5_), channel_id=1, source_target_pairs={{0,1},{1,0},{2,3},{3,2},{4,5},{5,4},{6,7},{7,6},{8,9},{9,8},{10,11... | collective-permute-start | bytes 1572872 | tf_op jit(solution)/shard_map/ppermute | solution.py:29
  42.0 7.3 %collective-permute-start.11 = (bf16[4,128,512]{2,1,0:T(8,128)(2,1)S(1)}, bf16[4,128,512]{2,1,0:T(8,128)(2,1)}, u32[]{:S(2)}, u32[]{:S(2)}) collective-permute-start(bf16[4,128,512]{2,1,0:T(8,128)(2,1)S(1)} %collective-permute-done.6.refs_3_), channel_id=1, source_target_pairs={{0,1},{1,0},{2,3},{3,2},{4,5},{5,4},{6,7},{7,6},{8,9},{9,8},{10,11... | collective-permute-start | bytes 1572872 | tf_op jit(solution)/shard_map/ppermute | solution.py:29
  49.4 16.0 %collective-permute-start.17 = (bf16[4,144,512]{2,1,0:T(8,128)(2,1)}, bf16[4,144,512]{2,1,0:T(8,128)(2,1)S(1)}, u32[]{:S(2)}, u32[]{:S(2)}) collective-permute-start(bf16[4,144,512]{2,1,0:T(8,128)(2,1)} %shard_map.355.refs_1_), channel_id=1, source_target_pairs={{0,16},{8,24},{16,0},{24,8},{1,17},{9,25},{17,1},{25,9},{2,18},{10... | collective-permute-start | bytes 1769480 | tf_op jit(solution)/shard_map/ppermute | solution.py:29
  50.9 15.7 %collective-permute-start.16 = (bf16[4,144,512]{2,1,0:T(8,128)(2,1)}, bf16[4,144,512]{2,1,0:T(8,128)(2,1)S(1)}, u32[]{:S(2)}, u32[]{:S(2)}) collective-permute-start(bf16[4,144,512]{2,1,0:T(8,128)(2,1)} %shard_map.355.refs_1_), channel_id=1, source_target_pairs={{0,8},{8,0},{16,24},{24,16},{1,9},{9,1},{17,25},{25,17},{2,10},{10... | collective-permute-start | bytes 1769480 | tf_op jit(solution)/shard_map/ppermute | solution.py:29
  57.5 14.9 %collective-permute-start.22 = (bf16[2,384,512]{2,1,0:T(8,128)(2,1)S(1)}, bf16[2,384,512]{2,1,0:T(8,128)(2,1)S(1)}, u32[]{:S(2)}, u32[]{:S(2)}) collective-permute-start(bf16[2,384,512]{2,1,0:T(8,128)(2,1)S(1)} %get-tuple-element.116), channel_id=1, source_target_pairs={{1,0},{2,1},{3,2},{4,3},{5,4},{6,5},{7,6},{9,8},{10,9},{11,10},{12... | collective-permute-start | bytes 2359304 | tf_op jit(solution)/shard_map/ppermute | solution.py:775
  58.8 13.6 %collective-permute-start.21 = (bf16[2,384,512]{2,1,0:T(8,128)(2,1)S(1)}, bf16[2,384,512]{2,1,0:T(8,128)(2,1)S(1)}, u32[]{:S(2)}, u32[]{:S(2)}) collective-permute-start(bf16[2,384,512]{2,1,0:T(8,128)(2,1)S(1)} %get-tuple-element.116), channel_id=1, source_target_pairs={{0,1},{1,2},{2,3},{3,4},{4,5},{5,6},{6,7},{8,9},{9,10},{10,11},{11... | collective-permute-start | bytes 2359304 | tf_op jit(solution)/shard_map/ppermute | solution.py:774
  72.4 6.7 %collective-permute-start.25 = (f32[2,4,512]{2,1,0:T(4,128)S(1)}, f32[2,4,512]{2,1,0:T(4,128)S(1)}, u32[]{:S(2)}, u32[]{:S(2)}) collective-permute-start(f32[2,4,512]{2,1,0:T(4,128)S(1)} %bitcast.146), channel_id=1, source_target_pairs={{0,6},{1,7},{2,4},{3,5},{4,2},{5,3},{6,0},{7,1},{8,14},{9,15},{10,... | collective-permute-start | bytes 49160 | tf_op jit(solution)/shard_map/ppermute | solution.py:29
  76.9 11.3 %collective-permute-start.30 = (bf16[2,144,512]{2,1,0:T(8,128)(2,1)S(1)}, bf16[2,144,512]{2,1,0:T(8,128)(2,1)S(1)}, u32[]{:S(2)}, u32[]{:S(2)}) collective-permute-start(bf16[2,144,512]{2,1,0:T(8,128)(2,1)S(1)} %slice.171), channel_id=1, source_target_pairs={{0,8},{8,0},{16,24},{24,16},{1,9},{9,1},{17,25},{25,17},{2,10},{10... | collective-permute-start | bytes 884744 | tf_op jit(solution)/shard_map/ppermute | solution.py:29
  78.4 9.8 %collective-permute-start.29 = (bf16[2,144,512]{2,1,0:T(8,128)(2,1)S(1)}, bf16[2,144,512]{2,1,0:T(8,128)(2,1)S(1)}, u32[]{:S(2)}, u32[]{:S(2)}) collective-permute-start(bf16[2,144,512]{2,1,0:T(8,128)(2,1)S(1)} %slice.170), channel_id=1, source_target_pairs={{0,16},{8,24},{16,0},{24,8},{1,17},{9,25},{17,1},{25,9},{2,18},{10... | collective-permute-start | bytes 884744 | tf_op jit(solution)/shard_map/ppermute | solution.py:29
  79.1 9.8 %collective-permute-start.26 = (bf16[4,144,512]{2,1,0:T(8,128)(2,1)S(1)}, bf16[4,144,512]{2,1,0:T(8,128)(2,1)S(1)}, u32[]{:S(2)}, u32[]{:S(2)}) collective-permute-start(bf16[4,144,512]{2,1,0:T(8,128)(2,1)S(1)} %copy-done.5), channel_id=1, source_target_pairs={{0,1},{1,0},{2,3},{3,2},{4,5},{5,4},{6,7},{7,6},{8,9},{9,8},{10,11... | collective-permute-start | bytes 1769480 | tf_op jit(solution)/shard_map/ppermute | solution.py:29
  80.8 9.5 %collective-permute-start.27 = (bf16[4,144,512]{2,1,0:T(8,128)(2,1)S(1)}, bf16[4,144,512]{2,1,0:T(8,128)(2,1)S(1)}, u32[]{:S(2)}, u32[]{:S(2)}) collective-permute-start(bf16[4,144,512]{2,1,0:T(8,128)(2,1)S(1)} %collective-permute-done.16.refs_3_), channel_id=1, source_target_pairs={{0,1},{1,0},{2,3},{3,2},{4,5},{5,4},{6,7},{7,6},{8,9},{9,8},{10,11... | collective-permute-start | bytes 1769480 | tf_op jit(solution)/shard_map/ppermute | solution.py:29
  80.8 9.5 %collective-permute-start.28 = (bf16[4,144,512]{2,1,0:T(8,128)(2,1)S(1)}, bf16[4,144,512]{2,1,0:T(8,128)(2,1)S(1)}, u32[]{:S(2)}, u32[]{:S(2)}) collective-permute-start(bf16[4,144,512]{2,1,0:T(8,128)(2,1)S(1)} %collective-permute-done.17.refs_5_), channel_id=1, source_target_pairs={{0,1},{1,0},{2,3},{3,2},{4,5},{5,4},{6,7},{7,6},{8,9},{9,8},{10,11... | collective-permute-start | bytes 1769480 | tf_op jit(solution)/shard_map/ppermute | solution.py:29
  107.5 6.0 %collective-permute-start.39 = (f32[2,2,512]{2,1,0:T(2,128)S(1)}, f32[2,2,512]{2,1,0:T(2,128)S(1)}, u32[]{:S(2)}, u32[]{:S(2)}) collective-permute-start(f32[2,2,512]{2,1,0:T(2,128)S(1)} %add_add_fusion.11), channel_id=1, source_target_pairs={{0,6},{1,7},{2,4},{3,5},{4,2},{5,3},{6,0},{7,1},{8,14},{9,15},{10,... | collective-permute-start | bytes 24584 | tf_op jit(solution)/shard_map/ppermute | solution.py:29
  128.0 5.8 %collective-permute-start.46 = (f32[2,2,2048]{2,1,0:T(2,128)S(1)}, f32[2,2,2048]{2,1,0:T(2,128)S(1)}, u32[]{:S(2)}, u32[]{:S(2)}) collective-permute-start(f32[2,2,2048]{2,1,0:T(2,128)S(1)} %add_add_fusion.3), channel_id=1, source_target_pairs={{0,6},{1,7},{2,4},{3,5},{4,2},{5,3},{6,0},{7,1},{8,14},{9,15},{10,... | collective-permute-start | bytes 98312 | tf_op jit(solution)/shard_map/ppermute | solution.py:29
  134.9 14.8 %collective-permute-start.48 = (bf16[2,384,512]{2,1,0:T(8,128)(2,1)S(1)}, bf16[2,384,512]{2,1,0:T(8,128)(2,1)S(1)}, u32[]{:S(2)}, u32[]{:S(2)}) collective-permute-start(bf16[2,384,512]{2,1,0:T(8,128)(2,1)S(1)} %get-tuple-element.137), channel_id=1, source_target_pairs={{1,0},{2,1},{3,2},{4,3},{5,4},{6,5},{7,6},{9,8},{10,9},{11,10},{12... | collective-permute-start | bytes 2359304 | tf_op jit(solution)/shard_map/ppermute | solution.py:775
  136.2 13.5 %collective-permute-start.47 = (bf16[2,384,512]{2,1,0:T(8,128)(2,1)S(1)}, bf16[2,384,512]{2,1,0:T(8,128)(2,1)S(1)}, u32[]{:S(2)}, u32[]{:S(2)}) collective-permute-start(bf16[2,384,512]{2,1,0:T(8,128)(2,1)S(1)} %get-tuple-element.137), channel_id=1, source_target_pairs={{0,1},{1,2},{2,3},{3,4},{4,5},{5,6},{6,7},{8,9},{9,10},{10,11},{11... | collective-permute-start | bytes 2359304 | tf_op jit(solution)/shard_map/ppermute | solution.py:774
  157.9 6.0 %collective-permute-start.55 = (f32[2,2,2048]{2,1,0:T(2,128)S(1)}, f32[2,2,2048]{2,1,0:T(2,128)S(1)}, u32[]{:S(2)}, u32[]{:S(2)}) collective-permute-start(f32[2,2,2048]{2,1,0:T(2,128)S(1)} %add_add_fusion.1), channel_id=1, source_target_pairs={{0,6},{1,7},{2,4},{3,5},{4,2},{5,3},{6,0},{7,1},{8,14},{9,15},{10,... | collective-permute-start | bytes 98312 | tf_op jit(solution)/shard_map/ppermute | solution.py:29
  159.9 5.2 %collective-permute-start.54 = (f32[2,2,2048]{2,1,0:T(2,128)S(1)}, f32[2,2,2048]{2,1,0:T(2,128)S(1)}, u32[]{:S(2)}, u32[]{:S(2)}) collective-permute-start(f32[2,2,2048]{2,1,0:T(2,128)S(1)} %add_add_fusion.1), channel_id=1, source_target_pairs={{0,4},{1,5},{2,6},{3,7},{4,0},{5,1},{6,2},{7,3},{8,12},{9,13},{10,... | collective-permute-start | bytes 98312 | tf_op jit(solution)/shard_map/ppermute | solution.py:29
  170.7 19.3 %collective-permute-start.64 = (bf16[2,384,512]{2,1,0:T(8,128)(2,1)S(1)}, bf16[2,384,512]{2,1,0:T(8,128)(2,1)S(1)}, u32[]{:S(2)}, u32[]{:S(2)}) collective-permute-start(bf16[2,384,512]{2,1,0:T(8,128)(2,1)S(1)} %get-tuple-element.144), channel_id=1, source_target_pairs={{1,0},{2,1},{3,2},{4,3},{5,4},{6,5},{7,6},{9,8},{10,9},{11,10},{12... | collective-permute-start | bytes 2359304 | tf_op jit(solution)/shard_map/ppermute | solution.py:775
  172.2 17.8 %collective-permute-start.63 = (bf16[2,384,512]{2,1,0:T(8,128)(2,1)S(1)}, bf16[2,384,512]{2,1,0:T(8,128)(2,1)S(1)}, u32[]{:S(2)}, u32[]{:S(2)}) collective-permute-start(bf16[2,384,512]{2,1,0:T(8,128)(2,1)S(1)} %get-tuple-element.144), channel_id=1, source_target_pairs={{0,1},{1,2},{2,3},{3,4},{4,5},{5,6},{6,7},{8,9},{9,10},{10,11},{11... | collective-permute-start | bytes 2359304 | tf_op jit(solution)/shard_map/ppermute | solution.py:774
  183.4 5.5 %collective-permute-start.62 = (f32[2,2,512]{2,1,0:T(2,128)S(1)}, f32[2,2,512]{2,1,0:T(2,128)S(1)}, u32[]{:S(2)}, u32[]{:S(2)}) collective-permute-start(f32[2,2,512]{2,1,0:T(2,128)S(1)} %add_add_fusion.9), channel_id=1, source_target_pairs={{0,6},{1,7},{2,4},{3,5},{4,2},{5,3},{6,0},{7,1},{8,14},{9,15},{10,... | collective-permute-start | bytes 24584 | tf_op jit(solution)/shard_map/ppermute | solution.py:29
  200.7 13.8 %collective-permute-start.69 = (bf16[16,208,512]{2,1,0:T(8,128)(2,1)S(1)}, bf16[16,208,512]{2,1,0:T(8,128)(2,1)S(1)}, u32[]{:S(2)}, u32[]{:S(2)}) collective-permute-start(bf16[16,208,512]{2,1,0:T(8,128)(2,1)S(1)} %get-tuple-element.150.refs_11_), channel_id=1, source_target_pairs={{0,1},{1,0},{2,3},{3,2},{4,5},{5,4},{6,7},{7,6},{8,9},{9,8},{10,11... | collective-permute-start | bytes 10223624 | tf_op jit(solution)/shard_map/ppermute | solution.py:29
  215.0 19.6 %collective-permute-start.73 = (bf16[2,2,208,512]{3,2,1,0:T(8,128)(2,1)S(1)}, bf16[2,2,208,512]{3,2,1,0:T(8,128)(2,1)S(1)}, u32[]{:S(2)}, u32[]{:S(2)}) collective-permute-start(bf16[2,2,208,512]{3,2,1,0:T(8,128)(2,1)S(1)} %get-tuple-element.158), channel_id=1, source_target_pairs={{0,8},{8,0},{16,24},{24,16},{1,9},{9,1},{17,25},{25,17},{2,10},{10... | collective-permute-start | bytes 2555912 | tf_op jit(solution)/shard_map/ppermute | solution.py:29
  216.0 19.2 %collective-permute-start.74 = (bf16[2,2,208,512]{3,2,1,0:T(8,128)(2,1)S(1)}, bf16[2,2,208,512]{3,2,1,0:T(8,128)(2,1)S(1)}, u32[]{:S(2)}, u32[]{:S(2)}) collective-permute-start(bf16[2,2,208,512]{3,2,1,0:T(8,128)(2,1)S(1)} %get-tuple-element.159), channel_id=1, source_target_pairs={{0,16},{8,24},{16,0},{24,8},{1,17},{9,25},{17,1},{25,9},{2,18},{10... | collective-permute-start | bytes 2555912 | tf_op jit(solution)/shard_map/ppermute | solution.py:29
  217.6 5.4 %collective-permute-start.72 = (f32[2,2,512]{2,1,0:T(2,128)S(1)}, f32[2,2,512]{2,1,0:T(2,128)S(1)}, u32[]{:S(2)}, u32[]{:S(2)}) collective-permute-start(f32[2,2,512]{2,1,0:T(2,128)S(1)} %add_add_fusion.7), channel_id=1, source_target_pairs={{0,6},{1,7},{2,4},{3,5},{4,2},{5,3},{6,0},{7,1},{8,14},{9,15},{10,... | collective-permute-start | bytes 24584 | tf_op jit(solution)/shard_map/ppermute | solution.py:29
  235.2 14.1 %collective-permute-start.77 = (bf16[16,64,512]{2,1,0:T(8,128)(2,1)S(1)}, bf16[16,64,512]{2,1,0:T(8,128)(2,1)S(1)}, u32[]{:S(2)}, u32[]{:S(2)}) collective-permute-start(bf16[16,64,512]{2,1,0:T(8,128)(2,1)S(1)} %get-tuple-element.169), channel_id=1, source_target_pairs={{0,1},{1,0},{2,3},{3,2},{4,5},{5,4},{6,7},{7,6},{8,9},{9,8},{10,11... | collective-permute-start | bytes 3145736 | tf_op jit(solution)/shard_map/ppermute | solution.py:29
  235.6 12.3 %collective-permute-start.75 = (bf16[2,208,512]{2,1,0:T(8,128)(2,1)S(1)}, bf16[2,208,512]{2,1,0:T(8,128)(2,1)S(1)}, u32[]{:S(2)}, u32[]{:S(2)}) collective-permute-start(bf16[2,208,512]{2,1,0:T(8,128)(2,1)S(1)} %get-tuple-element.165), channel_id=1, source_target_pairs={{0,8},{8,0},{16,24},{24,16},{1,9},{9,1},{17,25},{25,17},{2,10},{10... | collective-permute-start | bytes 1277960 | tf_op jit(solution)/shard_map/ppermute | solution.py:29
  236.7 11.9 %collective-permute-start.76 = (bf16[2,208,512]{2,1,0:T(8,128)(2,1)S(1)}, bf16[2,208,512]{2,1,0:T(8,128)(2,1)S(1)}, u32[]{:S(2)}, u32[]{:S(2)}) collective-permute-start(bf16[2,208,512]{2,1,0:T(8,128)(2,1)S(1)} %get-tuple-element.166), channel_id=1, source_target_pairs={{0,16},{8,24},{16,0},{24,8},{1,17},{9,25},{17,1},{25,9},{2,18},{10... | collective-permute-start | bytes 1277960 | tf_op jit(solution)/shard_map/ppermute | solution.py:29
  249.4 14.3 %collective-permute-start.80 = (bf16[2,2,64,512]{3,2,1,0:T(8,128)(2,1)S(1)}, bf16[2,2,64,512]{3,2,1,0:T(8,128)(2,1)S(1)}, u32[]{:S(2)}, u32[]{:S(2)}) collective-permute-start(bf16[2,2,64,512]{3,2,1,0:T(8,128)(2,1)S(1)} %get-tuple-element.173), channel_id=1, source_target_pairs={{0,8},{8,0},{16,24},{24,16},{1,9},{9,1},{17,25},{25,17},{2,10},{10... | collective-permute-start | bytes 786440 | tf_op jit(solution)/shard_map/ppermute | solution.py:29
  250.4 13.3 %collective-permute-start.81 = (bf16[2,2,64,512]{3,2,1,0:T(8,128)(2,1)S(1)}, bf16[2,2,64,512]{3,2,1,0:T(8,128)(2,1)S(1)}, u32[]{:S(2)}, u32[]{:S(2)}) collective-permute-start(bf16[2,2,64,512]{3,2,1,0:T(8,128)(2,1)S(1)} %get-tuple-element.174), channel_id=1, source_target_pairs={{0,16},{8,24},{16,0},{24,8},{1,17},{9,25},{17,1},{25,9},{2,18},{10... | collective-permute-start | bytes 786440 | tf_op jit(solution)/shard_map/ppermute | solution.py:29
  252.2 11.5 %collective-permute-start.79 = (bf16[1,208,512]{2,1,0:T(8,128)(2,1)S(1)}, bf16[1,208,512]{2,1,0:T(8,128)(2,1)S(1)}, u32[]{:S(2)}, u32[]{:S(2)}) collective-permute-start(bf16[1,208,512]{2,1,0:T(8,128)(2,1)S(1)} %get-tuple-element.253), channel_id=1, source_target_pairs={{0,4},{1,5},{2,6},{3,7},{4,0},{5,1},{6,2},{7,3},{8,12},{9,13},{10,... | collective-permute-start | bytes 638984 | tf_op jit(solution)/shard_map/ppermute | solution.py:29
  254.1 9.6 %collective-permute-start.78 = (bf16[1,208,512]{2,1,0:T(8,128)(2,1)S(1)}, bf16[1,208,512]{2,1,0:T(8,128)(2,1)S(1)}, u32[]{:S(2)}, u32[]{:S(2)}) collective-permute-start(bf16[1,208,512]{2,1,0:T(8,128)(2,1)S(1)} %get-tuple-element.254), channel_id=1, source_target_pairs={{0,2},{1,3},{2,0},{3,1},{4,6},{5,7},{6,4},{7,5},{8,10},{9,11},{10,... | collective-permute-start | bytes 638984 | tf_op jit(solution)/shard_map/ppermute | solution.py:29
  269.9 8.8 %collective-permute-start.87 = (bf16[1,208,512]{2,1,0:T(8,128)(2,1)S(1)}, bf16[1,208,512]{2,1,0:T(8,128)(2,1)S(1)}, u32[]{:S(2)}, u32[]{:S(2)}) collective-permute-start(bf16[1,208,512]{2,1,0:T(8,128)(2,1)S(1)} %get-tuple-element.252), channel_id=1, source_target_pairs={{0,6},{1,7},{2,4},{3,5},{4,2},{5,3},{6,0},{7,1},{8,14},{9,15},{10,... | collective-permute-start | bytes 638984 | tf_op jit(solution)/shard_map/ppermute | solution.py:29
  271.9 7.6 %collective-permute-start.83 = (bf16[1,64,512]{2,1,0:T(8,128)(2,1)S(1)}, bf16[1,64,512]{2,1,0:T(8,128)(2,1)S(1)}, u32[]{:S(2)}, u32[]{:S(2)}) collective-permute-start(bf16[1,64,512]{2,1,0:T(8,128)(2,1)S(1)} %slice.304), channel_id=1, source_target_pairs={{0,2},{1,3},{2,0},{3,1},{4,6},{5,7},{6,4},{7,5},{8,10},{9,11},{10,... | collective-permute-start | bytes 196616 | tf_op jit(solution)/shard_map/ppermute | solution.py:29
  274.1 9.5 %collective-permute-start.85 = (bf16[1,64,512]{2,1,0:T(8,128)(2,1)S(1)}, bf16[1,64,512]{2,1,0:T(8,128)(2,1)S(1)}, u32[]{:S(2)}, u32[]{:S(2)}) collective-permute-start(bf16[1,64,512]{2,1,0:T(8,128)(2,1)S(1)} %get-tuple-element.255), channel_id=1, source_target_pairs={{0,4},{1,5},{2,6},{3,7},{4,0},{5,1},{6,2},{7,3},{8,12},{9,13},{10,... | collective-permute-start | bytes 196616 | tf_op jit(solution)/shard_map/ppermute | solution.py:29
  275.8 7.9 %collective-permute-start.86 = (bf16[1,64,512]{2,1,0:T(8,128)(2,1)S(1)}, bf16[1,64,512]{2,1,0:T(8,128)(2,1)S(1)}, u32[]{:S(2)}, u32[]{:S(2)}) collective-permute-start(bf16[1,64,512]{2,1,0:T(8,128)(2,1)S(1)} %get-tuple-element.256), channel_id=1, source_target_pairs={{0,6},{1,7},{2,4},{3,5},{4,2},{5,3},{6,0},{7,1},{8,14},{9,15},{10,... | collective-permute-start | bytes 196616 | tf_op jit(solution)/shard_map/ppermute | solution.py:29
  291.3 5.4 %collective-permute-start.94 = (f32[4,128]{1,0:T(4,128)S(1)}, f32[4,128]{1,0:T(4,128)S(1)}, u32[]{:S(2)}, u32[]{:S(2)}) collective-permute-start(f32[4,128]{1,0:T(4,128)S(1)} %add_add_fusion.12), channel_id=1, source_target_pairs={{0,6},{1,7},{2,4},{3,5},{4,2},{5,3},{6,0},{7,1},{8,14},{9,15},{10,... | collective-permute-start | bytes 6152 | tf_op jit(solution)/shard_map/ppermute | solution.py:29
  (79 other events, 821.7 us)

commit v3 on v2

--- a/solution.py
+++ b/solution.py
@@ -572,8 +572,9 @@
         centred = a_ref[0, rows, :] - mean
         u = centred * scale + (shift + x_ref[0, rows, :].astype(F32))
         mask = wide(mask_ref[0, 0, rows, :], width)
-        block_ref[0, rows, :] = (softplus(u) * mask).astype(BF16)
-        du = up_ref[0, rows, :].astype(F32) * sigmoid(u)
+        upper = 0.5 * jnp.tanh(0.5 * jnp.abs(u)) + 0.5
+        block_ref[0, rows, :] = ((jnp.maximum(u, 0.0) - jnp.log(upper)) * mask).astype(BF16)
+        du = up_ref[0, rows, :].astype(F32) * jnp.where(u >= 0.0, upper, 1.0 - upper)
         du_ref[0, rows, :] = du.astype(BF16)
         return carry[0] + fold(du), carry[1] + fold(du * centred)
 
@@ -862,7 +863,6 @@
     chip_one = group_sum(core_one, "batch", 0, lax.axis_size("batch"))
     chip_one, a_one_up, a_one_down = in_order(chip_one, a_one_up, a_one_down)
     if direct:
-        chip_one, *from_mid = in_order(chip_one, *from_mid)
         far_mid = gather_mid.far(*from_mid)
     stats_one = line_sums(chip_one)
     upstream = call(

time: 305 us -> 304 us (level)
  transfers between devices with their start and end apart: 95 -> 95, of which waited for: 59 -> 58; matrix products, arithmetic and copies ran while one was open for 3% -> 3% of each run, Pallas kernels for 13% -> 13%
where the time goes in v3:
time: 304 us
  starting transfers between devices  110 us (36%)
  waiting for transfers between devices  90.4 us (30%)
  Pallas kernels  72.4 us (24%)
  local copies, waits for them, and re-layouts  15 us (5%)
  other arithmetic  11.7 us (4%)
  between operations  3.98 us (1%)
    ppermute x89, starting transfers between devices, swap(): lax.ppermute(x, axis, [(i, i ^ mask) for i in range(lax.axis_size(axis))])  96.9 us
    ppermute x89, waiting for transfers between devices, swap(): lax.ppermute(x, axis, [(i, i ^ mask) for i in range(lax.axis_size(axis))])  90.4 us
    pallas_call x14, Pallas kernels, call(): pl.pallas_call(kernel, grid=grid, in_specs=[spec for _, spec in ins], out...  68.5 us
    unnamed x64, local copies, waits for them, and re-layouts  11.3 us
    ppermute x3, starting transfers between devices, neighbours(): above = lax.ppermute(x, 'rows', [(i, i + 1) for i in range(count - 1)])  9.24 us
  transfers between devices with their start and end apart: 95, of which 58 were waited for; matrix products, arithmetic and copies ran while one was open for 3% of the time, Pallas kernels for 13%

profile of v3, /device:TPU:0, one launch (start us, length us, event | category | flops | bytes accessed | tf_op | source)
XLA Modules:
  0.0 303.6 jit_solution(6095745025112886942)
XLA Ops:
  2.5 5.1 %collective-permute-start.2 = (bf16[1,128,512]{2,1,0:T(8,128)(2,1)S(1)}, bf16[1,128,512]{2,1,0:T(8,128)(2,1)S(1)}, u32[]{:S(2)}, u32[]{:S(2)}) collective-permute-start(bf16[1,128,512]{2,1,0:T(8,128)(2,1)S(1)} %maximum_bitcast_fusion.refs_0_), channel_id=1, source_target_pairs={{0,6},{1,7},{2,4},{3,5},{4,2},{5,3},{6,0},{7,1},{8,14},{9,15},{10,... | collective-permute-start | bytes 393224 | tf_op jit(solution)/shard_map/ppermute | solution.py:29
  11.8 3.7 %copy-done = bf16[3,2,1,4,96,2048]{5,4,3,2,1,0:T(8,128)(2,1)S(1)} copy-done((bf16[3,2,1,4,96,2048]{5,4,3,2,1,0:T(8,128)(2,1)S(1)}, bf16[3,2,1,4,96,2048]{5,4,3,2,1,0:T(8,128)(2,1)}, u32[]{:S(2)}) %copy-start) | copy-done | bytes 9437208
  15.5 2.1 shard_map.353.refs_5_
  17.7 2.1 shard_map.352.refs_4_
  21.8 1.9 shard_map.354.refs_1_
  26.9 3.6 %collective-permute-start.5 = (bf16[1,144,512]{2,1,0:T(8,128)(2,1)}, bf16[1,144,512]{2,1,0:T(8,128)(2,1)}, u32[]{:S(2)}, u32[]{:S(2)}) collective-permute-start(bf16[1,144,512]{2,1,0:T(8,128)(2,1)} %bitcast.5.refs_0_), channel_id=1, source_target_pairs={{0,6},{1,7},{2,4},{3,5},{4,2},{5,3},{6,0},{7,1},{8,14},{9,15},{10,... | collective-permute-start | bytes 442376 | tf_op jit(solution)/shard_map/ppermute | solution.py:29
  31.2 5.8 %collective-permute-done.8.refs_5_ = bf16[4,128,512]{2,1,0:T(8,128)(2,1)S(1)} collective-permute-done((bf16[4,128,512]{2,1,0:T(8,128)(2,1)}, bf16[4,128,512]{2,1,0:T(8,128)(2,1)S(1)}, u32[]{:S(2)}, u32[]{:S(2)}) %collective-permute-start.8) | collective-permute-done | bytes 524320 | tf_op jit(solution)/shard_map/ppermute | solution.py:29
  42.3 2.3 collective-permute-done.9.refs_9_
  44.6 2.0 collective-permute-done.7.refs_7_
  47.3 2.0 shard_map.355.refs_1_
  51.5 1.9 copy-done.2
  53.4 4.1 %shard_map.356 = (f32[2,384,512]{2,1,0:T(8,128)S(1)}, bf16[2,384,512]{2,1,0:T(8,128)(2,1)S(1)}, f32[2,4,512]{2,1,0:T(4,128)S(1)}, bf16[2048,512]{1,0:T(8,128)(2,1)S(1)}) custom-call(bf16[2,384,2048]{2,1,0:T(8,128)(2,1)S(1)} %bitcast.116, f32[3,2,384,128]{3,2,1,0:T(8,128)S(1)} %broadcast_in_dim.6.mask_ref, f32[2,8,128]{2,1,0:T(8,128)S(1)} %pad_maximum_fusion.1.gram_ref, ...), custom_call_target="tpu_custom_call" | custom-call | flops 1610612736 | bytes 6291456 | tf_op jit(solution)/shard_map/pallas_call | solution.py:333
  58.8 3.1 %collective-permute-start.21 = (bf16[2,384,512]{2,1,0:T(8,128)(2,1)S(1)}, bf16[2,384,512]{2,1,0:T(8,128)(2,1)S(1)}, u32[]{:S(2)}, u32[]{:S(2)}) collective-permute-start(bf16[2,384,512]{2,1,0:T(8,128)(2,1)S(1)} %get-tuple-element.113), channel_id=1, source_target_pairs={{0,1},{1,2},{2,3},{3,4},{4,5},{5,6},{6,7},{8,9},{9,10},{10,11},{11... | collective-permute-start | bytes 2359304 | tf_op jit(solution)/shard_map/ppermute | solution.py:775
  72.5 3.6 %collective-permute-start.25 = (f32[2,4,512]{2,1,0:T(4,128)S(1)}, f32[2,4,512]{2,1,0:T(4,128)S(1)}, u32[]{:S(2)}, u32[]{:S(2)}) collective-permute-start(f32[2,4,512]{2,1,0:T(4,128)S(1)} %bitcast.146), channel_id=1, source_target_pairs={{0,6},{1,7},{2,4},{3,5},{4,2},{5,3},{6,0},{7,1},{8,14},{9,15},{10,... | collective-permute-start | bytes 49160 | tf_op jit(solution)/shard_map/ppermute | solution.py:29
  78.2 2.7 collective-permute-done.24
  81.4 3.7 %copy-done.1 = bf16[3,2,1,4,96,2048]{5,4,3,2,1,0:T(8,128)(2,1)S(1)} copy-done((bf16[3,2,1,4,96,2048]{5,4,3,2,1,0:T(8,128)(2,1)S(1)}, bf16[3,2,1,4,96,2048]{5,4,3,2,1,0:T(8,128)(2,1)}, u32[]{:S(2)}) %copy-start.1) | copy-done | bytes 9437208
  85.0 3.2 %shard_map.357.refs_11_.up_ref = bf16[2,384,2048]{2,1,0:T(8,128)(2,1)S(1)} custom-call(f32[2,4,512]{2,1,0:T(4,128)S(1)} %bitcast.128, bf16[3,2,1,4,96,2048]{5,4,3,2,1,0:T(8,128)(2,1)S(1)} %copy-done.1, f32[3,2,384,128]{3,2,1,0:T(8,128)S(1)} %broadcast_in_dim.6.mask_ref), custom_call_target="tpu_custom_call" | custom-call | flops 12582912 | bytes 15728640 | tf_op jit(solution)/shard_map/pallas_call | solution.py:333
  90.3 9.3 %shard_map.358 = (bf16[3,2,384,512]{3,2,1,0:T(8,128)(2,1)S(1)}, f32[2,384,512]{2,1,0:T(8,128)S(1)}, bf16[2,384,512]{2,1,0:T(8,128)(2,1)S(1)}, f32[2,2,512]{2,1,0:T(2,128)S(1)}) custom-call(f32[2]{0:T(128)S(1)} %convert_divide_fusion.inv_ref, f32[2,4,512]{2,1,0:T(4,128)S(1)} %bitcast.129, f32[2,512]{1,0:T(2,128)S(1)} %get-tuple-element.252.param_ref.param1_ref, ...), custom_call_target="tpu_custom_call" | custom-call | flops 3623878656 | bytes 12582912 | tf_op jit(solution)/shard_map/pallas_call | solution.py:333
  100.9 2.1 collective-permute-start.36
  109.4 2.6 collective-permute-start.37
  113.6 6.3 %shard_map.360 = (bf16[2,384,512]{2,1,0:T(8,128)(2,1)S(1)}, f32[2,384,2048]{2,1,0:T(8,128)S(1)}, f32[2,2,2048]{2,1,0:T(2,128)S(1)}) custom-call(f32[2]{0:T(128)S(1)} %convert_divide_fusion.inv_ref, f32[2,2,512]{2,1,0:T(2,128)S(1)} %add_add_fusion.10.sums_ref.stats2_ref, f32[2,512]{1,0:T(2,128)S(1)} %get-tuple-element.251.param_ref.param2_ref, ...), custom_call_target="tpu_custom_call" | custom-call | flops 1610612736 | bytes 9437184 | tf_op jit(solution)/shard_map/pallas_call | solution.py:333
  127.3 2.4 collective-permute-start.46
  136.2 3.1 %collective-permute-start.47 = (bf16[2,384,512]{2,1,0:T(8,128)(2,1)S(1)}, bf16[2,384,512]{2,1,0:T(8,128)(2,1)S(1)}, u32[]{:S(2)}, u32[]{:S(2)}) collective-permute-start(bf16[2,384,512]{2,1,0:T(8,128)(2,1)S(1)} %get-tuple-element.131), channel_id=1, source_target_pairs={{0,1},{1,2},{2,3},{3,4},{4,5},{5,6},{6,7},{8,9},{9,10},{10,11},{11... | collective-permute-start | bytes 2359304 | tf_op jit(solution)/shard_map/ppermute | solution.py:775
  139.3 9.2 %shard_map.361 = (bf16[2,384,2048]{2,1,0:T(8,128)(2,1)}, bf16[2,384,2048]{2,1,0:T(8,128)(2,1)S(1)}, f32[2,2,2048]{2,1,0:T(2,128)S(1)}) custom-call(f32[2]{0:T(128)S(1)} %convert_divide_fusion.inv_ref, f32[2,2,2048]{2,1,0:T(2,128)S(1)} %add_add_fusion.2.sums_ref.stats3_ref, f32[2,2048]{1,0:T(2,128)S(1)} %slice.173.param_ref.param3_ref, ...), custom_call_target="tpu_custom_call" | custom-call | flops 62914560 | bytes 25165824 | tf_op jit(solution)/shard_map/pallas_call | solution.py:333
  149.7 2.2 collective-permute-start.52
  156.7 3.2 %collective-permute-start.55 = (f32[2,2,2048]{2,1,0:T(2,128)S(1)}, f32[2,2,2048]{2,1,0:T(2,128)S(1)}, u32[]{:S(2)}, u32[]{:S(2)}) collective-permute-start(f32[2,2,2048]{2,1,0:T(2,128)S(1)} %add_add_fusion.1), channel_id=1, source_target_pairs={{0,6},{1,7},{2,4},{3,5},{4,2},{5,3},{6,0},{7,1},{8,14},{9,15},{10,... | collective-permute-start | bytes 98312 | tf_op jit(solution)/shard_map/ppermute | solution.py:29
  162.5 2.5 collective-permute-done.54
  165.1 5.5 %shard_map.362 = (bf16[2,384,2048]{2,1,0:T(8,128)(2,1)S(1)}, f32[2,384,512]{2,1,0:T(8,128)S(1)}, bf16[2,384,512]{2,1,0:T(8,128)(2,1)S(1)}, f32[2,2,512]{2,1,0:T(2,128)S(1)}) custom-call(f32[2]{0:T(128)S(1)} %convert_divide_fusion.inv_ref, f32[2,2,2048]{2,1,0:T(2,128)S(1)} %add_add_fusion.2.sums_ref.stats3_ref, f32[2,2,2048]{2,1,0:T(2,128)S(1)} %add_add_fusion.grads3_ref, ...), custom_call_target="tpu_custom_call" | custom-call | flops 1610612736 | bytes 15728640 | tf_op jit(solution)/shard_map/pallas_call | solution.py:333
  172.2 3.1 %collective-permute-start.63 = (bf16[2,384,512]{2,1,0:T(8,128)(2,1)S(1)}, bf16[2,384,512]{2,1,0:T(8,128)(2,1)S(1)}, u32[]{:S(2)}, u32[]{:S(2)}) collective-permute-start(bf16[2,384,512]{2,1,0:T(8,128)(2,1)S(1)} %get-tuple-element.138), channel_id=1, source_target_pairs={{0,1},{1,2},{2,3},{3,4},{4,5},{5,6},{6,7},{8,9},{9,10},{10,11},{11... | collective-permute-start | bytes 2359304 | tf_op jit(solution)/shard_map/ppermute | solution.py:775
  175.4 1.7 collective-permute-done.56
  182.8 1.9 collective-permute-start.62
  185.1 2.1 collective-permute-start.60
  189.3 2.6 shard_map.363
  191.9 8.1 %shard_map.364 = (bf16[16,208,512]{2,1,0:T(8,128)(2,1)S(1)}, bf16[16,208,512]{2,1,0:T(8,128)(2,1)S(1)}) custom-call(bf16[3,768,512]{2,1,0:T(8,128)(2,1)S(1)} %bitcast.136, bf16[768,1536]{1,0:T(8,128)(2,1)S(1)} %bitcast.135, bf16[768,2048]{1,0:T(8,128)(2,1)S(1)} %bitcast.134, bf16[768,512]{1,0:T(8,128)(2,1)S(1)} %bitcast.137, s32[16]{0:T(128)S(1)} %fusion.22.place_ref, ...), custom_call_target="tpu_custom_call" | custom-call | flops 5234491392 | bytes 9437184 | tf_op jit(solution)/shard_map/pallas_call | solution.py:333
  200.1 6.1 %shard_map.365 = (f32[2,384,512]{2,1,0:T(8,128)S(1)}, f32[2,2,512]{2,1,0:T(2,128)S(1)}) custom-call(f32[2]{0:T(128)S(1)} %convert_divide_fusion.inv_ref, f32[2,4,512]{2,1,0:T(4,128)S(1)} %bitcast.130, f32[2,512]{1,0:T(2,128)S(1)} %get-tuple-element.252.param_ref.param1_ref, bf16[2,384,1536]{2,1,0:T(8,128)(2,1)S(1)} %get-tuple-element.139.cat_ref, ...), custom_call_target="tpu_custom_call" | custom-call | flops 3623878656 | bytes 16515072 | tf_op jit(solution)/shard_map/pallas_call | solution.py:333
  207.6 2.1 collective-permute-start.68
  216.7 1.9 collective-permute-start.72
  223.4 4.0 %shard_map.366 = (bf16[2,384,512]{2,1,0:T(8,128)(2,1)S(1)}, bf16[16,64,512]{2,1,0:T(8,128)(2,1)S(1)}, bf16[16,64,512]{2,1,0:T(8,128)(2,1)S(1)}) custom-call(f32[2]{0:T(128)S(1)} %convert_divide_fusion.inv_ref, f32[2,4,512]{2,1,0:T(4,128)S(1)} %bitcast.131, f32[2,2,512]{2,1,0:T(2,128)S(1)} %add_add_fusion.6.grads_ref, ...), custom_call_target="tpu_custom_call" | custom-call | flops 1610612736 | bytes 6291456 | tf_op jit(solution)/shard_map/pallas_call | solution.py:333
  227.4 6.9 %collective-permute-done.73 = bf16[2,2,208,512]{3,2,1,0:T(8,128)(2,1)S(1)} collective-permute-done((bf16[2,2,208,512]{3,2,1,0:T(8,128)(2,1)S(1)}, bf16[2,2,208,512]{3,2,1,0:T(8,128)(2,1)S(1)}, u32[]{:S(2)}, u32[]{:S(2)}) %collective-permute-start.73) | collective-permute-done | bytes 852000 | tf_op jit(solution)/shard_map/ppermute | solution.py:29
  238.0 4.3 %shard_map.367 = bf16[768,2048]{1,0:T(8,128)(2,1)} custom-call(bf16[768,512]{1,0:T(8,128)(2,1)S(1)} %bitcast.127, bf16[2048,512]{1,0:T(8,128)(2,1)S(1)} %get-tuple-element.158.w_ref, bf16[768,2048]{1,0:T(8,128)(2,1)S(1)} %bitcast.119), custom_call_target="tpu_custom_call" | custom-call | flops 1610612736 | bytes 12582912 | tf_op jit(solution)/shard_map/pallas_call | solution.py:333
  242.3 5.3 %collective-permute-done.75 = bf16[2,208,512]{2,1,0:T(8,128)(2,1)S(1)} collective-permute-done((bf16[2,208,512]{2,1,0:T(8,128)(2,1)S(1)}, bf16[2,208,512]{2,1,0:T(8,128)(2,1)S(1)}, u32[]{:S(2)}, u32[]{:S(2)}) %collective-permute-start.75) | collective-permute-done | bytes 426016 | tf_op jit(solution)/shard_map/ppermute | solution.py:29
  251.5 2.1 collective-permute-start.79
  254.1 9.0 %collective-permute-done.79 = bf16[1,208,512]{2,1,0:T(8,128)(2,1)S(1)} collective-permute-done((bf16[1,208,512]{2,1,0:T(8,128)(2,1)S(1)}, bf16[1,208,512]{2,1,0:T(8,128)(2,1)S(1)}, u32[]{:S(2)}, u32[]{:S(2)}) %collective-permute-start.79) | collective-permute-done | bytes 213024 | tf_op jit(solution)/shard_map/ppermute | solution.py:29
  264.0 4.2 %collective-permute-done.82 = bf16[2,64,512]{2,1,0:T(8,128)(2,1)S(1)} collective-permute-done((bf16[2,64,512]{2,1,0:T(8,128)(2,1)S(1)}, bf16[2,64,512]{2,1,0:T(8,128)(2,1)S(1)}, u32[]{:S(2)}, u32[]{:S(2)}) %collective-permute-start.82) | collective-permute-done | bytes 131104 | tf_op jit(solution)/shard_map/ppermute | solution.py:29
  269.9 1.9 collective-permute-start.87
  275.2 1.9 collective-permute-start.86
  279.4 4.2 %collective-permute-done.85 = bf16[1,64,512]{2,1,0:T(8,128)(2,1)S(1)} collective-permute-done((bf16[1,64,512]{2,1,0:T(8,128)(2,1)S(1)}, bf16[1,64,512]{2,1,0:T(8,128)(2,1)S(1)}, u32[]{:S(2)}, u32[]{:S(2)}) %collective-permute-start.85) | collective-permute-done | bytes 65568 | tf_op jit(solution)/shard_map/ppermute | solution.py:29
  290.6 1.9 collective-permute-start.94
  (294 shorter events, 122.9 us)
Async XLA Ops:
  2.5 17.9 %collective-permute-start.2 = (bf16[1,128,512]{2,1,0:T(8,128)(2,1)S(1)}, bf16[1,128,512]{2,1,0:T(8,128)(2,1)S(1)}, u32[]{:S(2)}, u32[]{:S(2)}) collective-permute-start(bf16[1,128,512]{2,1,0:T(8,128)(2,1)S(1)} %maximum_bitcast_fusion.refs_0_), channel_id=1, source_target_pairs={{0,6},{1,7},{2,4},{3,5},{4,2},{5,3},{6,0},{7,1},{8,14},{9,15},{10,... | collective-permute-start | bytes 393224 | tf_op jit(solution)/shard_map/ppermute | solution.py:29
  7.6 12.8 %collective-permute-start.1 = (bf16[1,128,512]{2,1,0:T(8,128)(2,1)S(1)}, bf16[1,128,512]{2,1,0:T(8,128)(2,1)S(1)}, u32[]{:S(2)}, u32[]{:S(2)}) collective-permute-start(bf16[1,128,512]{2,1,0:T(8,128)(2,1)S(1)} %maximum_bitcast_fusion.refs_0_), channel_id=1, source_target_pairs={{0,4},{1,5},{2,6},{3,7},{4,0},{5,1},{6,2},{7,3},{8,12},{9,13},{10,... | collective-permute-start | bytes 393224 | tf_op jit(solution)/shard_map/ppermute | solution.py:29
  7.6 12.8 %collective-permute-start = (bf16[1,128,512]{2,1,0:T(8,128)(2,1)S(1)}, bf16[1,128,512]{2,1,0:T(8,128)(2,1)S(1)}, u32[]{:S(2)}, u32[]{:S(2)}) collective-permute-start(bf16[1,128,512]{2,1,0:T(8,128)(2,1)S(1)} %maximum_bitcast_fusion.refs_0_), channel_id=1, source_target_pairs={{0,2},{1,3},{2,0},{3,1},{4,6},{5,7},{6,4},{7,5},{8,10},{9,11},{10,... | collective-permute-start | bytes 393224 | tf_op jit(solution)/shard_map/ppermute | solution.py:29
  23.7 13.3 %collective-permute-start.8 = (bf16[4,128,512]{2,1,0:T(8,128)(2,1)}, bf16[4,128,512]{2,1,0:T(8,128)(2,1)S(1)}, u32[]{:S(2)}, u32[]{:S(2)}) collective-permute-start(bf16[4,128,512]{2,1,0:T(8,128)(2,1)} %shard_map.354.refs_1_), channel_id=1, source_target_pairs={{0,16},{8,24},{16,0},{24,8},{1,17},{9,25},{17,1},{25,9},{2,18},{10... | collective-permute-start | bytes 1572872 | tf_op jit(solution)/shard_map/ppermute | solution.py:29
  25.4 13.9 %collective-permute-start.6 = (bf16[4,128,512]{2,1,0:T(8,128)(2,1)}, bf16[4,128,512]{2,1,0:T(8,128)(2,1)S(1)}, u32[]{:S(2)}, u32[]{:S(2)}) collective-permute-start(bf16[4,128,512]{2,1,0:T(8,128)(2,1)} %shard_map.354.refs_1_), channel_id=1, source_target_pairs={{0,8},{8,0},{16,24},{24,16},{1,9},{9,1},{17,25},{25,17},{2,10},{10... | collective-permute-start | bytes 1572872 | tf_op jit(solution)/shard_map/ppermute | solution.py:29
  26.9 14.6 %collective-permute-start.5 = (bf16[1,144,512]{2,1,0:T(8,128)(2,1)}, bf16[1,144,512]{2,1,0:T(8,128)(2,1)}, u32[]{:S(2)}, u32[]{:S(2)}) collective-permute-start(bf16[1,144,512]{2,1,0:T(8,128)(2,1)} %bitcast.5.refs_0_), channel_id=1, source_target_pairs={{0,6},{1,7},{2,4},{3,5},{4,2},{5,3},{6,0},{7,1},{8,14},{9,15},{10,... | collective-permute-start | bytes 442376 | tf_op jit(solution)/shard_map/ppermute | solution.py:29
  30.5 11.3 %collective-permute-start.4 = (bf16[1,144,512]{2,1,0:T(8,128)(2,1)}, bf16[1,144,512]{2,1,0:T(8,128)(2,1)}, u32[]{:S(2)}, u32[]{:S(2)}) collective-permute-start(bf16[1,144,512]{2,1,0:T(8,128)(2,1)} %bitcast.5.refs_0_), channel_id=1, source_target_pairs={{0,4},{1,5},{2,6},{3,7},{4,0},{5,1},{6,2},{7,3},{8,12},{9,13},{10,... | collective-permute-start | bytes 442376 | tf_op jit(solution)/shard_map/ppermute | solution.py:29
  30.5 11.5 %collective-permute-start.3 = (bf16[1,144,512]{2,1,0:T(8,128)(2,1)}, bf16[1,144,512]{2,1,0:T(8,128)(2,1)}, u32[]{:S(2)}, u32[]{:S(2)}) collective-permute-start(bf16[1,144,512]{2,1,0:T(8,128)(2,1)} %bitcast.5.refs_0_), channel_id=1, source_target_pairs={{0,2},{1,3},{2,0},{3,1},{4,6},{5,7},{6,4},{7,5},{8,10},{9,11},{10,... | collective-permute-start | bytes 442376 | tf_op jit(solution)/shard_map/ppermute | solution.py:29
  37.7 6.9 %collective-permute-start.9 = (bf16[2,128,512]{2,1,0:T(8,128)(2,1)}, bf16[2,128,512]{2,1,0:T(8,128)(2,1)S(1)}, u32[]{:S(2)}, u32[]{:S(2)}) collective-permute-start(bf16[2,128,512]{2,1,0:T(8,128)(2,1)} %slice.217), channel_id=1, source_target_pairs={{0,8},{8,0},{16,24},{24,16},{1,9},{9,1},{17,25},{25,17},{2,10},{10... | collective-permute-start | bytes 786440 | tf_op jit(solution)/shard_map/ppermute | solution.py:29
  39.9 6.7 %collective-permute-start.7 = (bf16[2,128,512]{2,1,0:T(8,128)(2,1)}, bf16[2,128,512]{2,1,0:T(8,128)(2,1)}, u32[]{:S(2)}, u32[]{:S(2)}) collective-permute-start(bf16[2,128,512]{2,1,0:T(8,128)(2,1)} %slice.216), channel_id=1, source_target_pairs={{0,16},{8,24},{16,0},{24,8},{1,17},{9,25},{17,1},{25,9},{2,18},{10... | collective-permute-start | bytes 786440 | tf_op jit(solution)/shard_map/ppermute | solution.py:29
  41.5 7.9 %collective-permute-start.10 = (bf16[4,128,512]{2,1,0:T(8,128)(2,1)}, bf16[4,128,512]{2,1,0:T(8,128)(2,1)S(1)}, u32[]{:S(2)}, u32[]{:S(2)}) collective-permute-start(bf16[4,128,512]{2,1,0:T(8,128)(2,1)} %shard_map.354.refs_1_), channel_id=1, source_target_pairs={{0,1},{1,0},{2,3},{3,2},{4,5},{5,4},{6,7},{7,6},{8,9},{9,8},{10,11... | collective-permute-start | bytes 1572872 | tf_op jit(solution)/shard_map/ppermute | solution.py:29
  41.8 7.5 %collective-permute-start.12 = (bf16[4,128,512]{2,1,0:T(8,128)(2,1)S(1)}, bf16[4,128,512]{2,1,0:T(8,128)(2,1)}, u32[]{:S(2)}, u32[]{:S(2)}) collective-permute-start(bf16[4,128,512]{2,1,0:T(8,128)(2,1)S(1)} %collective-permute-done.8.refs_5_), channel_id=1, source_target_pairs={{0,1},{1,0},{2,3},{3,2},{4,5},{5,4},{6,7},{7,6},{8,9},{9,8},{10,11... | collective-permute-start | bytes 1572872 | tf_op jit(solution)/shard_map/ppermute | solution.py:29
  42.0 7.3 %collective-permute-start.11 = (bf16[4,128,512]{2,1,0:T(8,128)(2,1)S(1)}, bf16[4,128,512]{2,1,0:T(8,128)(2,1)}, u32[]{:S(2)}, u32[]{:S(2)}) collective-permute-start(bf16[4,128,512]{2,1,0:T(8,128)(2,1)S(1)} %collective-permute-done.6.refs_3_), channel_id=1, source_target_pairs={{0,1},{1,0},{2,3},{3,2},{4,5},{5,4},{6,7},{7,6},{8,9},{9,8},{10,11... | collective-permute-start | bytes 1572872 | tf_op jit(solution)/shard_map/ppermute | solution.py:29
  49.4 16.0 %collective-permute-start.17 = (bf16[4,144,512]{2,1,0:T(8,128)(2,1)}, bf16[4,144,512]{2,1,0:T(8,128)(2,1)S(1)}, u32[]{:S(2)}, u32[]{:S(2)}) collective-permute-start(bf16[4,144,512]{2,1,0:T(8,128)(2,1)} %shard_map.355.refs_1_), channel_id=1, source_target_pairs={{0,16},{8,24},{16,0},{24,8},{1,17},{9,25},{17,1},{25,9},{2,18},{10... | collective-permute-start | bytes 1769480 | tf_op jit(solution)/shard_map/ppermute | solution.py:29
  50.9 15.7 %collective-permute-start.16 = (bf16[4,144,512]{2,1,0:T(8,128)(2,1)}, bf16[4,144,512]{2,1,0:T(8,128)(2,1)S(1)}, u32[]{:S(2)}, u32[]{:S(2)}) collective-permute-start(bf16[4,144,512]{2,1,0:T(8,128)(2,1)} %shard_map.355.refs_1_), channel_id=1, source_target_pairs={{0,8},{8,0},{16,24},{24,16},{1,9},{9,1},{17,25},{25,17},{2,10},{10... | collective-permute-start | bytes 1769480 | tf_op jit(solution)/shard_map/ppermute | solution.py:29
  57.5 15.0 %collective-permute-start.22 = (bf16[2,384,512]{2,1,0:T(8,128)(2,1)S(1)}, bf16[2,384,512]{2,1,0:T(8,128)(2,1)S(1)}, u32[]{:S(2)}, u32[]{:S(2)}) collective-permute-start(bf16[2,384,512]{2,1,0:T(8,128)(2,1)S(1)} %get-tuple-element.113), channel_id=1, source_target_pairs={{1,0},{2,1},{3,2},{4,3},{5,4},{6,5},{7,6},{9,8},{10,9},{11,10},{12... | collective-permute-start | bytes 2359304 | tf_op jit(solution)/shard_map/ppermute | solution.py:776
  58.8 13.7 %collective-permute-start.21 = (bf16[2,384,512]{2,1,0:T(8,128)(2,1)S(1)}, bf16[2,384,512]{2,1,0:T(8,128)(2,1)S(1)}, u32[]{:S(2)}, u32[]{:S(2)}) collective-permute-start(bf16[2,384,512]{2,1,0:T(8,128)(2,1)S(1)} %get-tuple-element.113), channel_id=1, source_target_pairs={{0,1},{1,2},{2,3},{3,4},{4,5},{5,6},{6,7},{8,9},{9,10},{10,11},{11... | collective-permute-start | bytes 2359304 | tf_op jit(solution)/shard_map/ppermute | solution.py:775
  71.3 17.0 %collective-permute-start.30 = (bf16[2,144,512]{2,1,0:T(8,128)(2,1)S(1)}, bf16[2,144,512]{2,1,0:T(8,128)(2,1)S(1)}, u32[]{:S(2)}, u32[]{:S(2)}) collective-permute-start(bf16[2,144,512]{2,1,0:T(8,128)(2,1)S(1)} %slice.171), channel_id=1, source_target_pairs={{0,8},{8,0},{16,24},{24,16},{1,9},{9,1},{17,25},{25,17},{2,10},{10... | collective-permute-start | bytes 884744 | tf_op jit(solution)/shard_map/ppermute | solution.py:29
  71.9 16.3 %collective-permute-start.29 = (bf16[2,144,512]{2,1,0:T(8,128)(2,1)S(1)}, bf16[2,144,512]{2,1,0:T(8,128)(2,1)S(1)}, u32[]{:S(2)}, u32[]{:S(2)}) collective-permute-start(bf16[2,144,512]{2,1,0:T(8,128)(2,1)S(1)} %slice.170), channel_id=1, source_target_pairs={{0,16},{8,24},{16,0},{24,8},{1,17},{9,25},{17,1},{25,9},{2,18},{10... | collective-permute-start | bytes 884744 | tf_op jit(solution)/shard_map/ppermute | solution.py:29
  72.5 5.6 %collective-permute-start.25 = (f32[2,4,512]{2,1,0:T(4,128)S(1)}, f32[2,4,512]{2,1,0:T(4,128)S(1)}, u32[]{:S(2)}, u32[]{:S(2)}) collective-permute-start(f32[2,4,512]{2,1,0:T(4,128)S(1)} %bitcast.146), channel_id=1, source_target_pairs={{0,6},{1,7},{2,4},{3,5},{4,2},{5,3},{6,0},{7,1},{8,14},{9,15},{10,... | collective-permute-start | bytes 49160 | tf_op jit(solution)/shard_map/ppermute | solution.py:29
  78.2 10.7 %collective-permute-start.26 = (bf16[4,144,512]{2,1,0:T(8,128)(2,1)S(1)}, bf16[4,144,512]{2,1,0:T(8,128)(2,1)S(1)}, u32[]{:S(2)}, u32[]{:S(2)}) collective-permute-start(bf16[4,144,512]{2,1,0:T(8,128)(2,1)S(1)} %copy-done.5), channel_id=1, source_target_pairs={{0,1},{1,0},{2,3},{3,2},{4,5},{5,4},{6,7},{7,6},{8,9},{9,8},{10,11... | collective-permute-start | bytes 1769480 | tf_op jit(solution)/shard_map/ppermute | solution.py:29
  80.8 9.5 %collective-permute-start.27 = (bf16[4,144,512]{2,1,0:T(8,128)(2,1)S(1)}, bf16[4,144,512]{2,1,0:T(8,128)(2,1)S(1)}, u32[]{:S(2)}, u32[]{:S(2)}) collective-permute-start(bf16[4,144,512]{2,1,0:T(8,128)(2,1)S(1)} %collective-permute-done.16.refs_3_), channel_id=1, source_target_pairs={{0,1},{1,0},{2,3},{3,2},{4,5},{5,4},{6,7},{7,6},{8,9},{9,8},{10,11... | collective-permute-start | bytes 1769480 | tf_op jit(solution)/shard_map/ppermute | solution.py:29
  80.8 9.5 %collective-permute-start.28 = (bf16[4,144,512]{2,1,0:T(8,128)(2,1)S(1)}, bf16[4,144,512]{2,1,0:T(8,128)(2,1)S(1)}, u32[]{:S(2)}, u32[]{:S(2)}) collective-permute-start(bf16[4,144,512]{2,1,0:T(8,128)(2,1)S(1)} %collective-permute-done.17.refs_5_), channel_id=1, source_target_pairs={{0,1},{1,0},{2,3},{3,2},{4,5},{5,4},{6,7},{7,6},{8,9},{9,8},{10,11... | collective-permute-start | bytes 1769480 | tf_op jit(solution)/shard_map/ppermute | solution.py:29
  107.5 6.0 %collective-permute-start.39 = (f32[2,2,512]{2,1,0:T(2,128)S(1)}, f32[2,2,512]{2,1,0:T(2,128)S(1)}, u32[]{:S(2)}, u32[]{:S(2)}) collective-permute-start(f32[2,2,512]{2,1,0:T(2,128)S(1)} %add_add_fusion.11), channel_id=1, source_target_pairs={{0,6},{1,7},{2,4},{3,5},{4,2},{5,3},{6,0},{7,1},{8,14},{9,15},{10,... | collective-permute-start | bytes 24584 | tf_op jit(solution)/shard_map/ppermute | solution.py:29
  127.3 5.8 %collective-permute-start.46 = (f32[2,2,2048]{2,1,0:T(2,128)S(1)}, f32[2,2,2048]{2,1,0:T(2,128)S(1)}, u32[]{:S(2)}, u32[]{:S(2)}) collective-permute-start(f32[2,2,2048]{2,1,0:T(2,128)S(1)} %add_add_fusion.3), channel_id=1, source_target_pairs={{0,6},{1,7},{2,4},{3,5},{4,2},{5,3},{6,0},{7,1},{8,14},{9,15},{10,... | collective-permute-start | bytes 98312 | tf_op jit(solution)/shard_map/ppermute | solution.py:29
  134.9 13.6 %collective-permute-start.48 = (bf16[2,384,512]{2,1,0:T(8,128)(2,1)S(1)}, bf16[2,384,512]{2,1,0:T(8,128)(2,1)S(1)}, u32[]{:S(2)}, u32[]{:S(2)}) collective-permute-start(bf16[2,384,512]{2,1,0:T(8,128)(2,1)S(1)} %get-tuple-element.131), channel_id=1, source_target_pairs={{1,0},{2,1},{3,2},{4,3},{5,4},{6,5},{7,6},{9,8},{10,9},{11,10},{12... | collective-permute-start | bytes 2359304 | tf_op jit(solution)/shard_map/ppermute | solution.py:776
  136.2 12.3 %collective-permute-start.47 = (bf16[2,384,512]{2,1,0:T(8,128)(2,1)S(1)}, bf16[2,384,512]{2,1,0:T(8,128)(2,1)S(1)}, u32[]{:S(2)}, u32[]{:S(2)}) collective-permute-start(bf16[2,384,512]{2,1,0:T(8,128)(2,1)S(1)} %get-tuple-element.131), channel_id=1, source_target_pairs={{0,1},{1,2},{2,3},{3,4},{4,5},{5,6},{6,7},{8,9},{9,10},{10,11},{11... | collective-permute-start | bytes 2359304 | tf_op jit(solution)/shard_map/ppermute | solution.py:775
  156.7 5.9 %collective-permute-start.55 = (f32[2,2,2048]{2,1,0:T(2,128)S(1)}, f32[2,2,2048]{2,1,0:T(2,128)S(1)}, u32[]{:S(2)}, u32[]{:S(2)}) collective-permute-start(f32[2,2,2048]{2,1,0:T(2,128)S(1)} %add_add_fusion.1), channel_id=1, source_target_pairs={{0,6},{1,7},{2,4},{3,5},{4,2},{5,3},{6,0},{7,1},{8,14},{9,15},{10,... | collective-permute-start | bytes 98312 | tf_op jit(solution)/shard_map/ppermute | solution.py:29
  159.9 5.2 %collective-permute-start.54 = (f32[2,2,2048]{2,1,0:T(2,128)S(1)}, f32[2,2,2048]{2,1,0:T(2,128)S(1)}, u32[]{:S(2)}, u32[]{:S(2)}) collective-permute-start(f32[2,2,2048]{2,1,0:T(2,128)S(1)} %add_add_fusion.1), channel_id=1, source_target_pairs={{0,4},{1,5},{2,6},{3,7},{4,0},{5,1},{6,2},{7,3},{8,12},{9,13},{10,... | collective-permute-start | bytes 98312 | tf_op jit(solution)/shard_map/ppermute | solution.py:29
  170.7 18.6 %collective-permute-start.64 = (bf16[2,384,512]{2,1,0:T(8,128)(2,1)S(1)}, bf16[2,384,512]{2,1,0:T(8,128)(2,1)S(1)}, u32[]{:S(2)}, u32[]{:S(2)}) collective-permute-start(bf16[2,384,512]{2,1,0:T(8,128)(2,1)S(1)} %get-tuple-element.138), channel_id=1, source_target_pairs={{1,0},{2,1},{3,2},{4,3},{5,4},{6,5},{7,6},{9,8},{10,9},{11,10},{12... | collective-permute-start | bytes 2359304 | tf_op jit(solution)/shard_map/ppermute | solution.py:776
  172.2 17.2 %collective-permute-start.63 = (bf16[2,384,512]{2,1,0:T(8,128)(2,1)S(1)}, bf16[2,384,512]{2,1,0:T(8,128)(2,1)S(1)}, u32[]{:S(2)}, u32[]{:S(2)}) collective-permute-start(bf16[2,384,512]{2,1,0:T(8,128)(2,1)S(1)} %get-tuple-element.138), channel_id=1, source_target_pairs={{0,1},{1,2},{2,3},{3,4},{4,5},{5,6},{6,7},{8,9},{9,10},{10,11},{11... | collective-permute-start | bytes 2359304 | tf_op jit(solution)/shard_map/ppermute | solution.py:775
  182.8 5.5 %collective-permute-start.62 = (f32[2,2,512]{2,1,0:T(2,128)S(1)}, f32[2,2,512]{2,1,0:T(2,128)S(1)}, u32[]{:S(2)}, u32[]{:S(2)}) collective-permute-start(f32[2,2,512]{2,1,0:T(2,128)S(1)} %add_add_fusion.9), channel_id=1, source_target_pairs={{0,6},{1,7},{2,4},{3,5},{4,2},{5,3},{6,0},{7,1},{8,14},{9,15},{10,... | collective-permute-start | bytes 24584 | tf_op jit(solution)/shard_map/ppermute | solution.py:29
  200.1 14.2 %collective-permute-start.69 = (bf16[16,208,512]{2,1,0:T(8,128)(2,1)S(1)}, bf16[16,208,512]{2,1,0:T(8,128)(2,1)S(1)}, u32[]{:S(2)}, u32[]{:S(2)}) collective-permute-start(bf16[16,208,512]{2,1,0:T(8,128)(2,1)S(1)} %get-tuple-element.144.refs_11_), channel_id=1, source_target_pairs={{0,1},{1,0},{2,3},{3,2},{4,5},{5,4},{6,7},{7,6},{8,9},{9,8},{10,11... | collective-permute-start | bytes 10223624 | tf_op jit(solution)/shard_map/ppermute | solution.py:29
  214.8 19.6 %collective-permute-start.73 = (bf16[2,2,208,512]{3,2,1,0:T(8,128)(2,1)S(1)}, bf16[2,2,208,512]{3,2,1,0:T(8,128)(2,1)S(1)}, u32[]{:S(2)}, u32[]{:S(2)}) collective-permute-start(bf16[2,2,208,512]{3,2,1,0:T(8,128)(2,1)S(1)} %get-tuple-element.152), channel_id=1, source_target_pairs={{0,8},{8,0},{16,24},{24,16},{1,9},{9,1},{17,25},{25,17},{2,10},{10... | collective-permute-start | bytes 2555912 | tf_op jit(solution)/shard_map/ppermute | solution.py:29
  215.4 19.5 %collective-permute-start.74 = (bf16[2,2,208,512]{3,2,1,0:T(8,128)(2,1)S(1)}, bf16[2,2,208,512]{3,2,1,0:T(8,128)(2,1)S(1)}, u32[]{:S(2)}, u32[]{:S(2)}) collective-permute-start(bf16[2,2,208,512]{3,2,1,0:T(8,128)(2,1)S(1)} %get-tuple-element.153), channel_id=1, source_target_pairs={{0,16},{8,24},{16,0},{24,8},{1,17},{9,25},{17,1},{25,9},{2,18},{10... | collective-permute-start | bytes 2555912 | tf_op jit(solution)/shard_map/ppermute | solution.py:29
  216.7 5.4 %collective-permute-start.72 = (f32[2,2,512]{2,1,0:T(2,128)S(1)}, f32[2,2,512]{2,1,0:T(2,128)S(1)}, u32[]{:S(2)}, u32[]{:S(2)}) collective-permute-start(f32[2,2,512]{2,1,0:T(2,128)S(1)} %add_add_fusion.7), channel_id=1, source_target_pairs={{0,6},{1,7},{2,4},{3,5},{4,2},{5,3},{6,0},{7,1},{8,14},{9,15},{10,... | collective-permute-start | bytes 24584 | tf_op jit(solution)/shard_map/ppermute | solution.py:29
  234.9 14.2 %collective-permute-start.77 = (bf16[16,64,512]{2,1,0:T(8,128)(2,1)S(1)}, bf16[16,64,512]{2,1,0:T(8,128)(2,1)S(1)}, u32[]{:S(2)}, u32[]{:S(2)}) collective-permute-start(bf16[16,64,512]{2,1,0:T(8,128)(2,1)S(1)} %get-tuple-element.163), channel_id=1, source_target_pairs={{0,1},{1,0},{2,3},{3,2},{4,5},{5,4},{6,7},{7,6},{8,9},{9,8},{10,11... | collective-permute-start | bytes 3145736 | tf_op jit(solution)/shard_map/ppermute | solution.py:29
  235.2 12.3 %collective-permute-start.75 = (bf16[2,208,512]{2,1,0:T(8,128)(2,1)S(1)}, bf16[2,208,512]{2,1,0:T(8,128)(2,1)S(1)}, u32[]{:S(2)}, u32[]{:S(2)}) collective-permute-start(bf16[2,208,512]{2,1,0:T(8,128)(2,1)S(1)} %get-tuple-element.159), channel_id=1, source_target_pairs={{0,8},{8,0},{16,24},{24,16},{1,9},{9,1},{17,25},{25,17},{2,10},{10... | collective-permute-start | bytes 1277960 | tf_op jit(solution)/shard_map/ppermute | solution.py:29
  236.5 11.9 %collective-permute-start.76 = (bf16[2,208,512]{2,1,0:T(8,128)(2,1)S(1)}, bf16[2,208,512]{2,1,0:T(8,128)(2,1)S(1)}, u32[]{:S(2)}, u32[]{:S(2)}) collective-permute-start(bf16[2,208,512]{2,1,0:T(8,128)(2,1)S(1)} %get-tuple-element.160), channel_id=1, source_target_pairs={{0,16},{8,24},{16,0},{24,8},{1,17},{9,25},{17,1},{25,9},{2,18},{10... | collective-permute-start | bytes 1277960 | tf_op jit(solution)/shard_map/ppermute | solution.py:29
  249.2 13.9 %collective-permute-start.80 = (bf16[2,2,64,512]{3,2,1,0:T(8,128)(2,1)S(1)}, bf16[2,2,64,512]{3,2,1,0:T(8,128)(2,1)S(1)}, u32[]{:S(2)}, u32[]{:S(2)}) collective-permute-start(bf16[2,2,64,512]{3,2,1,0:T(8,128)(2,1)S(1)} %get-tuple-element.167), channel_id=1, source_target_pairs={{0,8},{8,0},{16,24},{24,16},{1,9},{9,1},{17,25},{25,17},{2,10},{10... | collective-permute-start | bytes 786440 | tf_op jit(solution)/shard_map/ppermute | solution.py:29
  250.1 13.0 %collective-permute-start.81 = (bf16[2,2,64,512]{3,2,1,0:T(8,128)(2,1)S(1)}, bf16[2,2,64,512]{3,2,1,0:T(8,128)(2,1)S(1)}, u32[]{:S(2)}, u32[]{:S(2)}) collective-permute-start(bf16[2,2,64,512]{3,2,1,0:T(8,128)(2,1)S(1)} %get-tuple-element.168), channel_id=1, source_target_pairs={{0,16},{8,24},{16,0},{24,8},{1,17},{9,25},{17,1},{25,9},{2,18},{10... | collective-permute-start | bytes 786440 | tf_op jit(solution)/shard_map/ppermute | solution.py:29
  251.5 11.5 %collective-permute-start.79 = (bf16[1,208,512]{2,1,0:T(8,128)(2,1)S(1)}, bf16[1,208,512]{2,1,0:T(8,128)(2,1)S(1)}, u32[]{:S(2)}, u32[]{:S(2)}) collective-permute-start(bf16[1,208,512]{2,1,0:T(8,128)(2,1)S(1)} %get-tuple-element.247), channel_id=1, source_target_pairs={{0,4},{1,5},{2,6},{3,7},{4,0},{5,1},{6,2},{7,3},{8,12},{9,13},{10,... | collective-permute-start | bytes 638984 | tf_op jit(solution)/shard_map/ppermute | solution.py:29
  253.6 9.5 %collective-permute-start.78 = (bf16[1,208,512]{2,1,0:T(8,128)(2,1)S(1)}, bf16[1,208,512]{2,1,0:T(8,128)(2,1)S(1)}, u32[]{:S(2)}, u32[]{:S(2)}) collective-permute-start(bf16[1,208,512]{2,1,0:T(8,128)(2,1)S(1)} %get-tuple-element.248), channel_id=1, source_target_pairs={{0,2},{1,3},{2,0},{3,1},{4,6},{5,7},{6,4},{7,5},{8,10},{9,11},{10,... | collective-permute-start | bytes 638984 | tf_op jit(solution)/shard_map/ppermute | solution.py:29
  269.9 8.8 %collective-permute-start.87 = (bf16[1,208,512]{2,1,0:T(8,128)(2,1)S(1)}, bf16[1,208,512]{2,1,0:T(8,128)(2,1)S(1)}, u32[]{:S(2)}, u32[]{:S(2)}) collective-permute-start(bf16[1,208,512]{2,1,0:T(8,128)(2,1)S(1)} %get-tuple-element.246), channel_id=1, source_target_pairs={{0,6},{1,7},{2,4},{3,5},{4,2},{5,3},{6,0},{7,1},{8,14},{9,15},{10,... | collective-permute-start | bytes 638984 | tf_op jit(solution)/shard_map/ppermute | solution.py:29
  271.8 7.6 %collective-permute-start.83 = (bf16[1,64,512]{2,1,0:T(8,128)(2,1)S(1)}, bf16[1,64,512]{2,1,0:T(8,128)(2,1)S(1)}, u32[]{:S(2)}, u32[]{:S(2)}) collective-permute-start(bf16[1,64,512]{2,1,0:T(8,128)(2,1)S(1)} %slice.304), channel_id=1, source_target_pairs={{0,2},{1,3},{2,0},{3,1},{4,6},{5,7},{6,4},{7,5},{8,10},{9,11},{10,... | collective-permute-start | bytes 196616 | tf_op jit(solution)/shard_map/ppermute | solution.py:29
  273.5 10.2 %collective-permute-start.85 = (bf16[1,64,512]{2,1,0:T(8,128)(2,1)S(1)}, bf16[1,64,512]{2,1,0:T(8,128)(2,1)S(1)}, u32[]{:S(2)}, u32[]{:S(2)}) collective-permute-start(bf16[1,64,512]{2,1,0:T(8,128)(2,1)S(1)} %get-tuple-element.249), channel_id=1, source_target_pairs={{0,4},{1,5},{2,6},{3,7},{4,0},{5,1},{6,2},{7,3},{8,12},{9,13},{10,... | collective-permute-start | bytes 196616 | tf_op jit(solution)/shard_map/ppermute | solution.py:29
  275.2 8.4 %collective-permute-start.86 = (bf16[1,64,512]{2,1,0:T(8,128)(2,1)S(1)}, bf16[1,64,512]{2,1,0:T(8,128)(2,1)S(1)}, u32[]{:S(2)}, u32[]{:S(2)}) collective-permute-start(bf16[1,64,512]{2,1,0:T(8,128)(2,1)S(1)} %get-tuple-element.250), channel_id=1, source_target_pairs={{0,6},{1,7},{2,4},{3,5},{4,2},{5,3},{6,0},{7,1},{8,14},{9,15},{10,... | collective-permute-start | bytes 196616 | tf_op jit(solution)/shard_map/ppermute | solution.py:29
  290.6 5.4 %collective-permute-start.94 = (f32[4,128]{1,0:T(4,128)S(1)}, f32[4,128]{1,0:T(4,128)S(1)}, u32[]{:S(2)}, u32[]{:S(2)}) collective-permute-start(f32[4,128]{1,0:T(4,128)S(1)} %add_add_fusion.12), channel_id=1, source_target_pairs={{0,6},{1,7},{2,4},{3,5},{4,2},{5,3},{6,0},{7,1},{8,14},{9,15},{10,... | collective-permute-start | bytes 6152 | tf_op jit(solution)/shard_map/ppermute | solution.py:29
  (79 other events, 817.2 us)
